TPU v7x, 256 devices: a whole 4x4x8 slice. The times are simulated.
256 devices in a mesh: vocab: 64 (over z, x, core), hidden: 4 (over y).
Axes of the slice: x: 4, y: 4, z: 8, core: 2. Of those that a mesh axis runs over, the one named last changes fastest.
Arguments:
- hidden_states: bfloat16 [1024, 3584], P('vocab', 'hidden'), may hold values from -6 to 6
- embedding: bfloat16 [131072, 3584], P('vocab', 'hidden'), may hold values from -9 to 9
- targets: int32 [1024], P('vocab'), may hold values from 0 to 131071
Outputs:
- loss: float32 [], replicated
- hidden_grad: float32 [1024, 3584], P('vocab', 'hidden')
- embedding_grad: float32 [131072, 3584], P('vocab', 'hidden')
All inputs are finite; a program needn't handle non-finite values.
Results may differ from a plain program's by a relative error of at most 0.0023.
Values may be sent and summed in bfloat16 or wider, within the bound.
No kernel may reach another device: no remote copies, remote signals or barrier semaphores. Data moves between devices by JAX's collectives and lax.ppermute only.
A program may use at most 128 MiB of HBM per device.

v0:
```python
import jax
import jax.numpy as jnp
from jax import lax
from jax.sharding import PartitionSpec as P

soft_ceiling = 30.0


def token_terms(logits, wanted, vocab_ids):
    capped = soft_ceiling * jnp.tanh(logits / soft_ceiling)
    matches = wanted[:, None] == vocab_ids[None, :]
    exponent = jnp.exp(capped)
    local_total = jnp.sum(exponent, axis=1)
    local_chosen = jnp.sum(jnp.where(matches, capped, jnp.zeros_like(capped)), axis=1)
    return (capped, matches, exponent, local_total, local_chosen)


def gradient_of(capped, matches, exponent, totals):
    factor = 1.0 - (capped / soft_ceiling) ** 2
    return ((exponent / totals[:, None] - matches.astype(jnp.float32)) * factor).astype(
        jnp.bfloat16
    )


def local(hidden_states, embedding, targets):
    token_rows, wanted = (
        lax.all_gather(hidden_states, "vocab", axis=0, tiled=True),
        lax.all_gather(targets, "vocab", axis=0, tiled=True),
    )
    vocab_rows = embedding.shape[0]
    token_count = token_rows.shape[0]
    first_id = lax.axis_index("vocab") * vocab_rows
    vocab_ids = first_id + jnp.arange(vocab_rows, dtype=jnp.int32)
    partial_value = lax.dot_general(
        token_rows, embedding, (((1,), (1,)), ((), ())), preferred_element_type=jnp.float32
    )
    logits = lax.psum(partial_value, "hidden")
    capped, matches, exponent, local_total, local_chosen = token_terms(logits, wanted, vocab_ids)
    totals, chosen = lax.psum((local_total, local_chosen), "vocab")
    loss_value = jnp.sum(jnp.log(totals) - chosen) / token_count
    logit_grad = gradient_of(capped, matches, exponent, totals)
    hidden_grad = lax.psum_scatter(
        jnp.dot(logit_grad, embedding, preferred_element_type=jnp.float32),
        "vocab",
        scatter_dimension=0,
        tiled=True,
    )
    table_grad = lax.dot_general(
        logit_grad, token_rows, (((0,), (0,)), ((), ())), preferred_element_type=jnp.float32
    )
    return (loss_value, hidden_grad, table_grad)


def solution(mesh):
    placed = (P("vocab", "hidden"), P("vocab", "hidden"), P("vocab"))
    return jax.shard_map(
        local,
        mesh=mesh,
        in_specs=placed,
        out_specs=(P(), P("vocab", "hidden"), P("vocab", "hidden")),
        check_vma=False,
    )
```

profile of v0, /device:TPU:8, one launch (start us, length us, event | category | flops | bytes accessed | tf_op | source)
XLA Modules:
  0.0 613.9 jit_solution(4026016056185159075)
XLA Ops:
  7.2 0.0 all-gather.2.cloned.1.call-start
  7.2 0.7 all-gather.2.cloned.1.call-update
  7.9 0.0 all-reduce.6.cloned.1.call-start
  7.9 82.7 %all-gather.2.cloned.1.call-done = bf16[1024,896]{1,0:T(8,128)(2,1)} async-done(((bf16[16,896]{1,0:T(8,128)(2,1)}), bf16[1024,896]{1,0:T(8,128)(2,1)}) %all-gather.2.cloned.1.call-update) | async-done | bytes 1835024 | tf_op jit(solution)/shard_map/all_gather | solution.py:27
  90.6 10.3 %fusion.5 = f32[1024,2048]{1,0:T(8,128)} fusion(bf16[1024,896]{1,0:T(8,128)(2,1)} %all-gather.2.cloned.1.call-done, bf16[2048,896]{1,0:T(8,128)(2,1)} %param.4), kind=kOutput, calls=%fused_computation.12 | convolution fusion | flops 3758096384 | bytes 13893632 | tf_op jit(solution)/shard_map/dot_general | solution.py:34
  101.0 0.0 copy-start.1
  101.0 0.0 copy-start.4
  101.0 0.0 all-reduce.6.cloned.1.call-update
  101.0 0.0 all-reduce.8.cloned.1.call-start
  101.1 0.6 copy-done.1
  101.6 0.6 fusion.4
  102.9 0.0 copy-done.4
  102.9 0.2 dynamic-update-slice
  103.2 18.3 %all-reduce = s32[1024]{0:T(1024)S(1)} all-reduce(s32[1024]{0:T(1024)S(1)} %dynamic-update-slice), channel_id=1, replica_groups=mesh['vocab'=64,'hidden'=4] {'vocab'}, use_global_device_ids=true, to_apply=%add | all-reduce | flops 1024 | bytes 8192
  121.5 141.6 %all-reduce.6.cloned.1.call-done = f32[1024,2048]{1,0:T(8,128)} async-done(((f32[1024,2048]{1,0:T(8,128)}), f32[1024,2048]{1,0:T(8,128)}) %all-reduce.6.cloned.1.call-update) | async-done | bytes 8388624 | tf_op jit(solution)/shard_map/psum | solution.py:37
  263.1 6.4 %exponential_reduce_fusion = (f32[1024]{0:T(1024)S(1)}, f32[1024]{0:T(1024)S(1)}) fusion(f32[1024,2048]{1,0:T(8,128)} %all-reduce.6.cloned.1.call-done, s32[2048]{0:T(1024)S(1)} %iota_add_fusion, s32[1024]{0:T(1024)S(1)} %all-reduce), kind=kLoop, calls=%fused_computation.7 | loop fusion | flops 12580864 | bytes 8409088 | tf_op jit(solution)/shard_map/reduce_sum | solution.py:13
  269.5 131.2 %all-reduce.2 = (f32[1024]{0:T(1024)S(1)}, f32[1024]{0:T(1024)S(1)}) all-reduce(f32[1024]{0:T(1024)S(1)} %get-tuple-element.4, f32[1024]{0:T(1024)S(1)} %get-tuple-element.3), channel_id=1, replica_groups=mesh['vocab'=64,'hidden'=4] {'vocab'}, use_global_device_ids=true, to_apply=%region_4.5 | all-reduce | flops 2048 | bytes 16384 | tf_op jit(solution)/shard_map/psum | solution.py:39
  400.6 0.0 copy-start.2
  400.6 6.0 fusion.3
  406.6 0.0 copy-start
  406.6 1.9 copy-done
  408.5 0.0 copy-done.2
  408.5 0.0 copy-start.3
  408.5 6.4 %fusion.6 = f32[1024,896]{1,0:T(8,128)} fusion(bf16[1024,2048]{1,0:T(8,128)(2,1)S(1)} %fusion.3, bf16[2048,896]{1,0:T(8,128)(2,1)S(1)} %copy-done.2), kind=kOutput, calls=%fused_computation.13 | convolution fusion | flops 3758096384 | bytes 11534336 | tf_op jit(solution)/shard_map/dot_general | solution.py:43
  414.9 0.0 all-reduce.8.cloned.1.call-update
  415.6 0.6 subtract_reduce_fusion
  416.9 0.0 copy-done.3
  416.9 8.7 %fusion.7 = f32[2048,896]{1,0:T(8,128)} fusion(bf16[1024,2048]{1,0:T(8,128)(2,1)} %copy-done, bf16[1024,896]{1,0:T(8,128)(2,1)S(1)} %copy-done.3), kind=kOutput, calls=%fused_computation.14 | convolution fusion | flops 3758096384 | bytes 13369344 | tf_op jit(solution)/shard_map/dot_general | solution.py:48
  425.6 179.2 %all-reduce.8.cloned.1.call-done = f32[1024,896]{1,0:T(8,128)} async-done(((f32[1024,896]{1,0:T(8,128)}), f32[1024,896]{1,0:T(8,128)}) %all-reduce.8.cloned.1.call-update) | async-done | bytes 3670032
  604.8 1.4 constant_dynamic-slice_fusion
  (2 shorter events, 0.0 us)
Async XLA Ops:
  7.2 83.5 %all-gather.2.cloned.1.call-start = ((), (), s32[]{:S(2)}) async-start(), calls=%async_computation | async-start | bytes 1863680 | tf_op jit(solution)/shard_map/all_gather | solution.py:27
  7.9 255.2 %all-reduce.6.cloned.1.call-start = ((), (), s32[]{:S(2)}) async-start(), calls=%async_computation.1 | async-start | bytes 16777216 | tf_op jit(solution)/shard_map/psum | solution.py:37
  101.0 0.7 copy-start.1
  101.0 1.9 copy-start.4
  101.0 503.8 %all-reduce.8.cloned.1.call-start = ((), (), s32[]{:S(2)}) async-start(), calls=%async_computation.2 | async-start | bytes 7340032
  400.6 7.9 %copy-start.2 = (bf16[2048,896]{1,0:T(8,128)(2,1)S(1)}, bf16[2048,896]{1,0:T(8,128)(2,1)}, u32[]{:S(2)}) copy-start(bf16[2048,896]{1,0:T(8,128)(2,1)} %param.4) | copy-start | bytes 11010052
  406.6 1.9 copy-start
  408.5 8.3 %copy-start.3 = (bf16[1024,896]{1,0:T(8,128)(2,1)S(1)}, bf16[1024,896]{1,0:T(8,128)(2,1)}, u32[]{:S(2)}) copy-start(bf16[1024,896]{1,0:T(8,128)(2,1)} %all-gather.2.cloned.1.call-done) | copy-start | bytes 5505028
Sparse Core Ops, SparseCore 0:
  10.7 79.9 all-gather.1
  101.1 161.8 all-reduce.5
  415.1 189.6 all-reduce.7
where the time goes:
time: 614 us
  waiting for transfers between devices  404 us (66%)
  blocking collectives  149 us (24%)
  matrix products  25.4 us (4%)
  between operations  16.9 us (3%)
  other arithmetic  13 us (2%)
    unnamed x4, waiting for transfers between devices  180 us
    psum x1, waiting for transfers between devices, local(): logits = lax.psum(partial_value, 'hidden')  142 us
    psum x1, blocking collectives, local(): totals, chosen = lax.psum((local_total, local_chosen), 'vocab')  131 us
    all_gather x1, waiting for transfers between devices, local(): lax.all_gather(hidden_states, 'vocab', axis=0, tiled=True)  82.7 us
    unnamed x1, blocking collectives  18.3 us
  transfers between devices with their start and end apart: 3, of which 3 were waited for; matrix products, arithmetic and copies ran while one was open for 2% of the time, Pallas kernels for 0%

commit v1 on v0

v1 whole, which is shorter than its diff:
```python
import functools

import jax
import jax.numpy as jnp
from jax import lax
from jax.experimental import pallas as pl
from jax.experimental.pallas import tpu as pltpu
from jax.sharding import Mesh, PartitionSpec as P

soft_ceiling = 30.0
swap = [(0, 1), (1, 0)]
f32, bf16 = jnp.float32, jnp.bfloat16
VM = pltpu.VMEM
NT = (((1,), (1,)), ((), ()))

def over(value, axis, n, s):
    return lax.ppermute(value, axis, [(i, (i + s) % n) for i in range(n)])


def beside_of(value):
    return lax.ppermute(value, "c", swap)


def tie(*values):
    return lax.optimization_barrier(values)


def in_hbm(*values):
    return [pltpu.with_memory_space_constraint(v, pltpu.HBM) for v in values]


def limit(mib):
    return pltpu.CompilerParams(vmem_limit_bytes=mib << 20)


def logits_kernel(pos, *refs):
    rows_ref, *ins = refs[:9]
    capped_ref, sums_ref, wanted_ref, own_ref, states, table, held, sems, out_sems = refs[9:]
    quarter, full = table.shape[1:]
    width = full // 4
    tokens = states.shape[0]
    copies = []

    def bring(src, dst):
        copy = pltpu.make_async_copy(src, dst, sems.at[len(copies)])
        copies.append(copy)
        copy.start()

    y = pos[1]
    size = tokens // 16
    for h in range(2):
        for z in range(8):
            bring(rows_ref.at[pl.ds((2 * z + h) * size, size)], states.at[pl.ds((8 * h + z) * size, size)])
    n_states = len(copies)
    ends = []
    for half in range(2):
        quarters, *arrived = ins[4 * half : 4 * half + 4]
        for s, src in enumerate([quarters.at[y], *arrived]):
            lanes = pl.ds(pl.multiple_of(lax.rem(y + 4 - s, 4) * width, width), width)
            bring(src, table.at[half, :, lanes])
        ends.append(len(copies))
    for copy in copies[:n_states]:
        copy.wait()

    lane = lax.broadcasted_iota(jnp.int32, (8, 128), 1)
    scale = jnp.where(lane == 0, 1.0, jnp.where(lane == 1, 256.0, jnp.where(lane == 2, 65536.0, 0.0)))
    scale = scale.astype(bf16)
    wanted = lax.dot_general(scale, states[:, full:], NT, preferred_element_type=f32)[:1].astype(jnp.int32)
    wanted_ref[...] = wanted
    total = jnp.zeros((1, tokens), f32)
    chosen = jnp.zeros((1, tokens), f32)
    tile = held.shape[1]
    outs = [pltpu.make_async_copy(states.at[:, pl.ds(pl.multiple_of(y * width, width), width)], own_ref, out_sems.at[held.shape[0]])]
    outs[0].start()
    for half in range(2):
        for copy in copies[ends[half - 1] if half else n_states : ends[half]]:
            copy.wait()
        for t in range(quarter // tile):
            rows = pl.ds(t * tile, tile)
            logits = lax.dot_general(table[half, rows], states[:, :full], NT, preferred_element_type=f32)
            capped = soft_ceiling * jnp.tanh(logits / soft_ceiling)
            k = half * (quarter // tile) + t
            held[k] = capped
            outs.append(pltpu.make_async_copy(held.at[k], capped_ref.at[pl.ds(k * tile, tile)], out_sems.at[k]))
            outs[-1].start()
            total = total + jnp.sum(jnp.exp(capped), 0, keepdims=True)
            ids = pos[4 + half] + t * tile + lax.broadcasted_iota(jnp.int32, (tile, tokens), 0)
            chosen = chosen + jnp.sum(jnp.where(ids == wanted, capped, 0.0), 0, keepdims=True)
    per = tokens // 4
    sums = [v[:, a * per : (a + 1) * per] for v in (total, chosen) for a in range(4)]
    sums_ref[...] = jnp.concatenate(sums, 0)
    for out in outs:
        out.wait()


def logits_of(pos, token_rows, entry_pieces, width, quarter):
    tokens = token_rows.shape[0]
    tile = 512
    lanes = 4 * width + 128
    return pl.pallas_call(
        logits_kernel,
        out_shape=(
            jax.ShapeDtypeStruct((2 * quarter, tokens), f32),
            jax.ShapeDtypeStruct((8, 128), f32),
            jax.ShapeDtypeStruct((1, tokens), jnp.int32),
            jax.ShapeDtypeStruct((tokens, width), bf16),
        ),
        in_specs=[pl.BlockSpec(memory_space=pltpu.SMEM)]
        + [pl.BlockSpec(memory_space=pltpu.HBM)] * (1 + len(entry_pieces)),
        out_specs=(
            pl.BlockSpec(memory_space=pltpu.HBM),
            pl.BlockSpec(memory_space=VM),
            pl.BlockSpec(memory_space=VM),
            pl.BlockSpec(memory_space=pltpu.HBM),
        ),
        scratch_shapes=[
            VM((tokens, lanes), bf16),
            VM((2, quarter, 4 * width), bf16),
            VM((2 * quarter // tile, tile, tokens), f32),
            pltpu.SemaphoreType.DMA((24,)),
            pltpu.SemaphoreType.DMA((2 * quarter // tile + 1,)),
        ],
        compiler_params=limit(26),
        cost_estimate=pl.CostEstimate(
            flops=2 * 2 * quarter * tokens * 4 * width, bytes_accessed=13 << 20, transcendentals=4 * quarter * tokens
        ),
    )(pos, *in_hbm(token_rows, *entry_pieces))


def logit_grad(capped, totals, ids, wanted):
    ratio = capped / soft_ceiling
    share = jnp.exp(capped) / totals - jnp.where(ids == wanted, 1.0, 0.0)
    return (share * (1.0 - ratio * ratio)).astype(bf16)


def grad_kernel(half, pos, got, capped_ref, wanted_ref, sums_ref, *outs):
    sums = got[0]
    for k in range(1, got.shape[0]):
        sums = sums + got[k]
    sums_ref[...] = sums
    tile, wide = capped_ref.shape
    start = pl.program_id(0) * tile
    first = jnp.where(start < half, pos[4], pos[5] - half) + start
    ids = first + lax.broadcasted_iota(jnp.int32, (tile, 128), 0)
    for at in range(0, wide, 128):
        row = at // 128
        wanted = wanted_ref[:, at : at + 128]
        out = outs[2 * at // wide]
        put = at % (wide // 2)
        out[:, put : put + 128] = logit_grad(capped_ref[:, at : at + 128], sums[row : row + 1], ids, wanted)


def grad_of(pos, got, capped, wanted):
    entries, wide = capped.shape
    tile = entries // 4
    return pl.pallas_call(
        functools.partial(grad_kernel, entries // 2),
        grid=(entries // tile,),
        out_shape=(jax.ShapeDtypeStruct((8, 128), f32),) + (jax.ShapeDtypeStruct((entries, wide // 2), bf16),) * 2,
        in_specs=[
            pl.BlockSpec(memory_space=pltpu.SMEM),
            pl.BlockSpec(got.shape, lambda i: (0, 0, 0)),
            pl.BlockSpec((tile, wide), lambda i: (i, 0)),
            pl.BlockSpec(wanted.shape, lambda i: (0, 0)),
        ],
        out_specs=(pl.BlockSpec((8, 128), lambda i: (0, 0)),) + (pl.BlockSpec((tile, wide // 2), lambda i: (i, 0)),) * 2,
        compiler_params=limit(12),
        cost_estimate=pl.CostEstimate(flops=8 * entries * wide, bytes_accessed=3 << 20, transcendentals=entries * wide),
    )(pos, got, *in_hbm(capped), wanted)


def pack_kernel(*refs):
    ins, out, sems = refs[:-2], refs[-2], refs[-1]
    half = ins[0].shape[0] // 2
    copies = []
    for s, ref in enumerate(ins):
        copies.append(pltpu.make_async_copy(ref.at[pl.ds(half, half)], out.at[pl.ds(s * half, half)], sems.at[s]))
        copies[-1].start()
    for copy in copies:
        copy.wait()


def lower_halves(pieces):
    rows, wide = pieces[0].shape
    return pl.pallas_call(
        pack_kernel,
        out_shape=jax.ShapeDtypeStruct((len(pieces) * rows // 2, wide), bf16),
        in_specs=[pl.BlockSpec(memory_space=pltpu.HBM)] * len(pieces),
        out_specs=pl.BlockSpec(memory_space=pltpu.HBM),
        scratch_shapes=[pltpu.SemaphoreType.DMA((len(pieces),))],
        compiler_params=limit(1),
        cost_estimate=pl.CostEstimate(flops=0, bytes_accessed=1 << 16, transcendentals=0),
    )(*in_hbm(*pieces))


def table_kernel(pos, own_states, beside_states, *refs):
    moved, lower, (out, grads, states, result, sems, out_sems) = refs[:8], refs[8:10], refs[10:]
    tokens, width = own_states.shape
    quarter = grads.shape[1]
    copies = []

    def bring(src, dst):
        copy = pltpu.make_async_copy(src, dst, sems.at[len(copies)])
        copies.append(copy)
        copy.start()

    bring(own_states, states.at[pl.ds(0, tokens)])
    bring(beside_states, states.at[pl.ds(tokens, tokens)])
    for s in range(4):
        for h in range(2):
            wide = tokens // 2
            bring(moved[4 * h + s].at[pl.ds(0, quarter)], grads.at[s, :, pl.ds(h * wide, wide)])
            bring(lower[h].at[pl.ds(s * quarter, quarter)], grads.at[s, :, pl.ds(tokens + h * wide, wide)])
    for copy in copies[:2]:
        copy.wait()
    outs = [None, None]
    tile = 256
    for s in range(4):
        for copy in copies[2 + 4 * s : 6 + 4 * s]:
            copy.wait()
        slot = s % 2
        if outs[slot] is not None:
            outs[slot].wait()

        @pl.loop(0, quarter // tile)
        def _(i):
            rows = pl.ds(pl.multiple_of(i * tile, tile), tile)
            result[slot, rows, :] = jnp.dot(grads[s, rows, :], states[...], preferred_element_type=f32)

        at = pl.multiple_of(lax.rem(pos[1] + 4 - s, 4) * quarter, quarter)
        outs[slot] = pltpu.make_async_copy(result.at[slot], out.at[pl.ds(at, quarter)], out_sems.at[slot])
        outs[slot].start()
    for copy in outs:
        copy.wait()


def table_grad_of(pos, own_states, beside_states, pieces, entries):
    tokens, width = own_states.shape
    quarter = entries // 4
    return pl.pallas_call(
        table_kernel,
        out_shape=jax.ShapeDtypeStruct((entries, width), f32),
        in_specs=[pl.BlockSpec(memory_space=pltpu.SMEM)] + [pl.BlockSpec(memory_space=pltpu.HBM)] * (2 + len(pieces)),
        out_specs=pl.BlockSpec(memory_space=pltpu.HBM),
        scratch_shapes=[
            VM((4, quarter, 2 * tokens), bf16),
            VM((2 * tokens, width), bf16),
            VM((2, quarter, width), f32),
            pltpu.SemaphoreType.DMA((18,)),
            pltpu.SemaphoreType.DMA((2,)),
        ],
        compiler_params=limit(20),
        cost_estimate=pl.CostEstimate(flops=1 << 20, bytes_accessed=1 << 18, transcendentals=0),
    )(pos, *in_hbm(own_states, beside_states, *pieces))


def local(hidden_states, embedding, targets):
    z, x, c, y = (lax.axis_index(a) for a in ("z", "x", "c", "y"))
    rows, width = hidden_states.shape
    entries = embedding.shape[0]
    quarter = entries // 4
    tokens = 32 * rows
    chip = (z * 4 + x) * 2
    first = [(chip + c) * entries + y * quarter, (chip + 1 - c) * entries + y * quarter]
    pos = jnp.stack([x, y, z, c, *first]).astype(jnp.int32)

    digits = jnp.stack([targets & 255, (targets >> 8) & 255, targets >> 16], 1).astype(bf16)
    block = jnp.concatenate([hidden_states, jnp.pad(digits, ((0, 0), (0, 125)))], 1)
    got = lax.all_to_all(jnp.broadcast_to(block, (16, *block.shape)), ("x", "y"), 0, 0, tiled=True)

    quarters = embedding.reshape(4, quarter, width)
    beside = beside_of(embedding).reshape(4, quarter, width)

    def quarter_at(q, k):
        return lax.dynamic_index_in_dim(q, (y + k) % 4, 0, False)

    own = {s: over(quarter_at(quarters, s), "y", 4, s) for s in (1, 3, 2)}
    other = {s: beside_of(own[s]) for s in (1, 3, 2)}

    got = got.reshape(4, 4, 2, rows // 2, width + 128).transpose(2, 0, 1, 3, 4)
    at_x = jnp.concatenate([got[:, :, k, :, :width] for k in range(4)] + [got[:, :, 0, :, width:]], 3)
    token_rows = lax.all_gather(at_x.reshape(4 * rows, -1), "z", axis=0, tiled=True)

    entry_pieces = (quarters, own[1], own[2], own[3], beside, other[1], other[2], other[3])
    capped, sums, wanted, own_states = logits_of(pos, token_rows, entry_pieces, width, quarter)

    got = lax.all_to_all(jnp.broadcast_to(sums, (16, *sums.shape)), ("x", "y"), 0, 0, tiled=True)
    sums = jnp.sum(got, 0)
    got = lax.all_to_all(jnp.broadcast_to(sums, (8, *sums.shape)), "z", 0, 0, tiled=True)
    sums, *grad = grad_of(pos, got, capped, wanted)
    beside_states = beside_of(own_states)
    moved = [[g] + [over(g, "y", 4, s) for s in (1, 2, 3)] for g in grad]

    def back(pieces):
        part = None
        for s in (0, 1, 3, 2):
            term = lax.dot_general(pieces[s], both[s], (((0,), (0,)), ((), ())), preferred_element_type=f32)
            part = term if part is None else part + term
        return part.astype(bf16).reshape(32, rows // 2, width)

    late, beside_late, moved[0][0] = tie(quarters, beside, moved[0][0])
    both = [jnp.concatenate([quarter_at(late, -s), quarter_at(beside_late, -s)]) for s in range(4)]
    home = back(moved[0])
    moved[1][2], home = tie(moved[1][2], home)
    got = [lax.all_to_all(home, ("z", "x"), 0, 0, tiled=True)]
    home = back(moved[1])
    got.append(lax.all_to_all(home, ("z", "x"), 0, 0, tiled=True))
    lower = [beside_of(lower_halves(pieces)) for pieces in moved]
    table_grad = table_grad_of(pos, own_states, beside_states, [*moved[0], *moved[1], *lower], entries)
    got[1], table_grad = tie(got[1], table_grad)
    hidden_grad = jnp.concatenate([jnp.sum(v.astype(f32), 0) for v in got], 0)

    terms = jnp.sum(jnp.log(sums[:4]) - sums[4:])
    loss = (terms + beside_of(terms)) / (2 * tokens)

    return (loss, hidden_grad, table_grad)


def solution(mesh):
    cut = Mesh(mesh.devices.reshape(8, 4, 2, 4), ("z", "x", "c", "y"))
    vocab = ("z", "x", "c")
    placed = (P(vocab, "y"), P(vocab, "y"), P(vocab))
    return jax.shard_map(
        local,
        mesh=cut,
        in_specs=placed,
        out_specs=(P(), P(vocab, "y"), P(vocab, "y")),
        check_vma=False,
    )
```

time: 614 us -> 213 us (0.35)
  waiting for transfers between devices: 404 us -> 76.3 us
  blocking collectives: 149 us -> 43.2 us
  starting transfers between devices: 0.12 us -> 25.5 us
  Pallas kernels: 0 us -> 24 us
  matrix products: 25.4 us -> 12.1 us
  other arithmetic: 13 us -> 3.86 us
    unnamed x4 -> x1, waiting for transfers between devices: 180 us -> 0.02 us
    psum x1 -> x0, waiting for transfers between devices: 142 us -> none  [local(): logits = lax.psum(partial_value, 'hidden')]
    psum x1 -> x0, blocking collectives: 131 us -> none  [local(): totals, chosen = lax.psum((local_total, local_chosen), 'vocab')]
    all_gather x1, waiting for transfers between devices: 82.7 us -> 2.75 us  [local(): lax.all_gather(at_x.reshape(4 * rows, -1), 'z', axis=0, tiled=True)]
    ppermute x0 -> x17, waiting for transfers between devices: none -> 67.2 us  [the longest x9 63.4 us: over(): return lax.ppermute(value, axis, [(i, (i + s) % n) for i in range(n)])]
    all_to_all x0 -> x3, blocking collectives: none -> 43.2 us  [the longest x1 17.3 us: local(): lax.all_to_all(jnp.broadcast_to(block, (16, *block.shape)), ('x', 'y'), 0...]
    pallas_call x0 -> x5, Pallas kernels: none -> 24 us  [the longest x1 9.4 us: table_grad_of(): pl.pallas_call(table_kernel, out_shape=jax.ShapeDtypeStruct((entries, wid...]
    unnamed x1 -> x0, blocking collectives: 18.3 us -> none
  transfers between devices with their start and end apart: 3 -> 20, of which waited for: 3 -> 10; matrix products, arithmetic and copies ran while one was open for 2% -> 9% of each run, Pallas kernels for 0% -> 6%
where the time goes in v1:
time: 213 us; the launch traced here: 211 us
  waiting for transfers between devices  76.3 us (36%)
  blocking collectives  43.2 us (20%)
  starting transfers between devices  25.5 us (12%)
  Pallas kernels  24 us (11%)
  between operations  16.9 us (8%)
  matrix products  12.1 us (6%)
  local copies, waits for them, and re-layouts  8.65 us (4%)
  other arithmetic  3.86 us (2%)
    ppermute x9, waiting for transfers between devices, over(): return lax.ppermute(value, axis, [(i, (i + s) % n) for i in range(n)])  63.4 us
    all_to_all x1, blocking collectives, local(): lax.all_to_all(jnp.broadcast_to(block, (16, *block.shape)), ('x', 'y'), 0...  17.3 us
    ppermute x9, starting transfers between devices, over(): return lax.ppermute(value, axis, [(i, (i + s) % n) for i in range(n)])  14.6 us
    all_to_all x1, blocking collectives, local(): lax.all_to_all(jnp.broadcast_to(sums, (16, *sums.shape)), ('x', 'y'), 0,...  13.3 us
    all_to_all x1, blocking collectives, local(): lax.all_to_all(jnp.broadcast_to(sums, (8, *sums.shape)), 'z', 0, 0, tiled...  12.5 us
    dot_general x8, matrix products, back(): lax.dot_general(pieces[s], both[s], (((0,), (0,)), ((), ())), preferred_e...  12.1 us
    pallas_call x1, Pallas kernels, table_grad_of(): pl.pallas_call(table_kernel, out_shape=jax.ShapeDtypeStruct((entries, wid...  9.4 us
    pallas_call x1, Pallas kernels, logits_of(): pl.pallas_call(logits_kernel, out_shape=(jax.ShapeDtypeStruct((2 * quarte...  9.37 us
  transfers between devices with their start and end apart: 20, of which 10 were waited for; matrix products, arithmetic and copies ran while one was open for 9% of the time, Pallas kernels for 6%

profile of v1, /device:TPU:8, one launch (start us, length us, event | category | flops | bytes accessed | tf_op | source)
XLA Modules:
  0.0 210.6 jit_solution(8851323283086846788)
XLA Ops:
  7.2 0.7 convert_bitcast_fusion.2
  7.9 0.1 copy.19
  8.0 0.8 fusion.11
  8.8 17.3 %all_to_all.25 = bf16[16,16,1024]{2,1,0:T(8,128)(2,1)S(1)} all-to-all(bf16[16,16,1024]{2,1,0:T(8,128)(2,1)S(1)} %broadcast_in_dim.9), channel_id=1, replica_groups=mesh['z'=8,'x'=4,'c'=2,'y'=4] {'x','y'}, dimensions={0} | all-to-all | bytes 1048576 | tf_op jit(solution)/shard_map/all_to_all | solution.py:269
  26.4 0.8 copy-done.20
  27.3 2.0 dynamic-slice_bitcast_fusion.8
  29.3 0.6 collective-permute-start
  29.9 3.0 %collective-permute-start.1 = (bf16[512,896]{1,0:T(8,128)(2,1)S(1)}, bf16[512,896]{1,0:T(8,128)(2,1)S(1)}, u32[]{:S(2)}, u32[]{:S(2)}) collective-permute-start(bf16[512,896]{1,0:T(8,128)(2,1)S(1)} %get-tuple-element.40), channel_id=1, source_target_pairs={{0,2},{1,3},{2,0},{3,1},{4,6},{5,7},{6,4},{7,5},{8,10},{9,11},{10,... | collective-permute-start | bytes 2752520 | tf_op jit(solution)/shard_map/ppermute | solution.py:17
  32.9 19.6 %collective-permute-done.refs_2_ = bf16[512,896]{1,0:T(8,128)(2,1)S(1)} collective-permute-done((bf16[512,896]{1,0:T(8,128)(2,1)S(1)}, bf16[512,896]{1,0:T(8,128)(2,1)S(1)}, u32[]{:S(2)}, u32[]{:S(2)}) %collective-permute-start) | collective-permute-done | bytes 917536 | tf_op jit(solution)/shard_map/ppermute | solution.py:17
  52.5 2.1 collective-permute-done.1.refs_3_
  54.6 18.8 %collective-permute-done.2.refs_4_ = bf16[512,896]{1,0:T(8,128)(2,1)S(1)} collective-permute-done((bf16[512,896]{1,0:T(8,128)(2,1)S(1)}, bf16[512,896]{1,0:T(8,128)(2,1)S(1)}, u32[]{:S(2)}, u32[]{:S(2)}) %collective-permute-start.2) | collective-permute-done | bytes 917536 | tf_op jit(solution)/shard_map/ppermute | solution.py:17
  73.4 0.1 collective-permute-start.6
  73.7 2.4 %collective-permute-done.6.refs_8_ = bf16[512,896]{1,0:T(8,128)(2,1)} collective-permute-done((bf16[512,896]{1,0:T(8,128)(2,1)S(1)}, bf16[512,896]{1,0:T(8,128)(2,1)}, u32[]{:S(2)}, u32[]{:S(2)}) %collective-permute-start.6) | collective-permute-done | bytes 917536 | tf_op jit(solution)/shard_map/ppermute | solution.py:21
  76.1 2.7 %all-gather.2.cloned.1.call-done.refs_0_ = bf16[512,3712]{1,0:T(8,128)(2,1)} async-done(((bf16[64,3712]{1,0:T(8,128)(2,1)}), bf16[512,3712]{1,0:T(8,128)(2,1)}) %all-gather.2.cloned.1.call-update) | async-done | bytes 3801104 | tf_op jit(solution)/shard_map/all_gather | solution.py:282
  78.8 9.4 %shard_map.58 = (f32[1024,512]{1,0:T(8,128)S(1)}, f32[8,128]{1,0:T(8,128)S(1)}, s32[1,512]{1,0:T(1,128)S(1)}, bf16[512,896]{1,0:T(8,128)(2,1)}) custom-call(s32[6]{0:T(128)S(1)} %stack.43.pos, bf16[512,3712]{1,0:T(8,128)(2,1)} %all-gather.2.cloned.1.call-done.refs_0_, bf16[4,512,896]{2,1,0:T(8,128)(2,1)} %bitcast.57, bf16[512,896]{1,0:T(8,128)(2,1)} %copy-done.8, ...), custom_call_target="tpu_custom_call" | custom-call | flops 3758096384 | bytes 13631488 | tf_op jit(solution)/shard_map/pallas_call | solution.py:100
  88.2 1.3 copy-done
  89.5 13.3 %all_to_all.26 = f32[16,8,128]{2,1,0:T(8,128)S(1)} all-to-all(f32[16,8,128]{2,1,0:T(8,128)S(1)} %broadcast_in_dim.10), channel_id=1, replica_groups=mesh['z'=8,'x'=4,'c'=2,'y'=4] {'x','y'}, dimensions={0} | all-to-all | bytes 131072 | tf_op jit(solution)/shard_map/all_to_all | solution.py:287
  102.9 12.5 %all_to_all.27.got = f32[8,8,128]{2,1,0:T(8,128)S(1)} all-to-all(f32[8,8,128]{2,1,0:T(8,128)S(1)} %broadcast_in_dim.11), channel_id=1, replica_groups=mesh['z'=8,'x'=4,'c'=2,'y'=4] {'z'}, dimensions={0} | all-to-all | bytes 65536 | tf_op jit(solution)/shard_map/all_to_all | solution.py:289
  115.4 2.8 %shard_map.59 = (f32[8,128]{1,0:T(8,128)S(1)}, bf16[1024,256]{1,0:T(8,128)(2,1)S(1)}, bf16[1024,256]{1,0:T(8,128)(2,1)S(1)}) custom-call(s32[6]{0:T(128)S(1)} %stack.43.pos, f32[8,8,128]{2,1,0:T(8,128)S(1)} %all_to_all.27.got, f32[1024,512]{1,0:T(8,128)} %copy-done, s32[1,512]{1,0:T(1,128)S(1)} %get-tuple-element.19.wanted_ref), custom_call_target="tpu_custom_call" | custom-call | flops 4194304 | bytes 3145728 | tf_op jit(solution)/shard_map/pallas_call | solution.py:156
  118.3 0.9 collective-permute-start.9
  119.1 2.7 %collective-permute-start.11 = (bf16[1024,256]{1,0:T(8,128)(2,1)S(1)}, bf16[1024,256]{1,0:T(8,128)(2,1)S(1)}, u32[]{:S(2)}, u32[]{:S(2)}) collective-permute-start(bf16[1024,256]{1,0:T(8,128)(2,1)S(1)} %get-tuple-element.23.refs_0_), channel_id=1, source_target_pairs={{0,2},{1,3},{2,0},{3,1},{4,6},{5,7},{6,4},{7,5},{8,10},{9,11},{10,... | collective-permute-start | bytes 1572872 | tf_op jit(solution)/shard_map/ppermute | solution.py:17
  121.9 0.6 collective-permute-start.10
  122.5 0.8 collective-permute-start.8
  123.3 3.7 %dynamic-slice_bitcast_fusion.2 = (bf16[512,896]{1,0:T(8,128)(2,1)S(1)}, bf16[512,896]{1,0:T(8,128)(2,1)S(1)}, bf16[512,896]{1,0:T(8,128)(2,1)S(1)}, bf16[512,89...) fusion(bf16[4,512,896]{2,1,0:T(8,128)(2,1)} %bitcast.21.refs_5_, ...), kind=kLoop, calls=%fused_computation.22 | loop fusion | bytes 14680080 | tf_op jit(solution)/shard_map/jit(dynamic_index_in_dim)/squeeze | solution.py:275
  127.0 21.8 %collective-permute-done.9.refs_1_ = bf16[1024,256]{1,0:T(8,128)(2,1)} collective-permute-done((bf16[1024,256]{1,0:T(8,128)(2,1)S(1)}, bf16[1024,256]{1,0:T(8,128)(2,1)}, u32[]{:S(2)}, u32[]{:S(2)}) %collective-permute-start.9) | collective-permute-done | bytes 524320 | tf_op jit(solution)/shard_map/ppermute | solution.py:17
  148.9 3.1 %collective-permute-start.12 = (bf16[1024,256]{1,0:T(8,128)(2,1)S(1)}, bf16[1024,256]{1,0:T(8,128)(2,1)}, u32[]{:S(2)}, u32[]{:S(2)}) collective-permute-start(bf16[1024,256]{1,0:T(8,128)(2,1)S(1)} %get-tuple-element.21.refs_0_.refs_4_), channel_id=1, source_target_pairs={{0,1},{1,2},{2,3},{3,0},{4,5},{5,6},{6,7},{7,4},{8,9},{9,10},{10,1... | collective-permute-start | bytes 1572872 | tf_op jit(solution)/shard_map/ppermute | solution.py:17
  152.0 1.8 fusion.9
  153.8 0.7 convolution_add_fusion.3
  154.6 2.9 %collective-permute-start.13 = (bf16[1024,256]{1,0:T(8,128)(2,1)S(1)}, bf16[1024,256]{1,0:T(8,128)(2,1)}, u32[]{:S(2)}, u32[]{:S(2)}) collective-permute-start(bf16[1024,256]{1,0:T(8,128)(2,1)S(1)} %get-tuple-element.21.refs_0_.refs_4_), channel_id=1, source_target_pairs={{0,3},{1,0},{2,1},{3,2},{4,7},{5,4},{6,5},{7,6},{8,11},{9,8},{10,9... | collective-permute-start | bytes 1572872 | tf_op jit(solution)/shard_map/ppermute | solution.py:17
  157.4 0.7 fusion.7
  158.2 1.5 fusion.5
  159.7 4.6 %all-to-all-start.3 = ((bf16[32,8,896]{2,1,0:T(8,128)(2,1)}), bf16[32,8,896]{2,1,0:T(8,128)(2,1)}, u32[]{:S(2)}, u32[]{:S(2)}) async-start(bf16[32,8,896]{2,1,0:T(8,128)(2,1)} %fusion.5), calls=%async_computation.3 | async-start | bytes 917504 | tf_op jit(solution)/shard_map/all_to_all | solution.py:305
  164.3 2.1 fusion.6
  166.4 1.2 shard_map.60
  167.8 1.0 collective-permute-done.13.refs_3_.refs_7_
  168.8 1.2 shard_map.61
  170.2 1.9 fusion.8
  172.1 0.7 convolution_add_fusion.1
  172.8 0.4 copy-done.5
  173.3 2.6 %fusion.4 = bf16[32,8,896]{2,1,0:T(8,128)(2,1)} fusion(f32[256,896]{1,0:T(8,128)S(1)} %fusion.6, f32[256,896]{1,0:T(8,128)S(1)} %convolution_add_fusion.1, bf16[1024,256]{1,0:T(8,128)(2,1)} %collective-permute-done.13.refs_3_.refs_7_, bf16[512,896]{1,0:T(8,128)(2,1)S(1)} %get-tuple-element.35, bf16[512,896]{1,0:T(8,128)(2,1)S(1)} %copy-done.5), kind=kOutput, calls=%fused_computation.12 | convolution fusion | flops 474120192 | bytes 4653056 | tf_op jit(solution)/shard_map/dot_general | solution.py:297
  175.9 3.4 %all-to-all-done.3 = bf16[32,8,896]{2,1,0:T(8,128)(2,1)} async-done(((bf16[32,8,896]{2,1,0:T(8,128)(2,1)}), bf16[32,8,896]{2,1,0:T(8,128)(2,1)}, u32[]{:S(2)}, u32[]{:S(2)}) %all-to-all-start.3) | async-done | bytes 458784 | tf_op jit(solution)/shard_map/all_to_all | solution.py:305
  179.3 5.9 %all-to-all-start.4 = ((bf16[32,8,896]{2,1,0:T(8,128)(2,1)}), bf16[32,8,896]{2,1,0:T(8,128)(2,1)S(1)}, u32[]{:S(2)}, u32[]{:S(2)}) async-start(bf16[32,8,896]{2,1,0:T(8,128)(2,1)} %fusion.4), calls=%async_computation.4 | async-start | bytes 917504 | tf_op jit(solution)/shard_map/all_to_all | solution.py:307
  185.2 0.6 subtract_reduce_fusion
  185.8 1.4 collective-permute-done.7
  188.4 1.1 convert_reduce_fusion.1
  189.5 9.4 %shard_map.62 = f32[2048,896]{1,0:T(8,128)} custom-call(s32[6]{0:T(128)S(1)} %stack.43.pos, bf16[512,896]{1,0:T(8,128)(2,1)} %get-tuple-element.28.own_states, bf16[512,896]{1,0:T(8,128)(2,1)} %collective-permute-done.14.beside_states, bf16[1024,256]{1,0:T(8,128)(2,1)} %copy-done.1, bf16[1024,256]{1,0:T(8,128)(2,1)} %collective-permute-done.9.refs_1_, ...), custom_call_target="tpu_custom_call" | custom-call | flops 1048576 | bytes 262144 | tf_op jit(solution)/shard_map/pallas_call | solution.py:240
  198.9 3.0 %all-to-all-done.4 = bf16[32,8,896]{2,1,0:T(8,128)(2,1)S(1)} async-done(((bf16[32,8,896]{2,1,0:T(8,128)(2,1)}), bf16[32,8,896]{2,1,0:T(8,128)(2,1)S(1)}, u32[]{:S(2)}, u32[]{:S(2)}) %all-to-all-start.4) | async-done | bytes 458784 | tf_op jit(solution)/shard_map/all_to_all | solution.py:307
  202.0 0.6 pad_maximum_fusion.12
  (78 shorter events, 0.9 us)
Async XLA Ops:
  7.2 71.6 %all-gather.2.cloned.1.call-start = ((), (), s32[]{:S(2)}) async-start(), calls=%async_computation.5 | async-start | bytes 4276224 | tf_op jit(solution)/shard_map/all_gather | solution.py:282
  26.4 0.8 copy-start.20
  27.2 48.9 %collective-permute-start.3 = (bf16[2048,896]{1,0:T(8,128)(2,1)}, bf16[2048,896]{1,0:T(8,128)(2,1)}, u32[]{:S(2)}, u32[]{:S(2)}) collective-permute-start(bf16[2048,896]{1,0:T(8,128)(2,1)} %param.4), channel_id=1, source_target_pairs={{0,4},{4,0},{1,5},{5,1},{2,6},{6,2},{3,7},{7,3},{8,12},{12,8},{9,1... | collective-permute-start | bytes 11010056 | tf_op jit(solution)/shard_map/ppermute | solution.py:21
  29.3 23.2 %collective-permute-start = (bf16[512,896]{1,0:T(8,128)(2,1)S(1)}, bf16[512,896]{1,0:T(8,128)(2,1)S(1)}, u32[]{:S(2)}, u32[]{:S(2)}) collective-permute-start(bf16[512,896]{1,0:T(8,128)(2,1)S(1)} %get-tuple-element.41), channel_id=1, source_target_pairs={{0,1},{1,2},{2,3},{3,0},{4,5},{5,6},{6,7},{7,4},{8,9},{9,10},{10,1... | collective-permute-start | bytes 2752520 | tf_op jit(solution)/shard_map/ppermute | solution.py:17
  29.9 24.7 %collective-permute-start.1 = (bf16[512,896]{1,0:T(8,128)(2,1)S(1)}, bf16[512,896]{1,0:T(8,128)(2,1)S(1)}, u32[]{:S(2)}, u32[]{:S(2)}) collective-permute-start(bf16[512,896]{1,0:T(8,128)(2,1)S(1)} %get-tuple-element.40), channel_id=1, source_target_pairs={{0,2},{1,3},{2,0},{3,1},{4,6},{5,7},{6,4},{7,5},{8,10},{9,11},{10,... | collective-permute-start | bytes 2752520 | tf_op jit(solution)/shard_map/ppermute | solution.py:17
  32.9 40.6 %collective-permute-start.2 = (bf16[512,896]{1,0:T(8,128)(2,1)S(1)}, bf16[512,896]{1,0:T(8,128)(2,1)S(1)}, u32[]{:S(2)}, u32[]{:S(2)}) collective-permute-start(bf16[512,896]{1,0:T(8,128)(2,1)S(1)} %get-tuple-element.39), channel_id=1, source_target_pairs={{0,3},{1,0},{2,1},{3,2},{4,7},{5,4},{6,5},{7,6},{8,11},{9,8},{10,9... | collective-permute-start | bytes 2752520 | tf_op jit(solution)/shard_map/ppermute | solution.py:17
  52.5 26.3 %copy-start.8 = (bf16[512,896]{1,0:T(8,128)(2,1)}, bf16[512,896]{1,0:T(8,128)(2,1)S(1)}, u32[]{:S(2)}) copy-start(bf16[512,896]{1,0:T(8,128)(2,1)S(1)} %collective-permute-done.refs_2_) | copy-start | bytes 2752516
  52.5 21.1 %collective-permute-start.4 = (bf16[512,896]{1,0:T(8,128)(2,1)S(1)}, bf16[512,896]{1,0:T(8,128)(2,1)}, u32[]{:S(2)}, u32[]{:S(2)}) collective-permute-start(bf16[512,896]{1,0:T(8,128)(2,1)S(1)} %collective-permute-done.refs_2_), channel_id=1, source_target_pairs={{0,4},{4,0},{1,5},{5,1},{2,6},{6,2},{3,7},{7,3},{8,12},{12,8},{9,1... | collective-permute-start | bytes 2752520 | tf_op jit(solution)/shard_map/ppermute | solution.py:21
  54.6 24.2 %copy-start.9 = (bf16[512,896]{1,0:T(8,128)(2,1)}, bf16[512,896]{1,0:T(8,128)(2,1)S(1)}, u32[]{:S(2)}) copy-start(bf16[512,896]{1,0:T(8,128)(2,1)S(1)} %collective-permute-done.1.refs_3_) | copy-start | bytes 2752516
  54.6 19.1 %collective-permute-start.5 = (bf16[512,896]{1,0:T(8,128)(2,1)S(1)}, bf16[512,896]{1,0:T(8,128)(2,1)}, u32[]{:S(2)}, u32[]{:S(2)}) collective-permute-start(bf16[512,896]{1,0:T(8,128)(2,1)S(1)} %collective-permute-done.1.refs_3_), channel_id=1, source_target_pairs={{0,4},{4,0},{1,5},{5,1},{2,6},{6,2},{3,7},{7,3},{8,12},{12,8},{9,1... | collective-permute-start | bytes 2752520 | tf_op jit(solution)/shard_map/ppermute | solution.py:21
  73.4 5.4 %copy-start.10 = (bf16[512,896]{1,0:T(8,128)(2,1)}, bf16[512,896]{1,0:T(8,128)(2,1)S(1)}, u32[]{:S(2)}) copy-start(bf16[512,896]{1,0:T(8,128)(2,1)S(1)} %collective-permute-done.2.refs_4_) | copy-start | bytes 2752516
  73.4 2.6 %collective-permute-start.6 = (bf16[512,896]{1,0:T(8,128)(2,1)S(1)}, bf16[512,896]{1,0:T(8,128)(2,1)}, u32[]{:S(2)}, u32[]{:S(2)}) collective-permute-start(bf16[512,896]{1,0:T(8,128)(2,1)S(1)} %collective-permute-done.2.refs_4_), channel_id=1, source_target_pairs={{0,4},{4,0},{1,5},{5,1},{2,6},{6,2},{3,7},{7,3},{8,12},{12,8},{9,1... | collective-permute-start | bytes 2752520 | tf_op jit(solution)/shard_map/ppermute | solution.py:21
  88.2 1.3 copy-start
  118.2 35.5 %copy-start.1 = (bf16[1024,256]{1,0:T(8,128)(2,1)}, bf16[1024,256]{1,0:T(8,128)(2,1)S(1)}, u32[]{:S(2)}) copy-start(bf16[1024,256]{1,0:T(8,128)(2,1)S(1)} %get-tuple-element.23.refs_0_) | copy-start | bytes 1572868
  118.2 36.3 %copy-start.2 = (bf16[1024,256]{1,0:T(8,128)(2,1)}, bf16[1024,256]{1,0:T(8,128)(2,1)S(1)}, u32[]{:S(2)}) copy-start(bf16[1024,256]{1,0:T(8,128)(2,1)S(1)} %get-tuple-element.21.refs_0_.refs_4_) | copy-start | bytes 1572868
  118.3 30.6 %collective-permute-start.9 = (bf16[1024,256]{1,0:T(8,128)(2,1)S(1)}, bf16[1024,256]{1,0:T(8,128)(2,1)}, u32[]{:S(2)}, u32[]{:S(2)}) collective-permute-start(bf16[1024,256]{1,0:T(8,128)(2,1)S(1)} %get-tuple-element.23.refs_0_), channel_id=1, source_target_pairs={{0,1},{1,2},{2,3},{3,0},{4,5},{5,6},{6,7},{7,4},{8,9},{9,10},{10,1... | collective-permute-start | bytes 1572872 | tf_op jit(solution)/shard_map/ppermute | solution.py:17
  119.1 70.4 %collective-permute-start.14 = (bf16[512,896]{1,0:T(8,128)(2,1)}, bf16[512,896]{1,0:T(8,128)(2,1)}, u32[]{:S(2)}, u32[]{:S(2)}) collective-permute-start(bf16[512,896]{1,0:T(8,128)(2,1)} %get-tuple-element.28.own_states), channel_id=1, source_target_pairs={{0,4},{4,0},{1,5},{5,1},{2,6},{6,2},{3,7},{7,3},{8,12},{12,8},{9,1... | collective-permute-start | bytes 2752520 | tf_op jit(solution)/shard_map/ppermute | solution.py:21
  119.1 35.4 %collective-permute-start.11 = (bf16[1024,256]{1,0:T(8,128)(2,1)S(1)}, bf16[1024,256]{1,0:T(8,128)(2,1)S(1)}, u32[]{:S(2)}, u32[]{:S(2)}) collective-permute-start(bf16[1024,256]{1,0:T(8,128)(2,1)S(1)} %get-tuple-element.23.refs_0_), channel_id=1, source_target_pairs={{0,2},{1,3},{2,0},{3,1},{4,6},{5,7},{6,4},{7,5},{8,10},{9,11},{10,... | collective-permute-start | bytes 1572872 | tf_op jit(solution)/shard_map/ppermute | solution.py:17
  121.9 36.3 %collective-permute-start.10 = (bf16[1024,256]{1,0:T(8,128)(2,1)S(1)}, bf16[1024,256]{1,0:T(8,128)(2,1)S(1)}, u32[]{:S(2)}, u32[]{:S(2)}) collective-permute-start(bf16[1024,256]{1,0:T(8,128)(2,1)S(1)} %get-tuple-element.23.refs_0_), channel_id=1, source_target_pairs={{0,3},{1,0},{2,1},{3,2},{4,7},{5,4},{6,5},{7,6},{8,11},{9,8},{10,9... | collective-permute-start | bytes 1572872 | tf_op jit(solution)/shard_map/ppermute | solution.py:17
  122.5 37.2 %collective-permute-start.8 = (bf16[1024,256]{1,0:T(8,128)(2,1)S(1)}, bf16[1024,256]{1,0:T(8,128)(2,1)}, u32[]{:S(2)}, u32[]{:S(2)}) collective-permute-start(bf16[1024,256]{1,0:T(8,128)(2,1)S(1)} %get-tuple-element.21.refs_0_.refs_4_), channel_id=1, source_target_pairs={{0,2},{1,3},{2,0},{3,1},{4,6},{5,7},{6,4},{7,5},{8,10},{9,11},{10,... | collective-permute-start | bytes 1572872 | tf_op jit(solution)/shard_map/ppermute | solution.py:17
  127.0 26.8 %copy-start.15 = (bf16[512,896]{1,0:T(8,128)(2,1)}, bf16[512,896]{1,0:T(8,128)(2,1)S(1)}, u32[]{:S(2)}) copy-start(bf16[512,896]{1,0:T(8,128)(2,1)S(1)} %get-tuple-element.37) | copy-start | bytes 2752516
  127.0 26.8 %copy-start.17 = (bf16[512,896]{1,0:T(8,128)(2,1)}, bf16[512,896]{1,0:T(8,128)(2,1)S(1)}, u32[]{:S(2)}) copy-start(bf16[512,896]{1,0:T(8,128)(2,1)S(1)} %get-tuple-element.50) | copy-start | bytes 2752516
  127.0 26.8 %copy-start.11 = (bf16[512,896]{1,0:T(8,128)(2,1)}, bf16[512,896]{1,0:T(8,128)(2,1)S(1)}, u32[]{:S(2)}) copy-start(bf16[512,896]{1,0:T(8,128)(2,1)S(1)} %get-tuple-element.38) | copy-start | bytes 2752516
  127.0 26.8 %copy-start.13 = (bf16[512,896]{1,0:T(8,128)(2,1)}, bf16[512,896]{1,0:T(8,128)(2,1)S(1)}, u32[]{:S(2)}) copy-start(bf16[512,896]{1,0:T(8,128)(2,1)S(1)} %get-tuple-element.49) | copy-start | bytes 2752516
  127.0 30.4 %copy-start.19 = (bf16[512,896]{1,0:T(8,128)(2,1)}, bf16[512,896]{1,0:T(8,128)(2,1)S(1)}, u32[]{:S(2)}) copy-start(bf16[512,896]{1,0:T(8,128)(2,1)S(1)} %get-tuple-element.51) | copy-start | bytes 2752516
  127.0 31.2 %copy-start.4 = (bf16[512,896]{1,0:T(8,128)(2,1)}, bf16[512,896]{1,0:T(8,128)(2,1)S(1)}, u32[]{:S(2)}) copy-start(bf16[512,896]{1,0:T(8,128)(2,1)S(1)} %get-tuple-element.52) | copy-start | bytes 2752516
  148.9 18.9 %collective-permute-start.12 = (bf16[1024,256]{1,0:T(8,128)(2,1)S(1)}, bf16[1024,256]{1,0:T(8,128)(2,1)}, u32[]{:S(2)}, u32[]{:S(2)}) collective-permute-start(bf16[1024,256]{1,0:T(8,128)(2,1)S(1)} %get-tuple-element.21.refs_0_.refs_4_), channel_id=1, source_target_pairs={{0,1},{1,2},{2,3},{3,0},{4,5},{5,6},{6,7},{7,4},{8,9},{9,10},{10,1... | collective-permute-start | bytes 1572872 | tf_op jit(solution)/shard_map/ppermute | solution.py:17
  154.5 3.6 %copy-start.7 = (bf16[1024,256]{1,0:T(8,128)(2,1)}, bf16[1024,256]{1,0:T(8,128)(2,1)S(1)}, u32[]{:S(2)}) copy-start(bf16[1024,256]{1,0:T(8,128)(2,1)S(1)} %collective-permute-done.11.refs_2_) | copy-start | bytes 1572868
  154.6 14.2 %collective-permute-start.13 = (bf16[1024,256]{1,0:T(8,128)(2,1)S(1)}, bf16[1024,256]{1,0:T(8,128)(2,1)}, u32[]{:S(2)}, u32[]{:S(2)}) collective-permute-start(bf16[1024,256]{1,0:T(8,128)(2,1)S(1)} %get-tuple-element.21.refs_0_.refs_4_), channel_id=1, source_target_pairs={{0,3},{1,0},{2,1},{3,2},{4,7},{5,4},{6,5},{7,6},{8,11},{9,8},{10,9... | collective-permute-start | bytes 1572872 | tf_op jit(solution)/shard_map/ppermute | solution.py:17
  158.2 1.5 copy-start.6
  159.7 19.5 %all-to-all-start.3 = ((bf16[32,8,896]{2,1,0:T(8,128)(2,1)}), bf16[32,8,896]{2,1,0:T(8,128)(2,1)}, u32[]{:S(2)}, u32[]{:S(2)}) async-start(bf16[32,8,896]{2,1,0:T(8,128)(2,1)} %fusion.5), calls=%async_computation.3 | async-start | bytes 917504 | tf_op jit(solution)/shard_map/all_to_all | solution.py:305
  167.7 2.5 %copy-start.16 = (bf16[512,896]{1,0:T(8,128)(2,1)S(1)}, bf16[512,896]{1,0:T(8,128)(2,1)}, u32[]{:S(2)}) copy-start(bf16[512,896]{1,0:T(8,128)(2,1)} %copy-done.15) | copy-start | bytes 2752516
  167.7 2.5 %copy-start.18 = (bf16[512,896]{1,0:T(8,128)(2,1)S(1)}, bf16[512,896]{1,0:T(8,128)(2,1)}, u32[]{:S(2)}) copy-start(bf16[512,896]{1,0:T(8,128)(2,1)} %copy-done.17) | copy-start | bytes 2752516
  167.7 21.8 %collective-permute-start.15 = (bf16[2048,256]{1,0:T(8,128)(2,1)S(1)}, bf16[2048,256]{1,0:T(8,128)(2,1)}, u32[]{:S(2)}, u32[]{:S(2)}) collective-permute-start(bf16[2048,256]{1,0:T(8,128)(2,1)S(1)} %shard_map.60), channel_id=1, source_target_pairs={{0,4},{4,0},{1,5},{5,1},{2,6},{6,2},{3,7},{7,3},{8,12},{12,8},{9,1... | collective-permute-start | bytes 3145736 | tf_op jit(solution)/shard_map/ppermute | solution.py:21
  170.0 2.1 copy-start.3
  170.0 2.1 copy-start.12
  170.0 2.1 copy-start.14
  170.0 19.5 %collective-permute-start.16 = (bf16[2048,256]{1,0:T(8,128)(2,1)S(1)}, bf16[2048,256]{1,0:T(8,128)(2,1)}, u32[]{:S(2)}, u32[]{:S(2)}) collective-permute-start(bf16[2048,256]{1,0:T(8,128)(2,1)S(1)} %shard_map.61), channel_id=1, source_target_pairs={{0,4},{4,0},{1,5},{5,1},{2,6},{6,2},{3,7},{7,3},{8,12},{12,8},{9,1... | collective-permute-start | bytes 3145736 | tf_op jit(solution)/shard_map/ppermute | solution.py:21
  172.1 1.2 copy-start.5
  179.3 22.6 %all-to-all-start.4 = ((bf16[32,8,896]{2,1,0:T(8,128)(2,1)}), bf16[32,8,896]{2,1,0:T(8,128)(2,1)S(1)}, u32[]{:S(2)}, u32[]{:S(2)}) async-start(bf16[32,8,896]{2,1,0:T(8,128)(2,1)} %fusion.4), calls=%async_computation.4 | async-start | bytes 917504 | tf_op jit(solution)/shard_map/all_to_all | solution.py:307
  185.8 1.4 collective-permute-start.7
Sparse Core Ops, SparseCore 0:
  27.3 51.4 all-gather.1

commit v2 on v1

--- a/solution.py
+++ b/solution.py
@@ -34,8 +34,8 @@
 
 
 def logits_kernel(pos, *refs):
-    rows_ref, *ins = refs[:9]
-    capped_ref, sums_ref, wanted_ref, own_ref, states, table, held, sems, out_sems = refs[9:]
+    pieces, ins = refs[:9], refs[9:17]
+    capped_ref, sums_ref, wanted_ref, own_ref, states, table, held, sems, out_sems = refs[17:]
     quarter, full = table.shape[1:]
     width = full // 4
     tokens = states.shape[0]
@@ -48,9 +48,12 @@
 
     y = pos[1]
     size = tokens // 16
-    for h in range(2):
-        for z in range(8):
-            bring(rows_ref.at[pl.ds((2 * z + h) * size, size)], states.at[pl.ds((8 * h + z) * size, size)])
+    for b in range(8):
+        place = lax.rem(pos[2] + b, 8)
+        for h in range(2):
+            src = pieces[4 + h] if b == 4 else pieces[b if b < 4 else b + 1].at[h]
+            row = pl.multiple_of((8 * h + place) * size, size)
+            bring(src, states.at[pl.ds(row, size)])
     n_states = len(copies)
     ends = []
     for half in range(2):
@@ -93,8 +96,8 @@
         out.wait()
 
 
-def logits_of(pos, token_rows, entry_pieces, width, quarter):
-    tokens = token_rows.shape[0]
+def logits_of(pos, row_pieces, entry_pieces, width, quarter):
+    tokens = 16 * row_pieces[0].shape[1]
     tile = 512
     lanes = 4 * width + 128
     return pl.pallas_call(
@@ -106,7 +109,7 @@
             jax.ShapeDtypeStruct((tokens, width), bf16),
         ),
         in_specs=[pl.BlockSpec(memory_space=pltpu.SMEM)]
-        + [pl.BlockSpec(memory_space=pltpu.HBM)] * (1 + len(entry_pieces)),
+        + [pl.BlockSpec(memory_space=pltpu.HBM)] * (len(row_pieces) + len(entry_pieces)),
         out_specs=(
             pl.BlockSpec(memory_space=pltpu.HBM),
             pl.BlockSpec(memory_space=VM),
@@ -124,7 +127,7 @@
         cost_estimate=pl.CostEstimate(
             flops=2 * 2 * quarter * tokens * 4 * width, bytes_accessed=13 << 20, transcendentals=4 * quarter * tokens
         ),
-    )(pos, *in_hbm(token_rows, *entry_pieces))
+    )(pos, *in_hbm(*row_pieces, *entry_pieces))
 
 
 def logit_grad(capped, totals, ids, wanted):
@@ -274,22 +277,35 @@
     def quarter_at(q, k):
         return lax.dynamic_index_in_dim(q, (y + k) % 4, 0, False)
 
-    own = {s: over(quarter_at(quarters, s), "y", 4, s) for s in (1, 3, 2)}
-    other = {s: beside_of(own[s]) for s in (1, 3, 2)}
+    own = {s: over(quarter_at(quarters, s), "y", 4, s) for s in (1, 3)}
 
     got = got.reshape(4, 4, 2, rows // 2, width + 128).transpose(2, 0, 1, 3, 4)
     at_x = jnp.concatenate([got[:, :, k, :, :width] for k in range(4)] + [got[:, :, 0, :, width:]], 3)
-    token_rows = lax.all_gather(at_x.reshape(4 * rows, -1), "z", axis=0, tiled=True)
+    at_x = at_x.reshape(2, 2 * rows, -1)
+    up, down = [at_x], [at_x]
+    for k in range(3):
+        up.append(over(up[-1], "z", 8, -1))
+        down.append(over(down[-1], "z", 8, 1))
+        if k == 1:
+            up[-1], down[-1], own[1], own[3] = tie(up[-1], down[-1], own[1], own[3])
+            send, own[1], own[3] = tie(quarter_at(quarters, 2), own[1], own[3])
+            own[2] = over(send, "y", 4, 2)
+    far = [over(up[3][0], "z", 8, -1), over(down[3][1], "z", 8, 1)]
+    own[2], *far = tie(own[2], *far)
+    other = {s: beside_of(own[s]) for s in (1, 3, 2)}
+    row_pieces = [*up, *far, down[3], down[2], down[1]]
 
     entry_pieces = (quarters, own[1], own[2], own[3], beside, other[1], other[2], other[3])
-    capped, sums, wanted, own_states = logits_of(pos, token_rows, entry_pieces, width, quarter)
+    capped, sums, wanted, own_states = logits_of(pos, row_pieces, entry_pieces, width, quarter)
 
     got = lax.all_to_all(jnp.broadcast_to(sums, (16, *sums.shape)), ("x", "y"), 0, 0, tiled=True)
     sums = jnp.sum(got, 0)
     got = lax.all_to_all(jnp.broadcast_to(sums, (8, *sums.shape)), "z", 0, 0, tiled=True)
     sums, *grad = grad_of(pos, got, capped, wanted)
     beside_states = beside_of(own_states)
-    moved = [[g] + [over(g, "y", 4, s) for s in (1, 2, 3)] for g in grad]
+    moved = [[grad[0]] + [over(grad[0], "y", 4, s) for s in (1, 2, 3)]]
+    grad[1], *moved[0][1:] = tie(grad[1], *moved[0][1:])
+    moved.append([grad[1]] + [over(grad[1], "y", 4, s) for s in (1, 2, 3)])
 
     def back(pieces):
         part = None
@@ -300,11 +316,14 @@
 
     late, beside_late, moved[0][0] = tie(quarters, beside, moved[0][0])
     both = [jnp.concatenate([quarter_at(late, -s), quarter_at(beside_late, -s)]) for s in range(4)]
-    home = back(moved[0])
-    moved[1][2], home = tie(moved[1][2], home)
-    got = [lax.all_to_all(home, ("z", "x"), 0, 0, tiled=True)]
-    home = back(moved[1])
-    got.append(lax.all_to_all(home, ("z", "x"), 0, 0, tiled=True))
+    home = [back(moved[0])]
+    got = [lax.all_to_all(home[0], ("z", "x"), 0, 0, tiled=True)]
+    moved[1][2], home[0] = tie(moved[1][2], home[0])
+    home.append(back(moved[1]))
+    home[1], got[0] = tie(home[1], got[0])
+    got.append(lax.all_to_all(home[1], ("z", "x"), 0, 0, tiled=True))
+    for k in range(2):
+        *moved[k], home[k] = tie(*moved[k], home[k])
     lower = [beside_of(lower_halves(pieces)) for pieces in moved]
     table_grad = table_grad_of(pos, own_states, beside_states, [*moved[0], *moved[1], *lower], entries)
     got[1], table_grad = tie(got[1], table_grad)

time: 213 us -> 196 us (0.920)
  blocking collectives: 43.2 us -> 21.4 us
  starting transfers between devices: 25.5 us -> 46.6 us
  between operations: 16.9 us -> 3.66 us
    all_to_all x1 -> x0, blocking collectives: 17.3 us -> none  [local(): lax.all_to_all(jnp.broadcast_to(block, (16, *block.shape)), ('x', 'y'), 0...]
    ppermute x9 -> x17, starting transfers between devices: 14.6 us -> 28.9 us  [over(): return lax.ppermute(value, axis, [(i, (i + s) % n) for i in range(n)])]
    all_to_all x2 -> x3, waiting for transfers between devices: 6.42 us -> 13.4 us  [the longest x1 10.1 us: local(): lax.all_to_all(jnp.broadcast_to(block, (16, *block.shape)), ('x', 'y'), 0...]
    all_to_all x2 -> x3, starting transfers between devices: 10.4 us -> 16 us  [the longest x1 7.39 us: local(): lax.all_to_all(jnp.broadcast_to(block, (16, *block.shape)), ('x', 'y'), 0...]
    ppermute x9 -> x17, waiting for transfers between devices: 63.4 us -> 58 us  [over(): return lax.ppermute(value, axis, [(i, (i + s) % n) for i in range(n)])]
    all_to_all x1, blocking collectives: 13.3 us -> 10.4 us  [local(): lax.all_to_all(jnp.broadcast_to(sums, (16, *sums.shape)), ('x', 'y'), 0,...]
    all_gather x1 -> x0, waiting for transfers between devices: 2.75 us -> none  [local(): lax.all_gather(at_x.reshape(4 * rows, -1), 'z', axis=0, tiled=True)]
  transfers between devices with their start and end apart: 20 -> 28, of which waited for: 10 -> 16; matrix products, arithmetic and copies ran while one was open for 9% -> 9% of each run, Pallas kernels for 6% -> 6%
where the time goes in v2:
time: 196 us; the launch traced here: 195 us
  waiting for transfers between devices  75.4 us (38%)
  starting transfers between devices  46.6 us (24%)
  Pallas kernels  23.8 us (12%)
  blocking collectives  21.4 us (11%)
  matrix products  10.7 us (5%)
  local copies, waits for them, and re-layouts  9.12 us (5%)
  other arithmetic  3.86 us (2%)
  between operations  3.66 us (2%)
    ppermute x17, waiting for transfers between devices, over(): return lax.ppermute(value, axis, [(i, (i + s) % n) for i in range(n)])  58 us
    ppermute x17, starting transfers between devices, over(): return lax.ppermute(value, axis, [(i, (i + s) % n) for i in range(n)])  28.9 us
    all_to_all x1, blocking collectives, local(): lax.all_to_all(jnp.broadcast_to(sums, (8, *sums.shape)), 'z', 0, 0, tiled...  11.1 us
    dot_general x8, matrix products, back(): lax.dot_general(pieces[s], both[s], (((0,), (0,)), ((), ())), preferred_e...  10.7 us
    all_to_all x1, blocking collectives, local(): lax.all_to_all(jnp.broadcast_to(sums, (16, *sums.shape)), ('x', 'y'), 0,...  10.4 us
    all_to_all x1, waiting for transfers between devices, local(): lax.all_to_all(jnp.broadcast_to(block, (16, *block.shape)), ('x', 'y'), 0...  10.1 us
    pallas_call x1, Pallas kernels, table_grad_of(): pl.pallas_call(table_kernel, out_shape=jax.ShapeDtypeStruct((entries, wid...  9.4 us
    pallas_call x1, Pallas kernels, logits_of(): pl.pallas_call(logits_kernel, out_shape=(jax.ShapeDtypeStruct((2 * quarte...  9.07 us
  transfers between devices with their start and end apart: 28, of which 16 were waited for; matrix products, arithmetic and copies ran while one was open for 9% of the time, Pallas kernels for 6%

profile of v2, /device:TPU:8, one launch (start us, length us, event | category | flops | bytes accessed | tf_op | source)
XLA Modules:
  0.0 194.6 jit_solution(11910573464875584479)
XLA Ops:
  1.4 0.8 fusion.13
  2.2 0.9 broadcast_in_dim.9
  3.0 7.4 %all-to-all-start = ((bf16[16,16,1024]{2,1,0:T(8,128)(2,1)}), bf16[16,16,1024]{2,1,0:T(8,128)(2,1)S(1)}, u32[]{:S(2)}, u32[]{:S(2)}) async-start(bf16[16,16,1024]{2,1,0:T(8,128)(2,1)} %broadcast_in_dim.9), calls=%async_computation | async-start | bytes 1048576 | tf_op jit(solution)/shard_map/all_to_all | solution.py:272
  10.4 10.1 %all-to-all-done = bf16[16,16,1024]{2,1,0:T(8,128)(2,1)S(1)} async-done(((bf16[16,16,1024]{2,1,0:T(8,128)(2,1)}), bf16[16,16,1024]{2,1,0:T(8,128)(2,1)S(1)}, u32[]{:S(2)}, u32[]{:S(2)}) %all-to-all-start) | async-done | bytes 524320 | tf_op jit(solution)/shard_map/all_to_all | solution.py:272
  20.7 5.9 %collective-permute-start = (bf16[2,32,3712]{2,1,0:T(8,128)(2,1)S(1)}, bf16[2,32,3712]{2,1,0:T(8,128)(2,1)S(1)}, u32[]{:S(2)}, u32[]{:S(2)}) collective-permute-start(bf16[2,32,3712]{2,1,0:T(8,128)(2,1)S(1)} %bitcast_dynamic-update-slice_fusion.4.refs_0_), channel_id=1, source_target_pairs={{0,224},{32,0},{64,32},{96,64},{128,96},{160,128},{192,160},{224,1... | collective-permute-start | bytes 1425416 | tf_op jit(solution)/shard_map/ppermute | solution.py:17
  26.6 2.0 %dynamic-slice_bitcast_fusion.8 = (bf16[512,896]{1,0:T(8,128)(2,1)S(1)}, bf16[512,896]{1,0:T(8,128)(2,1)S(1)}, bf16[512,896]{1,0:T(8,128)(2,1)S(1)}) fusion(bf16[4,512,896]{2,1,0:T(8,128)(2,1)} %bitcast.17.refs_9_, s32[]{:T(128)S(6)} %select_n.70, s32[]{:T(128)S(6)} %select_n.68, s32[]{:T(128)S(6)} %select_n.66), kind=kLoop, calls=%fused_computation.29 | loop fusion | bytes 5505036 | tf_op jit(solution)/shard_map/jit(dynamic_index_in_dim)/squeeze | solution.py:278
  29.2 1.5 collective-permute-start.5
  30.7 4.8 %collective-permute-done.refs_1_ = bf16[2,32,3712]{2,1,0:T(8,128)(2,1)S(1)} collective-permute-done((bf16[2,32,3712]{2,1,0:T(8,128)(2,1)S(1)}, bf16[2,32,3712]{2,1,0:T(8,128)(2,1)S(1)}, u32[]{:S(2)}, u32[]{:S(2)}) %collective-permute-start) | collective-permute-done | bytes 475168 | tf_op jit(solution)/shard_map/ppermute | solution.py:17
  35.5 3.7 %collective-permute-start.1 = (bf16[2,32,3712]{2,1,0:T(8,128)(2,1)S(1)}, bf16[2,32,3712]{2,1,0:T(8,128)(2,1)S(1)}, u32[]{:S(2)}, u32[]{:S(2)}) collective-permute-start(bf16[2,32,3712]{2,1,0:T(8,128)(2,1)S(1)} %collective-permute-done.refs_1_), channel_id=1, source_target_pairs={{0,224},{32,0},{64,32},{96,64},{128,96},{160,128},{192,160},{224,1... | collective-permute-start | bytes 1425416 | tf_op jit(solution)/shard_map/ppermute | solution.py:17
  39.3 9.9 %collective-permute-done.4.refs_10_ = bf16[512,896]{1,0:T(8,128)(2,1)S(1)} collective-permute-done((bf16[512,896]{1,0:T(8,128)(2,1)S(1)}, bf16[512,896]{1,0:T(8,128)(2,1)S(1)}, u32[]{:S(2)}, u32[]{:S(2)}) %collective-permute-start.4) | collective-permute-done | bytes 917536 | tf_op jit(solution)/shard_map/ppermute | solution.py:17
  49.5 1.1 collective-permute-done.3.refs_7_
  50.6 1.9 collective-permute-start.6
  52.5 4.0 %collective-permute-start.7 = (bf16[512,896]{1,0:T(8,128)(2,1)S(1)}, bf16[512,896]{1,0:T(8,128)(2,1)}, u32[]{:S(2)}, u32[]{:S(2)}) collective-permute-start(bf16[512,896]{1,0:T(8,128)(2,1)S(1)} %get-tuple-element.43), channel_id=1, source_target_pairs={{0,2},{1,3},{2,0},{3,1},{4,6},{5,7},{6,4},{7,5},{8,10},{9,11},{10,... | collective-permute-start | bytes 2752520 | tf_op jit(solution)/shard_map/ppermute | solution.py:17
  56.6 4.6 %collective-permute-done.6.refs_3_ = bf16[2,32,3712]{2,1,0:T(8,128)(2,1)S(1)} collective-permute-done((bf16[2,32,3712]{2,1,0:T(8,128)(2,1)S(1)}, bf16[2,32,3712]{2,1,0:T(8,128)(2,1)S(1)}, u32[]{:S(2)}, u32[]{:S(2)}) %collective-permute-start.6) | collective-permute-done | bytes 475168 | tf_op jit(solution)/shard_map/ppermute | solution.py:17
  61.2 2.4 %collective-permute-start.8 = (bf16[32,3712]{1,0:T(8,128)(2,1)S(1)}, bf16[32,3712]{1,0:T(8,128)(2,1)S(1)}, u32[]{:S(2)}, u32[]{:S(2)}) collective-permute-start(bf16[32,3712]{1,0:T(8,128)(2,1)S(1)} %slice_bitcast_fusion.1), channel_id=1, source_target_pairs={{0,224},{32,0},{64,32},{96,64},{128,96},{160,128},{192,160},{224,1... | collective-permute-start | bytes 712712 | tf_op jit(solution)/shard_map/ppermute | solution.py:17
  63.6 3.9 %collective-permute-done.9.refs_6_ = bf16[2,32,3712]{2,1,0:T(8,128)(2,1)S(1)} collective-permute-done((bf16[2,32,3712]{2,1,0:T(8,128)(2,1)S(1)}, bf16[2,32,3712]{2,1,0:T(8,128)(2,1)S(1)}, u32[]{:S(2)}, u32[]{:S(2)}) %collective-permute-start.9) | collective-permute-done | bytes 475168 | tf_op jit(solution)/shard_map/ppermute | solution.py:17
  68.2 6.7 %collective-permute-done.10.refs_5_ = bf16[32,3712]{1,0:T(8,128)(2,1)S(1)} collective-permute-done((bf16[32,3712]{1,0:T(8,128)(2,1)S(1)}, bf16[32,3712]{1,0:T(8,128)(2,1)S(1)}, u32[]{:S(2)}, u32[]{:S(2)}) %collective-permute-start.10) | collective-permute-done | bytes 237600 | tf_op jit(solution)/shard_map/ppermute | solution.py:17
  75.7 2.7 %collective-permute-done.13.refs_15_ = bf16[512,896]{1,0:T(8,128)(2,1)} collective-permute-done((bf16[512,896]{1,0:T(8,128)(2,1)}, bf16[512,896]{1,0:T(8,128)(2,1)}, u32[]{:S(2)}, u32[]{:S(2)}) %collective-permute-start.13) | collective-permute-done | bytes 917536 | tf_op jit(solution)/shard_map/ppermute | solution.py:21
  78.5 9.1 %shard_map.58 = (f32[1024,512]{1,0:T(8,128)S(1)}, f32[8,128]{1,0:T(8,128)S(1)}, s32[1,512]{1,0:T(1,128)S(1)}, bf16[512,896]{1,0:T(8,128)(2,1)S(1)}) custom-call(s32[6]{0:T(128)S(1)} %stack.43.pos, bf16[2,32,3712]{2,1,0:T(8,128)(2,1)} %copy-done.27, bf16[2,32,3712]{2,1,0:T(8,128)(2,1)} %copy-done.28, bf16[2,32,3712]{2,1,0:T(8,128)(2,1)} %copy-done.30, ...), custom_call_target="tpu_custom_call" | custom-call | flops 3758096384 | bytes 13631488 | tf_op jit(solution)/shard_map/pallas_call | solution.py:103
  87.6 1.3 copy-done.1
  88.9 10.4 %all_to_all.25 = f32[16,8,128]{2,1,0:T(8,128)S(1)} all-to-all(f32[16,8,128]{2,1,0:T(8,128)S(1)} %broadcast_in_dim.10), channel_id=1, replica_groups=mesh['z'=8,'x'=4,'c'=2,'y'=4] {'x','y'}, dimensions={0} | all-to-all | bytes 131072 | tf_op jit(solution)/shard_map/all_to_all | solution.py:301
  99.3 11.1 %all_to_all.26.got = f32[8,8,128]{2,1,0:T(8,128)S(1)} all-to-all(f32[8,8,128]{2,1,0:T(8,128)S(1)} %broadcast_in_dim.11), channel_id=1, replica_groups=mesh['z'=8,'x'=4,'c'=2,'y'=4] {'z'}, dimensions={0} | all-to-all | bytes 65536 | tf_op jit(solution)/shard_map/all_to_all | solution.py:303
  110.3 2.8 %shard_map.59 = (f32[8,128]{1,0:T(8,128)S(1)}, bf16[1024,256]{1,0:T(8,128)(2,1)S(1)}, bf16[1024,256]{1,0:T(8,128)(2,1)S(1)}) custom-call(s32[6]{0:T(128)S(1)} %stack.43.pos, f32[8,8,128]{2,1,0:T(8,128)S(1)} %all_to_all.26.got, f32[1024,512]{1,0:T(8,128)} %copy-done.1, s32[1,512]{1,0:T(1,128)S(1)} %get-tuple-element.52.wanted_ref), custom_call_target="tpu_custom_call" | custom-call | flops 4194304 | bytes 3145728 | tf_op jit(solution)/shard_map/pallas_call | solution.py:159
  113.2 0.9 collective-permute-start.16
  114.0 2.7 %collective-permute-start.17 = (bf16[1024,256]{1,0:T(8,128)(2,1)S(1)}, bf16[1024,256]{1,0:T(8,128)(2,1)S(1)}, u32[]{:S(2)}, u32[]{:S(2)}) collective-permute-start(bf16[1024,256]{1,0:T(8,128)(2,1)S(1)} %get-tuple-element.67.refs_0_), channel_id=1, source_target_pairs={{0,2},{1,3},{2,0},{3,1},{4,6},{5,7},{6,4},{7,5},{8,10},{9,11},{10,... | collective-permute-start | bytes 1572872 | tf_op jit(solution)/shard_map/ppermute | solution.py:17
  117.4 3.8 %dynamic-slice_bitcast_fusion.2 = (bf16[512,896]{1,0:T(8,128)(2,1)S(1)}, bf16[512,896]{1,0:T(8,128)(2,1)S(1)}, bf16[512,896]{1,0:T(8,128)(2,1)S(1)}, bf16[512,89...) fusion(bf16[4,512,896]{2,1,0:T(8,128)(2,1)} %bitcast.23.refs_13, ...), kind=kLoop, calls=%fused_computation.23 | loop fusion | bytes 14680080 | tf_op jit(solution)/shard_map/jit(dynamic_index_in_dim)/squeeze | solution.py:278
  121.4 6.7 %collective-permute-done.16.refs_1_ = bf16[1024,256]{1,0:T(8,128)(2,1)S(1)} collective-permute-done((bf16[1024,256]{1,0:T(8,128)(2,1)S(1)}, bf16[1024,256]{1,0:T(8,128)(2,1)S(1)}, u32[]{:S(2)}, u32[]{:S(2)}) %collective-permute-start.16) | collective-permute-done | bytes 524320 | tf_op jit(solution)/shard_map/ppermute | solution.py:17
  128.1 2.3 %collective-permute-done.17.refs_2_ = bf16[1024,256]{1,0:T(8,128)(2,1)S(1)} collective-permute-done((bf16[1024,256]{1,0:T(8,128)(2,1)S(1)}, bf16[1024,256]{1,0:T(8,128)(2,1)S(1)}, u32[]{:S(2)}, u32[]{:S(2)}) %collective-permute-start.17) | collective-permute-done | bytes 524320 | tf_op jit(solution)/shard_map/ppermute | solution.py:17
  130.4 7.5 %collective-permute-done.18.refs_3_ = bf16[1024,256]{1,0:T(8,128)(2,1)S(1)} collective-permute-done((bf16[1024,256]{1,0:T(8,128)(2,1)S(1)}, bf16[1024,256]{1,0:T(8,128)(2,1)S(1)}, u32[]{:S(2)}, u32[]{:S(2)}) %collective-permute-start.18) | collective-permute-done | bytes 524320 | tf_op jit(solution)/shard_map/ppermute | solution.py:17
  137.9 2.5 %collective-permute-start.21 = (bf16[1024,256]{1,0:T(8,128)(2,1)S(1)}, bf16[1024,256]{1,0:T(8,128)(2,1)}, u32[]{:S(2)}, u32[]{:S(2)}) collective-permute-start(bf16[1024,256]{1,0:T(8,128)(2,1)S(1)} %get-tuple-element.71.refs_0_.refs_4_), channel_id=1, source_target_pairs={{0,2},{1,3},{2,0},{3,1},{4,6},{5,7},{6,4},{7,5},{8,10},{9,11},{10,... | collective-permute-start | bytes 1572872 | tf_op jit(solution)/shard_map/ppermute | solution.py:17
  140.6 1.8 collective-permute-start.19
  143.2 0.7 convolution_add_fusion.1
  143.9 0.7 fusion.8
  144.7 1.5 fusion.5
  146.2 4.7 %all-to-all-start.3 = ((bf16[32,8,896]{2,1,0:T(8,128)(2,1)}), bf16[32,8,896]{2,1,0:T(8,128)(2,1)}, u32[]{:S(2)}, u32[]{:S(2)}) async-start(bf16[32,8,896]{2,1,0:T(8,128)(2,1)} %fusion.5), calls=%async_computation.3 | async-start | bytes 917504 | tf_op jit(solution)/shard_map/all_to_all | solution.py:320
  151.0 1.3 shard_map.60
  152.6 1.7 collective-permute-done.21.refs_2_.refs_6_
  154.3 1.8 fusion.7
  156.1 8.4 %collective-permute-done.20.refs_3_.refs_7_ = bf16[1024,256]{1,0:T(8,128)(2,1)} collective-permute-done((bf16[1024,256]{1,0:T(8,128)(2,1)S(1)}, bf16[1024,256]{1,0:T(8,128)(2,1)}, u32[]{:S(2)}, u32[]{:S(2)}) %collective-permute-start.20) | collective-permute-done | bytes 524320 | tf_op jit(solution)/shard_map/ppermute | solution.py:17
  164.6 1.8 fusion.9
  166.4 1.9 fusion.11
  168.4 1.5 fusion.6
  169.9 1.2 shard_map.61
  171.7 3.9 %all-to-all-start.4 = ((bf16[32,8,896]{2,1,0:T(8,128)(2,1)}), bf16[32,8,896]{2,1,0:T(8,128)(2,1)S(1)}, u32[]{:S(2)}, u32[]{:S(2)}) async-start(bf16[32,8,896]{2,1,0:T(8,128)(2,1)} %fusion.6), calls=%async_computation.4 | async-start | bytes 917504 | tf_op jit(solution)/shard_map/all_to_all | solution.py:324
  176.3 1.3 collective-permute-done.15
  178.9 1.1 convert_reduce_fusion.1
  180.0 9.4 %shard_map.62 = f32[2048,896]{1,0:T(8,128)} custom-call(s32[6]{0:T(128)S(1)} %stack.43.pos, bf16[512,896]{1,0:T(8,128)(2,1)} %copy-done.3, bf16[512,896]{1,0:T(8,128)(2,1)} %collective-permute-done.22.beside_states, bf16[1024,256]{1,0:T(8,128)(2,1)} %copy-done.2, bf16[1024,256]{1,0:T(8,128)(2,1)} %copy-done.13, bf16[1024,256]{1,0:T(8,128)(2,1)} %copy-done.14, ...), custom_call_target="tpu_custom_call" | custom-call | flops 1048576 | bytes 262144 | tf_op jit(solution)/shard_map/pallas_call | solution.py:243
  189.5 3.3 %all-to-all-done.4 = bf16[32,8,896]{2,1,0:T(8,128)(2,1)S(1)} async-done(((bf16[32,8,896]{2,1,0:T(8,128)(2,1)}), bf16[32,8,896]{2,1,0:T(8,128)(2,1)S(1)}, u32[]{:S(2)}, u32[]{:S(2)}) %all-to-all-start.4) | async-done | bytes 458784 | tf_op jit(solution)/shard_map/all_to_all | solution.py:324
  (114 shorter events, 7.4 us)
Async XLA Ops:
  3.0 17.5 %all-to-all-start = ((bf16[16,16,1024]{2,1,0:T(8,128)(2,1)}), bf16[16,16,1024]{2,1,0:T(8,128)(2,1)S(1)}, u32[]{:S(2)}, u32[]{:S(2)}) async-start(bf16[16,16,1024]{2,1,0:T(8,128)(2,1)} %broadcast_in_dim.9), calls=%async_computation | async-start | bytes 1048576 | tf_op jit(solution)/shard_map/all_to_all | solution.py:272
  20.7 14.8 %collective-permute-start = (bf16[2,32,3712]{2,1,0:T(8,128)(2,1)S(1)}, bf16[2,32,3712]{2,1,0:T(8,128)(2,1)S(1)}, u32[]{:S(2)}, u32[]{:S(2)}) collective-permute-start(bf16[2,32,3712]{2,1,0:T(8,128)(2,1)S(1)} %bitcast_dynamic-update-slice_fusion.4.refs_0_), channel_id=1, source_target_pairs={{0,224},{32,0},{64,32},{96,64},{128,96},{160,128},{192,160},{224,1... | collective-permute-start | bytes 1425416 | tf_op jit(solution)/shard_map/ppermute | solution.py:17
  26.6 12.6 %collective-permute-start.2 = (bf16[2,32,3712]{2,1,0:T(8,128)(2,1)S(1)}, bf16[2,32,3712]{2,1,0:T(8,128)(2,1)S(1)}, u32[]{:S(2)}, u32[]{:S(2)}) collective-permute-start(bf16[2,32,3712]{2,1,0:T(8,128)(2,1)S(1)} %bitcast_dynamic-update-slice_fusion.4.refs_0_), channel_id=1, source_target_pairs={{0,32},{32,64},{64,96},{96,128},{128,160},{160,192},{192,224},{224... | collective-permute-start | bytes 1425416 | tf_op jit(solution)/shard_map/ppermute | solution.py:17
  28.6 20.7 %collective-permute-start.4 = (bf16[512,896]{1,0:T(8,128)(2,1)S(1)}, bf16[512,896]{1,0:T(8,128)(2,1)S(1)}, u32[]{:S(2)}, u32[]{:S(2)}) collective-permute-start(bf16[512,896]{1,0:T(8,128)(2,1)S(1)} %get-tuple-element.87), channel_id=1, source_target_pairs={{0,1},{1,2},{2,3},{3,0},{4,5},{5,6},{6,7},{7,4},{8,9},{9,10},{10,1... | collective-permute-start | bytes 2752520 | tf_op jit(solution)/shard_map/ppermute | solution.py:17
  29.2 20.3 %collective-permute-start.5 = (bf16[512,896]{1,0:T(8,128)(2,1)S(1)}, bf16[512,896]{1,0:T(8,128)(2,1)S(1)}, u32[]{:S(2)}, u32[]{:S(2)}) collective-permute-start(bf16[512,896]{1,0:T(8,128)(2,1)S(1)} %get-tuple-element.86), channel_id=1, source_target_pairs={{0,3},{1,0},{2,1},{3,2},{4,7},{5,4},{6,5},{7,6},{8,11},{9,8},{10,9... | collective-permute-start | bytes 2752520 | tf_op jit(solution)/shard_map/ppermute | solution.py:17
  35.5 13.9 %copy-start.28 = (bf16[2,32,3712]{2,1,0:T(8,128)(2,1)}, bf16[2,32,3712]{2,1,0:T(8,128)(2,1)S(1)}, u32[]{:S(2)}) copy-start(bf16[2,32,3712]{2,1,0:T(8,128)(2,1)S(1)} %collective-permute-done.refs_1_) | copy-start | bytes 1425412
  35.5 13.9 %collective-permute-start.1 = (bf16[2,32,3712]{2,1,0:T(8,128)(2,1)S(1)}, bf16[2,32,3712]{2,1,0:T(8,128)(2,1)S(1)}, u32[]{:S(2)}, u32[]{:S(2)}) collective-permute-start(bf16[2,32,3712]{2,1,0:T(8,128)(2,1)S(1)} %collective-permute-done.refs_1_), channel_id=1, source_target_pairs={{0,224},{32,0},{64,32},{96,64},{128,96},{160,128},{192,160},{224,1... | collective-permute-start | bytes 1425416 | tf_op jit(solution)/shard_map/ppermute | solution.py:17
  39.2 11.4 %collective-permute-start.3 = (bf16[2,32,3712]{2,1,0:T(8,128)(2,1)S(1)}, bf16[2,32,3712]{2,1,0:T(8,128)(2,1)S(1)}, u32[]{:S(2)}, u32[]{:S(2)}) collective-permute-start(bf16[2,32,3712]{2,1,0:T(8,128)(2,1)S(1)} %collective-permute-done.2.refs_8_), channel_id=1, source_target_pairs={{0,32},{32,64},{64,96},{96,128},{128,160},{160,192},{192,224},{224... | collective-permute-start | bytes 1425416 | tf_op jit(solution)/shard_map/ppermute | solution.py:17
  39.2 39.2 %collective-permute-start.11 = (bf16[2048,896]{1,0:T(8,128)(2,1)}, bf16[2048,896]{1,0:T(8,128)(2,1)}, u32[]{:S(2)}, u32[]{:S(2)}) collective-permute-start(bf16[2048,896]{1,0:T(8,128)(2,1)} %param.4), channel_id=1, source_target_pairs={{0,4},{4,0},{1,5},{5,1},{2,6},{6,2},{3,7},{7,3},{8,12},{12,8},{9,1... | collective-permute-start | bytes 11010056 | tf_op jit(solution)/shard_map/ppermute | solution.py:21
  49.2 29.2 %copy-start.17 = (bf16[512,896]{1,0:T(8,128)(2,1)}, bf16[512,896]{1,0:T(8,128)(2,1)S(1)}, u32[]{:S(2)}) copy-start(bf16[512,896]{1,0:T(8,128)(2,1)S(1)} %collective-permute-done.4.refs_10_) | copy-start | bytes 2752516
  49.5 29.0 %copy-start.18 = (bf16[512,896]{1,0:T(8,128)(2,1)}, bf16[512,896]{1,0:T(8,128)(2,1)S(1)}, u32[]{:S(2)}) copy-start(bf16[512,896]{1,0:T(8,128)(2,1)S(1)} %collective-permute-done.5.refs_12_) | copy-start | bytes 2752516
  50.6 27.8 %copy-start.31 = (bf16[2,32,3712]{2,1,0:T(8,128)(2,1)}, bf16[2,32,3712]{2,1,0:T(8,128)(2,1)S(1)}, u32[]{:S(2)}) copy-start(bf16[2,32,3712]{2,1,0:T(8,128)(2,1)S(1)} %collective-permute-done.3.refs_7_) | copy-start | bytes 1425412
  50.6 10.6 %collective-permute-start.6 = (bf16[2,32,3712]{2,1,0:T(8,128)(2,1)S(1)}, bf16[2,32,3712]{2,1,0:T(8,128)(2,1)S(1)}, u32[]{:S(2)}, u32[]{:S(2)}) collective-permute-start(bf16[2,32,3712]{2,1,0:T(8,128)(2,1)S(1)} %collective-permute-done.1.refs_2_), channel_id=1, source_target_pairs={{0,224},{32,0},{64,32},{96,64},{128,96},{160,128},{192,160},{224,1... | collective-permute-start | bytes 1425416 | tf_op jit(solution)/shard_map/ppermute | solution.py:17
  52.5 22.4 %collective-permute-start.7 = (bf16[512,896]{1,0:T(8,128)(2,1)S(1)}, bf16[512,896]{1,0:T(8,128)(2,1)}, u32[]{:S(2)}, u32[]{:S(2)}) collective-permute-start(bf16[512,896]{1,0:T(8,128)(2,1)S(1)} %get-tuple-element.43), channel_id=1, source_target_pairs={{0,2},{1,3},{2,0},{3,1},{4,6},{5,7},{6,4},{7,5},{8,10},{9,11},{10,... | collective-permute-start | bytes 2752520 | tf_op jit(solution)/shard_map/ppermute | solution.py:17
  56.6 10.9 %collective-permute-start.9 = (bf16[2,32,3712]{2,1,0:T(8,128)(2,1)S(1)}, bf16[2,32,3712]{2,1,0:T(8,128)(2,1)S(1)}, u32[]{:S(2)}, u32[]{:S(2)}) collective-permute-start(bf16[2,32,3712]{2,1,0:T(8,128)(2,1)S(1)} %collective-permute-done.3.refs_7_), channel_id=1, source_target_pairs={{0,32},{32,64},{64,96},{96,128},{128,160},{160,192},{192,224},{224... | collective-permute-start | bytes 1425416 | tf_op jit(solution)/shard_map/ppermute | solution.py:17
  61.2 17.3 %copy-start.15 = (bf16[2,32,3712]{2,1,0:T(8,128)(2,1)}, bf16[2,32,3712]{2,1,0:T(8,128)(2,1)S(1)}, u32[]{:S(2)}) copy-start(bf16[2,32,3712]{2,1,0:T(8,128)(2,1)S(1)} %collective-permute-done.6.refs_3_) | copy-start | bytes 1425412
  61.2 6.5 %collective-permute-start.8 = (bf16[32,3712]{1,0:T(8,128)(2,1)S(1)}, bf16[32,3712]{1,0:T(8,128)(2,1)S(1)}, u32[]{:S(2)}, u32[]{:S(2)}) collective-permute-start(bf16[32,3712]{1,0:T(8,128)(2,1)S(1)} %slice_bitcast_fusion.1), channel_id=1, source_target_pairs={{0,224},{32,0},{64,32},{96,64},{128,96},{160,128},{192,160},{224,1... | collective-permute-start | bytes 712712 | tf_op jit(solution)/shard_map/ppermute | solution.py:17
  67.5 7.4 %collective-permute-start.10 = (bf16[32,3712]{1,0:T(8,128)(2,1)S(1)}, bf16[32,3712]{1,0:T(8,128)(2,1)S(1)}, u32[]{:S(2)}, u32[]{:S(2)}) collective-permute-start(bf16[32,3712]{1,0:T(8,128)(2,1)S(1)} %slice_bitcast_fusion), channel_id=1, source_target_pairs={{0,32},{32,64},{64,96},{96,128},{128,160},{160,192},{192,224},{224... | collective-permute-start | bytes 712712 | tf_op jit(solution)/shard_map/ppermute | solution.py:17
  67.6 8.1 %collective-permute-start.12 = (bf16[512,896]{1,0:T(8,128)(2,1)S(1)}, bf16[512,896]{1,0:T(8,128)(2,1)}, u32[]{:S(2)}, u32[]{:S(2)}) collective-permute-start(bf16[512,896]{1,0:T(8,128)(2,1)S(1)} %collective-permute-done.4.refs_10_), channel_id=1, source_target_pairs={{0,4},{4,0},{1,5},{5,1},{2,6},{6,2},{3,7},{7,3},{8,12},{12,8},{9,1... | collective-permute-start | bytes 2752520 | tf_op jit(solution)/shard_map/ppermute | solution.py:21
  67.7 8.0 %collective-permute-start.14 = (bf16[512,896]{1,0:T(8,128)(2,1)S(1)}, bf16[512,896]{1,0:T(8,128)(2,1)}, u32[]{:S(2)}, u32[]{:S(2)}) collective-permute-start(bf16[512,896]{1,0:T(8,128)(2,1)S(1)} %collective-permute-done.5.refs_12_), channel_id=1, source_target_pairs={{0,4},{4,0},{1,5},{5,1},{2,6},{6,2},{3,7},{7,3},{8,12},{12,8},{9,1... | collective-permute-start | bytes 2752520 | tf_op jit(solution)/shard_map/ppermute | solution.py:21
  75.6 2.8 %collective-permute-start.13 = (bf16[512,896]{1,0:T(8,128)(2,1)}, bf16[512,896]{1,0:T(8,128)(2,1)}, u32[]{:S(2)}, u32[]{:S(2)}) collective-permute-start(bf16[512,896]{1,0:T(8,128)(2,1)} %collective-permute-done.7.refs_11_), channel_id=1, source_target_pairs={{0,4},{4,0},{1,5},{5,1},{2,6},{6,2},{3,7},{7,3},{8,12},{12,8},{9,1... | collective-permute-start | bytes 2752520 | tf_op jit(solution)/shard_map/ppermute | solution.py:21
  88.9 82.4 %copy-start.3 = (bf16[512,896]{1,0:T(8,128)(2,1)}, bf16[512,896]{1,0:T(8,128)(2,1)S(1)}, u32[]{:S(2)}) copy-start(bf16[512,896]{1,0:T(8,128)(2,1)S(1)} %get-tuple-element.66.own_states) | copy-start | bytes 2752516
  113.2 30.0 %copy-start.2 = (bf16[1024,256]{1,0:T(8,128)(2,1)}, bf16[1024,256]{1,0:T(8,128)(2,1)S(1)}, u32[]{:S(2)}) copy-start(bf16[1024,256]{1,0:T(8,128)(2,1)S(1)} %get-tuple-element.67.refs_0_) | copy-start | bytes 1572868
  113.2 55.2 %copy-start = (bf16[1024,256]{1,0:T(8,128)(2,1)}, bf16[1024,256]{1,0:T(8,128)(2,1)S(1)}, u32[]{:S(2)}) copy-start(bf16[1024,256]{1,0:T(8,128)(2,1)S(1)} %get-tuple-element.71.refs_0_.refs_4_) | copy-start | bytes 1572868
  113.2 14.9 %collective-permute-start.16 = (bf16[1024,256]{1,0:T(8,128)(2,1)S(1)}, bf16[1024,256]{1,0:T(8,128)(2,1)S(1)}, u32[]{:S(2)}, u32[]{:S(2)}) collective-permute-start(bf16[1024,256]{1,0:T(8,128)(2,1)S(1)} %get-tuple-element.67.refs_0_), channel_id=1, source_target_pairs={{0,1},{1,2},{2,3},{3,0},{4,5},{5,6},{6,7},{7,4},{8,9},{9,10},{10,1... | collective-permute-start | bytes 1572872 | tf_op jit(solution)/shard_map/ppermute | solution.py:17
  114.0 16.4 %collective-permute-start.17 = (bf16[1024,256]{1,0:T(8,128)(2,1)S(1)}, bf16[1024,256]{1,0:T(8,128)(2,1)S(1)}, u32[]{:S(2)}, u32[]{:S(2)}) collective-permute-start(bf16[1024,256]{1,0:T(8,128)(2,1)S(1)} %get-tuple-element.67.refs_0_), channel_id=1, source_target_pairs={{0,2},{1,3},{2,0},{3,1},{4,6},{5,7},{6,4},{7,5},{8,10},{9,11},{10,... | collective-permute-start | bytes 1572872 | tf_op jit(solution)/shard_map/ppermute | solution.py:17
  116.8 21.1 %collective-permute-start.18 = (bf16[1024,256]{1,0:T(8,128)(2,1)S(1)}, bf16[1024,256]{1,0:T(8,128)(2,1)S(1)}, u32[]{:S(2)}, u32[]{:S(2)}) collective-permute-start(bf16[1024,256]{1,0:T(8,128)(2,1)S(1)} %get-tuple-element.67.refs_0_), channel_id=1, source_target_pairs={{0,3},{1,0},{2,1},{3,2},{4,7},{5,4},{6,5},{7,6},{8,11},{9,8},{10,9... | collective-permute-start | bytes 1572872 | tf_op jit(solution)/shard_map/ppermute | solution.py:17
  121.3 21.9 %copy-start.5 = (bf16[512,896]{1,0:T(8,128)(2,1)}, bf16[512,896]{1,0:T(8,128)(2,1)S(1)}, u32[]{:S(2)}) copy-start(bf16[512,896]{1,0:T(8,128)(2,1)S(1)} %get-tuple-element.84) | copy-start | bytes 2752516
  121.3 21.9 %copy-start.7 = (bf16[512,896]{1,0:T(8,128)(2,1)}, bf16[512,896]{1,0:T(8,128)(2,1)S(1)}, u32[]{:S(2)}) copy-start(bf16[512,896]{1,0:T(8,128)(2,1)S(1)} %get-tuple-element.95) | copy-start | bytes 2752516
  121.3 23.4 %copy-start.19 = (bf16[512,896]{1,0:T(8,128)(2,1)}, bf16[512,896]{1,0:T(8,128)(2,1)S(1)}, u32[]{:S(2)}) copy-start(bf16[512,896]{1,0:T(8,128)(2,1)S(1)} %get-tuple-element.83) | copy-start | bytes 2752516
  121.3 23.4 %copy-start.21 = (bf16[512,896]{1,0:T(8,128)(2,1)}, bf16[512,896]{1,0:T(8,128)(2,1)S(1)}, u32[]{:S(2)}) copy-start(bf16[512,896]{1,0:T(8,128)(2,1)S(1)} %get-tuple-element.96) | copy-start | bytes 2752516
  121.3 23.4 %copy-start.23 = (bf16[512,896]{1,0:T(8,128)(2,1)}, bf16[512,896]{1,0:T(8,128)(2,1)S(1)}, u32[]{:S(2)}) copy-start(bf16[512,896]{1,0:T(8,128)(2,1)S(1)} %get-tuple-element.82) | copy-start | bytes 2752516
  121.3 23.4 %copy-start.25 = (bf16[512,896]{1,0:T(8,128)(2,1)}, bf16[512,896]{1,0:T(8,128)(2,1)S(1)}, u32[]{:S(2)}) copy-start(bf16[512,896]{1,0:T(8,128)(2,1)S(1)} %get-tuple-element.97) | copy-start | bytes 2752516
  121.4 23.4 %copy-start.9 = (bf16[512,896]{1,0:T(8,128)(2,1)}, bf16[512,896]{1,0:T(8,128)(2,1)S(1)}, u32[]{:S(2)}) copy-start(bf16[512,896]{1,0:T(8,128)(2,1)S(1)} %get-tuple-element.81) | copy-start | bytes 2752516
  121.4 23.4 %copy-start.11 = (bf16[512,896]{1,0:T(8,128)(2,1)}, bf16[512,896]{1,0:T(8,128)(2,1)S(1)}, u32[]{:S(2)}) copy-start(bf16[512,896]{1,0:T(8,128)(2,1)S(1)} %get-tuple-element.98) | copy-start | bytes 2752516
  128.1 15.0 %copy-start.13 = (bf16[1024,256]{1,0:T(8,128)(2,1)}, bf16[1024,256]{1,0:T(8,128)(2,1)S(1)}, u32[]{:S(2)}) copy-start(bf16[1024,256]{1,0:T(8,128)(2,1)S(1)} %collective-permute-done.16.refs_1_) | copy-start | bytes 1572868
  130.4 13.5 %copy-start.14 = (bf16[1024,256]{1,0:T(8,128)(2,1)}, bf16[1024,256]{1,0:T(8,128)(2,1)S(1)}, u32[]{:S(2)}) copy-start(bf16[1024,256]{1,0:T(8,128)(2,1)S(1)} %collective-permute-done.17.refs_2_) | copy-start | bytes 1572868
  137.9 16.4 %collective-permute-start.21 = (bf16[1024,256]{1,0:T(8,128)(2,1)S(1)}, bf16[1024,256]{1,0:T(8,128)(2,1)}, u32[]{:S(2)}, u32[]{:S(2)}) collective-permute-start(bf16[1024,256]{1,0:T(8,128)(2,1)S(1)} %get-tuple-element.71.refs_0_.refs_4_), channel_id=1, source_target_pairs={{0,2},{1,3},{2,0},{3,1},{4,6},{5,7},{6,4},{7,5},{8,10},{9,11},{10,... | collective-permute-start | bytes 1572872 | tf_op jit(solution)/shard_map/ppermute | solution.py:17
  140.3 24.2 %collective-permute-start.20 = (bf16[1024,256]{1,0:T(8,128)(2,1)S(1)}, bf16[1024,256]{1,0:T(8,128)(2,1)}, u32[]{:S(2)}, u32[]{:S(2)}) collective-permute-start(bf16[1024,256]{1,0:T(8,128)(2,1)S(1)} %get-tuple-element.71.refs_0_.refs_4_), channel_id=1, source_target_pairs={{0,3},{1,0},{2,1},{3,2},{4,7},{5,4},{6,5},{7,6},{8,11},{9,8},{10,9... | collective-permute-start | bytes 1572872 | tf_op jit(solution)/shard_map/ppermute | solution.py:17
  140.6 25.8 %collective-permute-start.19 = (bf16[1024,256]{1,0:T(8,128)(2,1)S(1)}, bf16[1024,256]{1,0:T(8,128)(2,1)}, u32[]{:S(2)}, u32[]{:S(2)}) collective-permute-start(bf16[1024,256]{1,0:T(8,128)(2,1)S(1)} %get-tuple-element.71.refs_0_.refs_4_), channel_id=1, source_target_pairs={{0,1},{1,2},{2,3},{3,0},{4,5},{5,6},{6,7},{7,4},{8,9},{9,10},{10,1... | collective-permute-start | bytes 1572872 | tf_op jit(solution)/shard_map/ppermute | solution.py:17
  146.2 23.7 %all-to-all-start.3 = ((bf16[32,8,896]{2,1,0:T(8,128)(2,1)}), bf16[32,8,896]{2,1,0:T(8,128)(2,1)}, u32[]{:S(2)}, u32[]{:S(2)}) async-start(bf16[32,8,896]{2,1,0:T(8,128)(2,1)} %fusion.5), calls=%async_computation.3 | async-start | bytes 917504 | tf_op jit(solution)/shard_map/all_to_all | solution.py:320
  152.3 12.3 %copy-start.10 = (bf16[512,896]{1,0:T(8,128)(2,1)S(1)}, bf16[512,896]{1,0:T(8,128)(2,1)}, u32[]{:S(2)}) copy-start(bf16[512,896]{1,0:T(8,128)(2,1)} %copy-done.9) | copy-start | bytes 2752516
  152.3 12.3 %copy-start.12 = (bf16[512,896]{1,0:T(8,128)(2,1)S(1)}, bf16[512,896]{1,0:T(8,128)(2,1)}, u32[]{:S(2)}) copy-start(bf16[512,896]{1,0:T(8,128)(2,1)} %copy-done.11) | copy-start | bytes 2752516
  152.3 27.7 %collective-permute-start.23 = (bf16[2048,256]{1,0:T(8,128)(2,1)S(1)}, bf16[2048,256]{1,0:T(8,128)(2,1)}, u32[]{:S(2)}, u32[]{:S(2)}) collective-permute-start(bf16[2048,256]{1,0:T(8,128)(2,1)S(1)} %shard_map.60), channel_id=1, source_target_pairs={{0,4},{4,0},{1,5},{5,1},{2,6},{6,2},{3,7},{7,3},{8,12},{12,8},{9,1... | collective-permute-start | bytes 3145736 | tf_op jit(solution)/shard_map/ppermute | solution.py:21
  171.1 8.9 %collective-permute-start.24 = (bf16[2048,256]{1,0:T(8,128)(2,1)S(1)}, bf16[2048,256]{1,0:T(8,128)(2,1)}, u32[]{:S(2)}, u32[]{:S(2)}) collective-permute-start(bf16[2048,256]{1,0:T(8,128)(2,1)S(1)} %shard_map.61), channel_id=1, source_target_pairs={{0,4},{4,0},{1,5},{5,1},{2,6},{6,2},{3,7},{7,3},{8,12},{12,8},{9,1... | collective-permute-start | bytes 3145736 | tf_op jit(solution)/shard_map/ppermute | solution.py:21
  171.2 8.8 %collective-permute-start.22 = (bf16[512,896]{1,0:T(8,128)(2,1)S(1)}, bf16[512,896]{1,0:T(8,128)(2,1)}, u32[]{:S(2)}, u32[]{:S(2)}) collective-permute-start(bf16[512,896]{1,0:T(8,128)(2,1)S(1)} %get-tuple-element.66.own_states), channel_id=1, source_target_pairs={{0,4},{4,0},{1,5},{5,1},{2,6},{6,2},{3,7},{7,3},{8,12},{12,8},{9,1... | collective-permute-start | bytes 2752520 | tf_op jit(solution)/shard_map/ppermute | solution.py:21
  171.7 21.0 %all-to-all-start.4 = ((bf16[32,8,896]{2,1,0:T(8,128)(2,1)}), bf16[32,8,896]{2,1,0:T(8,128)(2,1)S(1)}, u32[]{:S(2)}, u32[]{:S(2)}) async-start(bf16[32,8,896]{2,1,0:T(8,128)(2,1)} %fusion.6), calls=%async_computation.4 | async-start | bytes 917504 | tf_op jit(solution)/shard_map/all_to_all | solution.py:324
  176.2 1.4 collective-permute-start.15
  (14 other events, 88.2 us)

commit v3 on v2

--- a/solution.py
+++ b/solution.py
@@ -103,7 +103,7 @@
     return pl.pallas_call(
         logits_kernel,
         out_shape=(
-            jax.ShapeDtypeStruct((2 * quarter, tokens), f32),
+            pltpu.HBM((2 * quarter, tokens), f32),
             jax.ShapeDtypeStruct((8, 128), f32),
             jax.ShapeDtypeStruct((1, tokens), jnp.int32),
             jax.ShapeDtypeStruct((tokens, width), bf16),
@@ -155,7 +155,7 @@
 
 def grad_of(pos, got, capped, wanted):
     entries, wide = capped.shape
-    tile = entries // 4
+    tile = entries // 2
     return pl.pallas_call(
         functools.partial(grad_kernel, entries // 2),
         grid=(entries // tile,),
@@ -167,7 +167,7 @@
             pl.BlockSpec(wanted.shape, lambda i: (0, 0)),
         ],
         out_specs=(pl.BlockSpec((8, 128), lambda i: (0, 0)),) + (pl.BlockSpec((tile, wide // 2), lambda i: (i, 0)),) * 2,
-        compiler_params=limit(12),
+        compiler_params=limit(16),
         cost_estimate=pl.CostEstimate(flops=8 * entries * wide, bytes_accessed=3 << 20, transcendentals=entries * wide),
     )(pos, got, *in_hbm(capped), wanted)
 

time: 196 us -> 194 us (0.990)
  transfers between devices with their start and end apart: 28 -> 28, of which waited for: 16 -> 16; matrix products, arithmetic and copies ran while one was open for 9% -> 10% of each run, Pallas kernels for 6% -> 6%
where the time goes in v3:
time: 194 us; the launch traced here: 193 us
  waiting for transfers between devices  75.4 us (39%)
  starting transfers between devices  46.6 us (24%)
  Pallas kernels  23.6 us (12%)
  blocking collectives  21.4 us (11%)
  matrix products  10.8 us (6%)
  local copies, waits for them, and re-layouts  7.81 us (4%)
  other arithmetic  3.86 us (2%)
  between operations  3.66 us (2%)
    ppermute x17, waiting for transfers between devices, over(): return lax.ppermute(value, axis, [(i, (i + s) % n) for i in range(n)])  58 us
    ppermute x17, starting transfers between devices, over(): return lax.ppermute(value, axis, [(i, (i + s) % n) for i in range(n)])  28.9 us
    all_to_all x1, blocking collectives, local(): lax.all_to_all(jnp.broadcast_to(sums, (8, *sums.shape)), 'z', 0, 0, tiled...  11.1 us
    dot_general x8, matrix products, back(): lax.dot_general(pieces[s], both[s], (((0,), (0,)), ((), ())), preferred_e...  10.8 us
    all_to_all x1, blocking collectives, local(): lax.all_to_all(jnp.broadcast_to(sums, (16, *sums.shape)), ('x', 'y'), 0,...  10.4 us
    all_to_all x1, waiting for transfers between devices, local(): lax.all_to_all(jnp.broadcast_to(block, (16, *block.shape)), ('x', 'y'), 0...  10.1 us
    pallas_call x1, Pallas kernels, logits_of(): pl.pallas_call(logits_kernel, out_shape=(pltpu.HBM((2 * quarter, tokens),...  9.64 us
    pallas_call x1, Pallas kernels, table_grad_of(): pl.pallas_call(table_kernel, out_shape=jax.ShapeDtypeStruct((entries, wid...  9.4 us
  transfers between devices with their start and end apart: 28, of which 16 were waited for; matrix products, arithmetic and copies ran while one was open for 10% of the time, Pallas kernels for 6%

profile of v3, /device:TPU:8, one launch (start us, length us, event | category | flops | bytes accessed | tf_op | source)
XLA Modules:
  0.0 193.1 jit_solution(1733246478212977441)
XLA Ops:
  1.4 0.8 fusion.13
  2.2 0.9 broadcast_in_dim.9
  3.0 7.4 %all-to-all-start = ((bf16[16,16,1024]{2,1,0:T(8,128)(2,1)}), bf16[16,16,1024]{2,1,0:T(8,128)(2,1)S(1)}, u32[]{:S(2)}, u32[]{:S(2)}) async-start(bf16[16,16,1024]{2,1,0:T(8,128)(2,1)} %broadcast_in_dim.9), calls=%async_computation | async-start | bytes 1048576 | tf_op jit(solution)/shard_map/all_to_all | solution.py:272
  10.4 10.1 %all-to-all-done = bf16[16,16,1024]{2,1,0:T(8,128)(2,1)S(1)} async-done(((bf16[16,16,1024]{2,1,0:T(8,128)(2,1)}), bf16[16,16,1024]{2,1,0:T(8,128)(2,1)S(1)}, u32[]{:S(2)}, u32[]{:S(2)}) %all-to-all-start) | async-done | bytes 524320 | tf_op jit(solution)/shard_map/all_to_all | solution.py:272
  20.7 5.9 %collective-permute-start = (bf16[2,32,3712]{2,1,0:T(8,128)(2,1)S(1)}, bf16[2,32,3712]{2,1,0:T(8,128)(2,1)S(1)}, u32[]{:S(2)}, u32[]{:S(2)}) collective-permute-start(bf16[2,32,3712]{2,1,0:T(8,128)(2,1)S(1)} %bitcast_dynamic-update-slice_fusion.4.refs_0_), channel_id=1, source_target_pairs={{0,224},{32,0},{64,32},{96,64},{128,96},{160,128},{192,160},{224,1... | collective-permute-start | bytes 1425416 | tf_op jit(solution)/shard_map/ppermute | solution.py:17
  26.6 2.0 %dynamic-slice_bitcast_fusion.8 = (bf16[512,896]{1,0:T(8,128)(2,1)S(1)}, bf16[512,896]{1,0:T(8,128)(2,1)S(1)}, bf16[512,896]{1,0:T(8,128)(2,1)S(1)}) fusion(bf16[4,512,896]{2,1,0:T(8,128)(2,1)} %bitcast.17.refs_9_, s32[]{:T(128)S(6)} %select_n.70, s32[]{:T(128)S(6)} %select_n.68, s32[]{:T(128)S(6)} %select_n.66), kind=kLoop, calls=%fused_computation.29 | loop fusion | bytes 5505036 | tf_op jit(solution)/shard_map/jit(dynamic_index_in_dim)/squeeze | solution.py:278
  29.2 1.5 collective-permute-start.5
  30.7 4.8 %collective-permute-done.refs_1_ = bf16[2,32,3712]{2,1,0:T(8,128)(2,1)S(1)} collective-permute-done((bf16[2,32,3712]{2,1,0:T(8,128)(2,1)S(1)}, bf16[2,32,3712]{2,1,0:T(8,128)(2,1)S(1)}, u32[]{:S(2)}, u32[]{:S(2)}) %collective-permute-start) | collective-permute-done | bytes 475168 | tf_op jit(solution)/shard_map/ppermute | solution.py:17
  35.5 3.7 %collective-permute-start.1 = (bf16[2,32,3712]{2,1,0:T(8,128)(2,1)S(1)}, bf16[2,32,3712]{2,1,0:T(8,128)(2,1)S(1)}, u32[]{:S(2)}, u32[]{:S(2)}) collective-permute-start(bf16[2,32,3712]{2,1,0:T(8,128)(2,1)S(1)} %collective-permute-done.refs_1_), channel_id=1, source_target_pairs={{0,224},{32,0},{64,32},{96,64},{128,96},{160,128},{192,160},{224,1... | collective-permute-start | bytes 1425416 | tf_op jit(solution)/shard_map/ppermute | solution.py:17
  39.3 9.9 %collective-permute-done.4.refs_10_ = bf16[512,896]{1,0:T(8,128)(2,1)S(1)} collective-permute-done((bf16[512,896]{1,0:T(8,128)(2,1)S(1)}, bf16[512,896]{1,0:T(8,128)(2,1)S(1)}, u32[]{:S(2)}, u32[]{:S(2)}) %collective-permute-start.4) | collective-permute-done | bytes 917536 | tf_op jit(solution)/shard_map/ppermute | solution.py:17
  49.5 1.1 collective-permute-done.3.refs_7_
  50.6 1.9 %collective-permute-start.6 = (bf16[2,32,3712]{2,1,0:T(8,128)(2,1)S(1)}, bf16[2,32,3712]{2,1,0:T(8,128)(2,1)S(1)}, u32[]{:S(2)}, u32[]{:S(2)}) collective-permute-start(bf16[2,32,3712]{2,1,0:T(8,128)(2,1)S(1)} %collective-permute-done.1.refs_2_), channel_id=1, source_target_pairs={{0,224},{32,0},{64,32},{96,64},{128,96},{160,128},{192,160},{224,1... | collective-permute-start | bytes 1425416 | tf_op jit(solution)/shard_map/ppermute | solution.py:17
  52.5 4.0 %collective-permute-start.7 = (bf16[512,896]{1,0:T(8,128)(2,1)S(1)}, bf16[512,896]{1,0:T(8,128)(2,1)}, u32[]{:S(2)}, u32[]{:S(2)}) collective-permute-start(bf16[512,896]{1,0:T(8,128)(2,1)S(1)} %get-tuple-element.43), channel_id=1, source_target_pairs={{0,2},{1,3},{2,0},{3,1},{4,6},{5,7},{6,4},{7,5},{8,10},{9,11},{10,... | collective-permute-start | bytes 2752520 | tf_op jit(solution)/shard_map/ppermute | solution.py:17
  56.6 4.6 %collective-permute-done.6.refs_3_ = bf16[2,32,3712]{2,1,0:T(8,128)(2,1)S(1)} collective-permute-done((bf16[2,32,3712]{2,1,0:T(8,128)(2,1)S(1)}, bf16[2,32,3712]{2,1,0:T(8,128)(2,1)S(1)}, u32[]{:S(2)}, u32[]{:S(2)}) %collective-permute-start.6) | collective-permute-done | bytes 475168 | tf_op jit(solution)/shard_map/ppermute | solution.py:17
  61.2 2.4 %collective-permute-start.8 = (bf16[32,3712]{1,0:T(8,128)(2,1)S(1)}, bf16[32,3712]{1,0:T(8,128)(2,1)S(1)}, u32[]{:S(2)}, u32[]{:S(2)}) collective-permute-start(bf16[32,3712]{1,0:T(8,128)(2,1)S(1)} %slice_bitcast_fusion.1), channel_id=1, source_target_pairs={{0,224},{32,0},{64,32},{96,64},{128,96},{160,128},{192,160},{224,1... | collective-permute-start | bytes 712712 | tf_op jit(solution)/shard_map/ppermute | solution.py:17
  63.6 3.9 %collective-permute-done.9.refs_6_ = bf16[2,32,3712]{2,1,0:T(8,128)(2,1)S(1)} collective-permute-done((bf16[2,32,3712]{2,1,0:T(8,128)(2,1)S(1)}, bf16[2,32,3712]{2,1,0:T(8,128)(2,1)S(1)}, u32[]{:S(2)}, u32[]{:S(2)}) %collective-permute-start.9) | collective-permute-done | bytes 475168 | tf_op jit(solution)/shard_map/ppermute | solution.py:17
  68.2 6.7 %collective-permute-done.10.refs_5_ = bf16[32,3712]{1,0:T(8,128)(2,1)S(1)} collective-permute-done((bf16[32,3712]{1,0:T(8,128)(2,1)S(1)}, bf16[32,3712]{1,0:T(8,128)(2,1)S(1)}, u32[]{:S(2)}, u32[]{:S(2)}) %collective-permute-start.10) | collective-permute-done | bytes 237600 | tf_op jit(solution)/shard_map/ppermute | solution.py:17
  75.7 2.7 %collective-permute-done.13.refs_15_ = bf16[512,896]{1,0:T(8,128)(2,1)} collective-permute-done((bf16[512,896]{1,0:T(8,128)(2,1)}, bf16[512,896]{1,0:T(8,128)(2,1)}, u32[]{:S(2)}, u32[]{:S(2)}) %collective-permute-start.13) | collective-permute-done | bytes 917536 | tf_op jit(solution)/shard_map/ppermute | solution.py:21
  78.5 9.6 %shard_map.58 = (f32[1024,512]{1,0:T(8,128)}, f32[8,128]{1,0:T(8,128)S(1)}, s32[1,512]{1,0:T(1,128)S(1)}, bf16[512,896]{1,0:T(8,128)(2,1)S(1)}) custom-call(s32[6]{0:T(128)S(1)} %stack.43.pos, bf16[2,32,3712]{2,1,0:T(8,128)(2,1)} %copy-done.26, bf16[2,32,3712]{2,1,0:T(8,128)(2,1)} %copy-done.27, bf16[2,32,3712]{2,1,0:T(8,128)(2,1)} %copy-done.29, ...), custom_call_target="tpu_custom_call" | custom-call | flops 3758096384 | bytes 13631488 | tf_op jit(solution)/shard_map/pallas_call | solution.py:103
  88.1 10.4 %all_to_all.25 = f32[16,8,128]{2,1,0:T(8,128)S(1)} all-to-all(f32[16,8,128]{2,1,0:T(8,128)S(1)} %broadcast_in_dim.10), channel_id=1, replica_groups=mesh['z'=8,'x'=4,'c'=2,'y'=4] {'x','y'}, dimensions={0} | all-to-all | bytes 131072 | tf_op jit(solution)/shard_map/all_to_all | solution.py:301
  98.6 11.1 %all_to_all.26.got = f32[8,8,128]{2,1,0:T(8,128)S(1)} all-to-all(f32[8,8,128]{2,1,0:T(8,128)S(1)} %broadcast_in_dim.11), channel_id=1, replica_groups=mesh['z'=8,'x'=4,'c'=2,'y'=4] {'z'}, dimensions={0} | all-to-all | bytes 65536 | tf_op jit(solution)/shard_map/all_to_all | solution.py:303
  109.6 2.1 %shard_map.59 = (f32[8,128]{1,0:T(8,128)S(1)}, bf16[1024,256]{1,0:T(8,128)(2,1)S(1)}, bf16[1024,256]{1,0:T(8,128)(2,1)S(1)}) custom-call(s32[6]{0:T(128)S(1)} %stack.43.pos, f32[8,8,128]{2,1,0:T(8,128)S(1)} %all_to_all.26.got, f32[1024,512]{1,0:T(8,128)} %get-tuple-element.51.capped_ref, s32[1,512]{1,0:T(1,128)S(1)} %get-tuple-element.52.wanted_ref), custom_call_target="tpu_custom_call" | custom-call | flops 4194304 | bytes 3145728 | tf_op jit(solution)/shard_map/pallas_call | solution.py:159
  111.7 0.9 collective-permute-start.16
  112.6 2.7 %collective-permute-start.17 = (bf16[1024,256]{1,0:T(8,128)(2,1)S(1)}, bf16[1024,256]{1,0:T(8,128)(2,1)S(1)}, u32[]{:S(2)}, u32[]{:S(2)}) collective-permute-start(bf16[1024,256]{1,0:T(8,128)(2,1)S(1)} %get-tuple-element.67.refs_0_), channel_id=1, source_target_pairs={{0,2},{1,3},{2,0},{3,1},{4,6},{5,7},{6,4},{7,5},{8,10},{9,11},{10,... | collective-permute-start | bytes 1572872 | tf_op jit(solution)/shard_map/ppermute | solution.py:17
  116.0 3.8 %dynamic-slice_bitcast_fusion.2 = (bf16[512,896]{1,0:T(8,128)(2,1)S(1)}, bf16[512,896]{1,0:T(8,128)(2,1)S(1)}, bf16[512,896]{1,0:T(8,128)(2,1)S(1)}, bf16[512,89...) fusion(bf16[4,512,896]{2,1,0:T(8,128)(2,1)} %bitcast.23.refs_13, ...), kind=kLoop, calls=%fused_computation.23 | loop fusion | bytes 14680080 | tf_op jit(solution)/shard_map/jit(dynamic_index_in_dim)/squeeze | solution.py:278
  119.9 6.7 %collective-permute-done.16.refs_1_ = bf16[1024,256]{1,0:T(8,128)(2,1)S(1)} collective-permute-done((bf16[1024,256]{1,0:T(8,128)(2,1)S(1)}, bf16[1024,256]{1,0:T(8,128)(2,1)S(1)}, u32[]{:S(2)}, u32[]{:S(2)}) %collective-permute-start.16) | collective-permute-done | bytes 524320 | tf_op jit(solution)/shard_map/ppermute | solution.py:17
  126.7 2.3 %collective-permute-done.17.refs_2_ = bf16[1024,256]{1,0:T(8,128)(2,1)S(1)} collective-permute-done((bf16[1024,256]{1,0:T(8,128)(2,1)S(1)}, bf16[1024,256]{1,0:T(8,128)(2,1)S(1)}, u32[]{:S(2)}, u32[]{:S(2)}) %collective-permute-start.17) | collective-permute-done | bytes 524320 | tf_op jit(solution)/shard_map/ppermute | solution.py:17
  129.0 7.5 %collective-permute-done.18.refs_3_ = bf16[1024,256]{1,0:T(8,128)(2,1)S(1)} collective-permute-done((bf16[1024,256]{1,0:T(8,128)(2,1)S(1)}, bf16[1024,256]{1,0:T(8,128)(2,1)S(1)}, u32[]{:S(2)}, u32[]{:S(2)}) %collective-permute-start.18) | collective-permute-done | bytes 524320 | tf_op jit(solution)/shard_map/ppermute | solution.py:17
  136.4 2.5 %collective-permute-start.21 = (bf16[1024,256]{1,0:T(8,128)(2,1)S(1)}, bf16[1024,256]{1,0:T(8,128)(2,1)}, u32[]{:S(2)}, u32[]{:S(2)}) collective-permute-start(bf16[1024,256]{1,0:T(8,128)(2,1)S(1)} %get-tuple-element.71.refs_0_.refs_4_), channel_id=1, source_target_pairs={{0,2},{1,3},{2,0},{3,1},{4,6},{5,7},{6,4},{7,5},{8,10},{9,11},{10,... | collective-permute-start | bytes 1572872 | tf_op jit(solution)/shard_map/ppermute | solution.py:17
  139.1 1.8 collective-permute-start.19
  140.9 0.7 fusion.10
  141.7 0.7 convolution_add_fusion.1
  142.5 0.7 fusion.8
  143.3 1.5 fusion.5
  144.8 4.7 %all-to-all-start.3 = ((bf16[32,8,896]{2,1,0:T(8,128)(2,1)}), bf16[32,8,896]{2,1,0:T(8,128)(2,1)}, u32[]{:S(2)}, u32[]{:S(2)}) async-start(bf16[32,8,896]{2,1,0:T(8,128)(2,1)} %fusion.5), calls=%async_computation.3 | async-start | bytes 917504 | tf_op jit(solution)/shard_map/all_to_all | solution.py:320
  149.5 1.3 shard_map.60
  151.2 1.7 collective-permute-done.21.refs_2_.refs_6_
  152.9 1.8 fusion.7
  154.7 8.4 %collective-permute-done.20.refs_3_.refs_7_ = bf16[1024,256]{1,0:T(8,128)(2,1)} collective-permute-done((bf16[1024,256]{1,0:T(8,128)(2,1)S(1)}, bf16[1024,256]{1,0:T(8,128)(2,1)}, u32[]{:S(2)}, u32[]{:S(2)}) %collective-permute-start.20) | collective-permute-done | bytes 524320 | tf_op jit(solution)/shard_map/ppermute | solution.py:17
  163.1 1.8 fusion.9
  165.0 1.9 fusion.11
  166.9 1.6 fusion.6
  168.5 1.2 shard_map.61
  170.3 3.9 %all-to-all-start.4 = ((bf16[32,8,896]{2,1,0:T(8,128)(2,1)}), bf16[32,8,896]{2,1,0:T(8,128)(2,1)S(1)}, u32[]{:S(2)}, u32[]{:S(2)}) async-start(bf16[32,8,896]{2,1,0:T(8,128)(2,1)} %fusion.6), calls=%async_computation.4 | async-start | bytes 917504 | tf_op jit(solution)/shard_map/all_to_all | solution.py:324
  174.9 1.3 collective-permute-done.15
  177.5 1.1 convert_reduce_fusion.1
  178.6 9.4 %shard_map.62 = f32[2048,896]{1,0:T(8,128)} custom-call(s32[6]{0:T(128)S(1)} %stack.43.pos, bf16[512,896]{1,0:T(8,128)(2,1)} %copy-done.2, bf16[512,896]{1,0:T(8,128)(2,1)} %collective-permute-done.22.beside_states, bf16[1024,256]{1,0:T(8,128)(2,1)} %copy-done.1, bf16[1024,256]{1,0:T(8,128)(2,1)} %copy-done.12, bf16[1024,256]{1,0:T(8,128)(2,1)} %copy-done.13, ...), custom_call_target="tpu_custom_call" | custom-call | flops 1048576 | bytes 262144 | tf_op jit(solution)/shard_map/pallas_call | solution.py:243
  188.0 3.3 %all-to-all-done.4 = bf16[32,8,896]{2,1,0:T(8,128)(2,1)S(1)} async-done(((bf16[32,8,896]{2,1,0:T(8,128)(2,1)}), bf16[32,8,896]{2,1,0:T(8,128)(2,1)S(1)}, u32[]{:S(2)}, u32[]{:S(2)}) %all-to-all-start.4) | async-done | bytes 458784 | tf_op jit(solution)/shard_map/all_to_all | solution.py:324
  (112 shorter events, 6.6 us)
Async XLA Ops:
  3.0 17.5 %all-to-all-start = ((bf16[16,16,1024]{2,1,0:T(8,128)(2,1)}), bf16[16,16,1024]{2,1,0:T(8,128)(2,1)S(1)}, u32[]{:S(2)}, u32[]{:S(2)}) async-start(bf16[16,16,1024]{2,1,0:T(8,128)(2,1)} %broadcast_in_dim.9), calls=%async_computation | async-start | bytes 1048576 | tf_op jit(solution)/shard_map/all_to_all | solution.py:272
  20.7 14.8 %collective-permute-start = (bf16[2,32,3712]{2,1,0:T(8,128)(2,1)S(1)}, bf16[2,32,3712]{2,1,0:T(8,128)(2,1)S(1)}, u32[]{:S(2)}, u32[]{:S(2)}) collective-permute-start(bf16[2,32,3712]{2,1,0:T(8,128)(2,1)S(1)} %bitcast_dynamic-update-slice_fusion.4.refs_0_), channel_id=1, source_target_pairs={{0,224},{32,0},{64,32},{96,64},{128,96},{160,128},{192,160},{224,1... | collective-permute-start | bytes 1425416 | tf_op jit(solution)/shard_map/ppermute | solution.py:17
  26.6 12.6 %collective-permute-start.2 = (bf16[2,32,3712]{2,1,0:T(8,128)(2,1)S(1)}, bf16[2,32,3712]{2,1,0:T(8,128)(2,1)S(1)}, u32[]{:S(2)}, u32[]{:S(2)}) collective-permute-start(bf16[2,32,3712]{2,1,0:T(8,128)(2,1)S(1)} %bitcast_dynamic-update-slice_fusion.4.refs_0_), channel_id=1, source_target_pairs={{0,32},{32,64},{64,96},{96,128},{128,160},{160,192},{192,224},{224... | collective-permute-start | bytes 1425416 | tf_op jit(solution)/shard_map/ppermute | solution.py:17
  28.6 20.7 %collective-permute-start.4 = (bf16[512,896]{1,0:T(8,128)(2,1)S(1)}, bf16[512,896]{1,0:T(8,128)(2,1)S(1)}, u32[]{:S(2)}, u32[]{:S(2)}) collective-permute-start(bf16[512,896]{1,0:T(8,128)(2,1)S(1)} %get-tuple-element.87), channel_id=1, source_target_pairs={{0,1},{1,2},{2,3},{3,0},{4,5},{5,6},{6,7},{7,4},{8,9},{9,10},{10,1... | collective-permute-start | bytes 2752520 | tf_op jit(solution)/shard_map/ppermute | solution.py:17
  29.2 20.3 %collective-permute-start.5 = (bf16[512,896]{1,0:T(8,128)(2,1)S(1)}, bf16[512,896]{1,0:T(8,128)(2,1)S(1)}, u32[]{:S(2)}, u32[]{:S(2)}) collective-permute-start(bf16[512,896]{1,0:T(8,128)(2,1)S(1)} %get-tuple-element.86), channel_id=1, source_target_pairs={{0,3},{1,0},{2,1},{3,2},{4,7},{5,4},{6,5},{7,6},{8,11},{9,8},{10,9... | collective-permute-start | bytes 2752520 | tf_op jit(solution)/shard_map/ppermute | solution.py:17
  35.5 13.9 %copy-start.27 = (bf16[2,32,3712]{2,1,0:T(8,128)(2,1)}, bf16[2,32,3712]{2,1,0:T(8,128)(2,1)S(1)}, u32[]{:S(2)}) copy-start(bf16[2,32,3712]{2,1,0:T(8,128)(2,1)S(1)} %collective-permute-done.refs_1_) | copy-start | bytes 1425412
  35.5 13.9 %collective-permute-start.1 = (bf16[2,32,3712]{2,1,0:T(8,128)(2,1)S(1)}, bf16[2,32,3712]{2,1,0:T(8,128)(2,1)S(1)}, u32[]{:S(2)}, u32[]{:S(2)}) collective-permute-start(bf16[2,32,3712]{2,1,0:T(8,128)(2,1)S(1)} %collective-permute-done.refs_1_), channel_id=1, source_target_pairs={{0,224},{32,0},{64,32},{96,64},{128,96},{160,128},{192,160},{224,1... | collective-permute-start | bytes 1425416 | tf_op jit(solution)/shard_map/ppermute | solution.py:17
  39.2 11.4 %collective-permute-start.3 = (bf16[2,32,3712]{2,1,0:T(8,128)(2,1)S(1)}, bf16[2,32,3712]{2,1,0:T(8,128)(2,1)S(1)}, u32[]{:S(2)}, u32[]{:S(2)}) collective-permute-start(bf16[2,32,3712]{2,1,0:T(8,128)(2,1)S(1)} %collective-permute-done.2.refs_8_), channel_id=1, source_target_pairs={{0,32},{32,64},{64,96},{96,128},{128,160},{160,192},{192,224},{224... | collective-permute-start | bytes 1425416 | tf_op jit(solution)/shard_map/ppermute | solution.py:17
  39.2 39.2 %collective-permute-start.11 = (bf16[2048,896]{1,0:T(8,128)(2,1)}, bf16[2048,896]{1,0:T(8,128)(2,1)}, u32[]{:S(2)}, u32[]{:S(2)}) collective-permute-start(bf16[2048,896]{1,0:T(8,128)(2,1)} %param.4), channel_id=1, source_target_pairs={{0,4},{4,0},{1,5},{5,1},{2,6},{6,2},{3,7},{7,3},{8,12},{12,8},{9,1... | collective-permute-start | bytes 11010056 | tf_op jit(solution)/shard_map/ppermute | solution.py:21
  49.2 29.2 %copy-start.16 = (bf16[512,896]{1,0:T(8,128)(2,1)}, bf16[512,896]{1,0:T(8,128)(2,1)S(1)}, u32[]{:S(2)}) copy-start(bf16[512,896]{1,0:T(8,128)(2,1)S(1)} %collective-permute-done.4.refs_10_) | copy-start | bytes 2752516
  49.5 29.0 %copy-start.17 = (bf16[512,896]{1,0:T(8,128)(2,1)}, bf16[512,896]{1,0:T(8,128)(2,1)S(1)}, u32[]{:S(2)}) copy-start(bf16[512,896]{1,0:T(8,128)(2,1)S(1)} %collective-permute-done.5.refs_12_) | copy-start | bytes 2752516
  50.6 27.8 %copy-start.30 = (bf16[2,32,3712]{2,1,0:T(8,128)(2,1)}, bf16[2,32,3712]{2,1,0:T(8,128)(2,1)S(1)}, u32[]{:S(2)}) copy-start(bf16[2,32,3712]{2,1,0:T(8,128)(2,1)S(1)} %collective-permute-done.3.refs_7_) | copy-start | bytes 1425412
  50.6 10.6 %collective-permute-start.6 = (bf16[2,32,3712]{2,1,0:T(8,128)(2,1)S(1)}, bf16[2,32,3712]{2,1,0:T(8,128)(2,1)S(1)}, u32[]{:S(2)}, u32[]{:S(2)}) collective-permute-start(bf16[2,32,3712]{2,1,0:T(8,128)(2,1)S(1)} %collective-permute-done.1.refs_2_), channel_id=1, source_target_pairs={{0,224},{32,0},{64,32},{96,64},{128,96},{160,128},{192,160},{224,1... | collective-permute-start | bytes 1425416 | tf_op jit(solution)/shard_map/ppermute | solution.py:17
  52.5 22.4 %collective-permute-start.7 = (bf16[512,896]{1,0:T(8,128)(2,1)S(1)}, bf16[512,896]{1,0:T(8,128)(2,1)}, u32[]{:S(2)}, u32[]{:S(2)}) collective-permute-start(bf16[512,896]{1,0:T(8,128)(2,1)S(1)} %get-tuple-element.43), channel_id=1, source_target_pairs={{0,2},{1,3},{2,0},{3,1},{4,6},{5,7},{6,4},{7,5},{8,10},{9,11},{10,... | collective-permute-start | bytes 2752520 | tf_op jit(solution)/shard_map/ppermute | solution.py:17
  56.6 10.9 %collective-permute-start.9 = (bf16[2,32,3712]{2,1,0:T(8,128)(2,1)S(1)}, bf16[2,32,3712]{2,1,0:T(8,128)(2,1)S(1)}, u32[]{:S(2)}, u32[]{:S(2)}) collective-permute-start(bf16[2,32,3712]{2,1,0:T(8,128)(2,1)S(1)} %collective-permute-done.3.refs_7_), channel_id=1, source_target_pairs={{0,32},{32,64},{64,96},{96,128},{128,160},{160,192},{192,224},{224... | collective-permute-start | bytes 1425416 | tf_op jit(solution)/shard_map/ppermute | solution.py:17
  61.2 17.3 %copy-start.14 = (bf16[2,32,3712]{2,1,0:T(8,128)(2,1)}, bf16[2,32,3712]{2,1,0:T(8,128)(2,1)S(1)}, u32[]{:S(2)}) copy-start(bf16[2,32,3712]{2,1,0:T(8,128)(2,1)S(1)} %collective-permute-done.6.refs_3_) | copy-start | bytes 1425412
  61.2 6.5 %collective-permute-start.8 = (bf16[32,3712]{1,0:T(8,128)(2,1)S(1)}, bf16[32,3712]{1,0:T(8,128)(2,1)S(1)}, u32[]{:S(2)}, u32[]{:S(2)}) collective-permute-start(bf16[32,3712]{1,0:T(8,128)(2,1)S(1)} %slice_bitcast_fusion.1), channel_id=1, source_target_pairs={{0,224},{32,0},{64,32},{96,64},{128,96},{160,128},{192,160},{224,1... | collective-permute-start | bytes 712712 | tf_op jit(solution)/shard_map/ppermute | solution.py:17
  67.5 7.4 %collective-permute-start.10 = (bf16[32,3712]{1,0:T(8,128)(2,1)S(1)}, bf16[32,3712]{1,0:T(8,128)(2,1)S(1)}, u32[]{:S(2)}, u32[]{:S(2)}) collective-permute-start(bf16[32,3712]{1,0:T(8,128)(2,1)S(1)} %slice_bitcast_fusion), channel_id=1, source_target_pairs={{0,32},{32,64},{64,96},{96,128},{128,160},{160,192},{192,224},{224... | collective-permute-start | bytes 712712 | tf_op jit(solution)/shard_map/ppermute | solution.py:17
  67.6 8.1 %collective-permute-start.12 = (bf16[512,896]{1,0:T(8,128)(2,1)S(1)}, bf16[512,896]{1,0:T(8,128)(2,1)}, u32[]{:S(2)}, u32[]{:S(2)}) collective-permute-start(bf16[512,896]{1,0:T(8,128)(2,1)S(1)} %collective-permute-done.4.refs_10_), channel_id=1, source_target_pairs={{0,4},{4,0},{1,5},{5,1},{2,6},{6,2},{3,7},{7,3},{8,12},{12,8},{9,1... | collective-permute-start | bytes 2752520 | tf_op jit(solution)/shard_map/ppermute | solution.py:21
  67.7 8.0 %collective-permute-start.14 = (bf16[512,896]{1,0:T(8,128)(2,1)S(1)}, bf16[512,896]{1,0:T(8,128)(2,1)}, u32[]{:S(2)}, u32[]{:S(2)}) collective-permute-start(bf16[512,896]{1,0:T(8,128)(2,1)S(1)} %collective-permute-done.5.refs_12_), channel_id=1, source_target_pairs={{0,4},{4,0},{1,5},{5,1},{2,6},{6,2},{3,7},{7,3},{8,12},{12,8},{9,1... | collective-permute-start | bytes 2752520 | tf_op jit(solution)/shard_map/ppermute | solution.py:21
  75.6 2.8 %collective-permute-start.13 = (bf16[512,896]{1,0:T(8,128)(2,1)}, bf16[512,896]{1,0:T(8,128)(2,1)}, u32[]{:S(2)}, u32[]{:S(2)}) collective-permute-start(bf16[512,896]{1,0:T(8,128)(2,1)} %collective-permute-done.7.refs_11_), channel_id=1, source_target_pairs={{0,4},{4,0},{1,5},{5,1},{2,6},{6,2},{3,7},{7,3},{8,12},{12,8},{9,1... | collective-permute-start | bytes 2752520 | tf_op jit(solution)/shard_map/ppermute | solution.py:21
  88.1 81.7 %copy-start.2 = (bf16[512,896]{1,0:T(8,128)(2,1)}, bf16[512,896]{1,0:T(8,128)(2,1)S(1)}, u32[]{:S(2)}) copy-start(bf16[512,896]{1,0:T(8,128)(2,1)S(1)} %get-tuple-element.66.own_states) | copy-start | bytes 2752516
  111.7 30.0 %copy-start.1 = (bf16[1024,256]{1,0:T(8,128)(2,1)}, bf16[1024,256]{1,0:T(8,128)(2,1)S(1)}, u32[]{:S(2)}) copy-start(bf16[1024,256]{1,0:T(8,128)(2,1)S(1)} %get-tuple-element.67.refs_0_) | copy-start | bytes 1572868
  111.7 55.2 %copy-start = (bf16[1024,256]{1,0:T(8,128)(2,1)}, bf16[1024,256]{1,0:T(8,128)(2,1)S(1)}, u32[]{:S(2)}) copy-start(bf16[1024,256]{1,0:T(8,128)(2,1)S(1)} %get-tuple-element.71.refs_0_.refs_4_) | copy-start | bytes 1572868
  111.7 14.9 %collective-permute-start.16 = (bf16[1024,256]{1,0:T(8,128)(2,1)S(1)}, bf16[1024,256]{1,0:T(8,128)(2,1)S(1)}, u32[]{:S(2)}, u32[]{:S(2)}) collective-permute-start(bf16[1024,256]{1,0:T(8,128)(2,1)S(1)} %get-tuple-element.67.refs_0_), channel_id=1, source_target_pairs={{0,1},{1,2},{2,3},{3,0},{4,5},{5,6},{6,7},{7,4},{8,9},{9,10},{10,1... | collective-permute-start | bytes 1572872 | tf_op jit(solution)/shard_map/ppermute | solution.py:17
  112.6 16.4 %collective-permute-start.17 = (bf16[1024,256]{1,0:T(8,128)(2,1)S(1)}, bf16[1024,256]{1,0:T(8,128)(2,1)S(1)}, u32[]{:S(2)}, u32[]{:S(2)}) collective-permute-start(bf16[1024,256]{1,0:T(8,128)(2,1)S(1)} %get-tuple-element.67.refs_0_), channel_id=1, source_target_pairs={{0,2},{1,3},{2,0},{3,1},{4,6},{5,7},{6,4},{7,5},{8,10},{9,11},{10,... | collective-permute-start | bytes 1572872 | tf_op jit(solution)/shard_map/ppermute | solution.py:17
  115.3 21.1 %collective-permute-start.18 = (bf16[1024,256]{1,0:T(8,128)(2,1)S(1)}, bf16[1024,256]{1,0:T(8,128)(2,1)S(1)}, u32[]{:S(2)}, u32[]{:S(2)}) collective-permute-start(bf16[1024,256]{1,0:T(8,128)(2,1)S(1)} %get-tuple-element.67.refs_0_), channel_id=1, source_target_pairs={{0,3},{1,0},{2,1},{3,2},{4,7},{5,4},{6,5},{7,6},{8,11},{9,8},{10,9... | collective-permute-start | bytes 1572872 | tf_op jit(solution)/shard_map/ppermute | solution.py:17
  119.8 21.9 %copy-start.4 = (bf16[512,896]{1,0:T(8,128)(2,1)}, bf16[512,896]{1,0:T(8,128)(2,1)S(1)}, u32[]{:S(2)}) copy-start(bf16[512,896]{1,0:T(8,128)(2,1)S(1)} %get-tuple-element.84) | copy-start | bytes 2752516
  119.9 21.9 %copy-start.6 = (bf16[512,896]{1,0:T(8,128)(2,1)}, bf16[512,896]{1,0:T(8,128)(2,1)S(1)}, u32[]{:S(2)}) copy-start(bf16[512,896]{1,0:T(8,128)(2,1)S(1)} %get-tuple-element.95) | copy-start | bytes 2752516
  119.9 23.4 %copy-start.18 = (bf16[512,896]{1,0:T(8,128)(2,1)}, bf16[512,896]{1,0:T(8,128)(2,1)S(1)}, u32[]{:S(2)}) copy-start(bf16[512,896]{1,0:T(8,128)(2,1)S(1)} %get-tuple-element.83) | copy-start | bytes 2752516
  119.9 23.4 %copy-start.20 = (bf16[512,896]{1,0:T(8,128)(2,1)}, bf16[512,896]{1,0:T(8,128)(2,1)S(1)}, u32[]{:S(2)}) copy-start(bf16[512,896]{1,0:T(8,128)(2,1)S(1)} %get-tuple-element.96) | copy-start | bytes 2752516
  119.9 23.4 %copy-start.22 = (bf16[512,896]{1,0:T(8,128)(2,1)}, bf16[512,896]{1,0:T(8,128)(2,1)S(1)}, u32[]{:S(2)}) copy-start(bf16[512,896]{1,0:T(8,128)(2,1)S(1)} %get-tuple-element.82) | copy-start | bytes 2752516
  119.9 23.4 %copy-start.24 = (bf16[512,896]{1,0:T(8,128)(2,1)}, bf16[512,896]{1,0:T(8,128)(2,1)S(1)}, u32[]{:S(2)}) copy-start(bf16[512,896]{1,0:T(8,128)(2,1)S(1)} %get-tuple-element.97) | copy-start | bytes 2752516
  119.9 23.4 %copy-start.8 = (bf16[512,896]{1,0:T(8,128)(2,1)}, bf16[512,896]{1,0:T(8,128)(2,1)S(1)}, u32[]{:S(2)}) copy-start(bf16[512,896]{1,0:T(8,128)(2,1)S(1)} %get-tuple-element.81) | copy-start | bytes 2752516
  119.9 23.4 %copy-start.10 = (bf16[512,896]{1,0:T(8,128)(2,1)}, bf16[512,896]{1,0:T(8,128)(2,1)S(1)}, u32[]{:S(2)}) copy-start(bf16[512,896]{1,0:T(8,128)(2,1)S(1)} %get-tuple-element.98) | copy-start | bytes 2752516
  126.7 15.0 %copy-start.12 = (bf16[1024,256]{1,0:T(8,128)(2,1)}, bf16[1024,256]{1,0:T(8,128)(2,1)S(1)}, u32[]{:S(2)}) copy-start(bf16[1024,256]{1,0:T(8,128)(2,1)S(1)} %collective-permute-done.16.refs_1_) | copy-start | bytes 1572868
  129.0 13.5 %copy-start.13 = (bf16[1024,256]{1,0:T(8,128)(2,1)}, bf16[1024,256]{1,0:T(8,128)(2,1)S(1)}, u32[]{:S(2)}) copy-start(bf16[1024,256]{1,0:T(8,128)(2,1)S(1)} %collective-permute-done.17.refs_2_) | copy-start | bytes 1572868
  136.4 16.4 %collective-permute-start.21 = (bf16[1024,256]{1,0:T(8,128)(2,1)S(1)}, bf16[1024,256]{1,0:T(8,128)(2,1)}, u32[]{:S(2)}, u32[]{:S(2)}) collective-permute-start(bf16[1024,256]{1,0:T(8,128)(2,1)S(1)} %get-tuple-element.71.refs_0_.refs_4_), channel_id=1, source_target_pairs={{0,2},{1,3},{2,0},{3,1},{4,6},{5,7},{6,4},{7,5},{8,10},{9,11},{10,... | collective-permute-start | bytes 1572872 | tf_op jit(solution)/shard_map/ppermute | solution.py:17
  138.9 24.2 %collective-permute-start.20 = (bf16[1024,256]{1,0:T(8,128)(2,1)S(1)}, bf16[1024,256]{1,0:T(8,128)(2,1)}, u32[]{:S(2)}, u32[]{:S(2)}) collective-permute-start(bf16[1024,256]{1,0:T(8,128)(2,1)S(1)} %get-tuple-element.71.refs_0_.refs_4_), channel_id=1, source_target_pairs={{0,3},{1,0},{2,1},{3,2},{4,7},{5,4},{6,5},{7,6},{8,11},{9,8},{10,9... | collective-permute-start | bytes 1572872 | tf_op jit(solution)/shard_map/ppermute | solution.py:17
  139.1 25.8 %collective-permute-start.19 = (bf16[1024,256]{1,0:T(8,128)(2,1)S(1)}, bf16[1024,256]{1,0:T(8,128)(2,1)}, u32[]{:S(2)}, u32[]{:S(2)}) collective-permute-start(bf16[1024,256]{1,0:T(8,128)(2,1)S(1)} %get-tuple-element.71.refs_0_.refs_4_), channel_id=1, source_target_pairs={{0,1},{1,2},{2,3},{3,0},{4,5},{5,6},{6,7},{7,4},{8,9},{9,10},{10,1... | collective-permute-start | bytes 1572872 | tf_op jit(solution)/shard_map/ppermute | solution.py:17
  144.8 23.7 %all-to-all-start.3 = ((bf16[32,8,896]{2,1,0:T(8,128)(2,1)}), bf16[32,8,896]{2,1,0:T(8,128)(2,1)}, u32[]{:S(2)}, u32[]{:S(2)}) async-start(bf16[32,8,896]{2,1,0:T(8,128)(2,1)} %fusion.5), calls=%async_computation.3 | async-start | bytes 917504 | tf_op jit(solution)/shard_map/all_to_all | solution.py:320
  150.9 12.3 %copy-start.9 = (bf16[512,896]{1,0:T(8,128)(2,1)S(1)}, bf16[512,896]{1,0:T(8,128)(2,1)}, u32[]{:S(2)}) copy-start(bf16[512,896]{1,0:T(8,128)(2,1)} %copy-done.8) | copy-start | bytes 2752516
  150.9 12.3 %copy-start.11 = (bf16[512,896]{1,0:T(8,128)(2,1)S(1)}, bf16[512,896]{1,0:T(8,128)(2,1)}, u32[]{:S(2)}) copy-start(bf16[512,896]{1,0:T(8,128)(2,1)} %copy-done.10) | copy-start | bytes 2752516
  150.9 27.7 %collective-permute-start.23 = (bf16[2048,256]{1,0:T(8,128)(2,1)S(1)}, bf16[2048,256]{1,0:T(8,128)(2,1)}, u32[]{:S(2)}, u32[]{:S(2)}) collective-permute-start(bf16[2048,256]{1,0:T(8,128)(2,1)S(1)} %shard_map.60), channel_id=1, source_target_pairs={{0,4},{4,0},{1,5},{5,1},{2,6},{6,2},{3,7},{7,3},{8,12},{12,8},{9,1... | collective-permute-start | bytes 3145736 | tf_op jit(solution)/shard_map/ppermute | solution.py:21
  169.7 8.9 %collective-permute-start.24 = (bf16[2048,256]{1,0:T(8,128)(2,1)S(1)}, bf16[2048,256]{1,0:T(8,128)(2,1)}, u32[]{:S(2)}, u32[]{:S(2)}) collective-permute-start(bf16[2048,256]{1,0:T(8,128)(2,1)S(1)} %shard_map.61), channel_id=1, source_target_pairs={{0,4},{4,0},{1,5},{5,1},{2,6},{6,2},{3,7},{7,3},{8,12},{12,8},{9,1... | collective-permute-start | bytes 3145736 | tf_op jit(solution)/shard_map/ppermute | solution.py:21
  169.8 8.8 %collective-permute-start.22 = (bf16[512,896]{1,0:T(8,128)(2,1)S(1)}, bf16[512,896]{1,0:T(8,128)(2,1)}, u32[]{:S(2)}, u32[]{:S(2)}) collective-permute-start(bf16[512,896]{1,0:T(8,128)(2,1)S(1)} %get-tuple-element.66.own_states), channel_id=1, source_target_pairs={{0,4},{4,0},{1,5},{5,1},{2,6},{6,2},{3,7},{7,3},{8,12},{12,8},{9,1... | collective-permute-start | bytes 2752520 | tf_op jit(solution)/shard_map/ppermute | solution.py:21
  170.3 21.0 %all-to-all-start.4 = ((bf16[32,8,896]{2,1,0:T(8,128)(2,1)}), bf16[32,8,896]{2,1,0:T(8,128)(2,1)S(1)}, u32[]{:S(2)}, u32[]{:S(2)}) async-start(bf16[32,8,896]{2,1,0:T(8,128)(2,1)} %fusion.6), calls=%async_computation.4 | async-start | bytes 917504 | tf_op jit(solution)/shard_map/all_to_all | solution.py:324
  174.8 1.4 collective-permute-start.15
  (13 other events, 86.9 us)

commit v4 on v3

--- a/solution.py
+++ b/solution.py
@@ -316,9 +316,11 @@
 
     late, beside_late, moved[0][0] = tie(quarters, beside, moved[0][0])
     both = [jnp.concatenate([quarter_at(late, -s), quarter_at(beside_late, -s)]) for s in range(4)]
+    terms = jnp.sum(jnp.log(sums[:4]) - sums[4:])
+    loss = (terms + beside_of(terms)) / (2 * tokens)
     home = [back(moved[0])]
     got = [lax.all_to_all(home[0], ("z", "x"), 0, 0, tiled=True)]
-    moved[1][2], home[0] = tie(moved[1][2], home[0])
+    moved[1][2], home[0], loss = tie(moved[1][2], home[0], loss)
     home.append(back(moved[1]))
     home[1], got[0] = tie(home[1], got[0])
     got.append(lax.all_to_all(home[1], ("z", "x"), 0, 0, tiled=True))
@@ -328,9 +330,6 @@
     table_grad = table_grad_of(pos, own_states, beside_states, [*moved[0], *moved[1], *lower], entries)
     got[1], table_grad = tie(got[1], table_grad)
     hidden_grad = jnp.concatenate([jnp.sum(v.astype(f32), 0) for v in got], 0)
-
-    terms = jnp.sum(jnp.log(sums[:4]) - sums[4:])
-    loss = (terms + beside_of(terms)) / (2 * tokens)
 
     return (loss, hidden_grad, table_grad)
 

time: 194 us -> 195 us (level)
  waiting for transfers between devices: 75.4 us -> 70.9 us
  local copies, waits for them, and re-layouts: 7.81 us -> 10.8 us
  matrix products: 10.8 us -> 13.6 us
    ppermute x17, waiting for transfers between devices: 58 us -> 50.4 us  [over(): return lax.ppermute(value, axis, [(i, (i + s) % n) for i in range(n)])]
    all_to_all x1, waiting for transfers between devices: 3.29 us -> 6.35 us  [local(): got.append(lax.all_to_all(home[1], ('z', 'x'), 0, 0, tiled=True))]
    dot_general x8, matrix products: 10.8 us -> 13.6 us  [back(): lax.dot_general(pieces[s], both[s], (((0,), (0,)), ((), ())), preferred_e...]
    squeeze x2, local copies, waits for them, and re-layouts: 5.8 us -> 8.12 us  [quarter_at(): return lax.dynamic_index_in_dim(q, (y + k) % 4, 0, False)]
  transfers between devices with their start and end apart: 28 -> 28, of which waited for: 16 -> 15; matrix products, arithmetic and copies ran while one was open for 10% -> 12% of each run, Pallas kernels for 6% -> 6%
where the time goes in v4:
time: 195 us; the launch traced here: 194 us
  waiting for transfers between devices  70.9 us (36%)
  starting transfers between devices  46.4 us (24%)
  Pallas kernels  23.6 us (12%)
  blocking collectives  21.4 us (11%)
  matrix products  13.6 us (7%)
  local copies, waits for them, and re-layouts  10.8 us (6%)
  other arithmetic  3.86 us (2%)
  between operations  3.52 us (2%)
    ppermute x17, waiting for transfers between devices, over(): return lax.ppermute(value, axis, [(i, (i + s) % n) for i in range(n)])  50.4 us
    ppermute x17, starting transfers between devices, over(): return lax.ppermute(value, axis, [(i, (i + s) % n) for i in range(n)])  28.8 us
    dot_general x8, matrix products, back(): lax.dot_general(pieces[s], both[s], (((0,), (0,)), ((), ())), preferred_e...  13.6 us
    all_to_all x1, blocking collectives, local(): lax.all_to_all(jnp.broadcast_to(sums, (8, *sums.shape)), 'z', 0, 0, tiled...  11.1 us
    all_to_all x1, blocking collectives, local(): lax.all_to_all(jnp.broadcast_to(sums, (16, *sums.shape)), ('x', 'y'), 0,...  10.4 us
    all_to_all x1, waiting for transfers between devices, local(): lax.all_to_all(jnp.broadcast_to(block, (16, *block.shape)), ('x', 'y'), 0...  10.1 us
    pallas_call x1, Pallas kernels, logits_of(): pl.pallas_call(logits_kernel, out_shape=(pltpu.HBM((2 * quarter, tokens),...  9.65 us
    pallas_call x1, Pallas kernels, table_grad_of(): pl.pallas_call(table_kernel, out_shape=jax.ShapeDtypeStruct((entries, wid...  9.4 us
  transfers between devices with their start and end apart: 28, of which 15 were waited for; matrix products, arithmetic and copies ran while one was open for 12% of the time, Pallas kernels for 6%

profile of v4, /device:TPU:8, one launch (start us, length us, event | category | flops | bytes accessed | tf_op | source)
XLA Modules:
  0.0 194.3 jit_solution(476589650397535860)
XLA Ops:
  1.4 0.8 fusion.13
  2.2 0.9 broadcast_in_dim.9
  3.0 7.4 %all-to-all-start = ((bf16[16,16,1024]{2,1,0:T(8,128)(2,1)}), bf16[16,16,1024]{2,1,0:T(8,128)(2,1)S(1)}, u32[]{:S(2)}, u32[]{:S(2)}) async-start(bf16[16,16,1024]{2,1,0:T(8,128)(2,1)} %broadcast_in_dim.9), calls=%async_computation | async-start | bytes 1048576 | tf_op jit(solution)/shard_map/all_to_all | solution.py:272
  10.4 10.1 %all-to-all-done = bf16[16,16,1024]{2,1,0:T(8,128)(2,1)S(1)} async-done(((bf16[16,16,1024]{2,1,0:T(8,128)(2,1)}), bf16[16,16,1024]{2,1,0:T(8,128)(2,1)S(1)}, u32[]{:S(2)}, u32[]{:S(2)}) %all-to-all-start) | async-done | bytes 524320 | tf_op jit(solution)/shard_map/all_to_all | solution.py:272
  20.7 5.9 %collective-permute-start = (bf16[2,32,3712]{2,1,0:T(8,128)(2,1)S(1)}, bf16[2,32,3712]{2,1,0:T(8,128)(2,1)S(1)}, u32[]{:S(2)}, u32[]{:S(2)}) collective-permute-start(bf16[2,32,3712]{2,1,0:T(8,128)(2,1)S(1)} %bitcast_dynamic-update-slice_fusion.4.refs_0_), channel_id=1, source_target_pairs={{0,224},{32,0},{64,32},{96,64},{128,96},{160,128},{192,160},{224,1... | collective-permute-start | bytes 1425416 | tf_op jit(solution)/shard_map/ppermute | solution.py:17
  26.6 2.0 %dynamic-slice_bitcast_fusion.8 = (bf16[512,896]{1,0:T(8,128)(2,1)S(1)}, bf16[512,896]{1,0:T(8,128)(2,1)S(1)}, bf16[512,896]{1,0:T(8,128)(2,1)S(1)}) fusion(bf16[4,512,896]{2,1,0:T(8,128)(2,1)} %bitcast.17.refs_9_, s32[]{:T(128)S(6)} %select_n.70, s32[]{:T(128)S(6)} %select_n.68, s32[]{:T(128)S(6)} %select_n.66), kind=kLoop, calls=%fused_computation.29 | loop fusion | bytes 5505036 | tf_op jit(solution)/shard_map/jit(dynamic_index_in_dim)/squeeze | solution.py:278
  29.2 1.5 collective-permute-start.5
  30.7 4.8 %collective-permute-done.refs_1_ = bf16[2,32,3712]{2,1,0:T(8,128)(2,1)S(1)} collective-permute-done((bf16[2,32,3712]{2,1,0:T(8,128)(2,1)S(1)}, bf16[2,32,3712]{2,1,0:T(8,128)(2,1)S(1)}, u32[]{:S(2)}, u32[]{:S(2)}) %collective-permute-start) | collective-permute-done | bytes 475168 | tf_op jit(solution)/shard_map/ppermute | solution.py:17
  35.5 3.7 %collective-permute-start.1 = (bf16[2,32,3712]{2,1,0:T(8,128)(2,1)S(1)}, bf16[2,32,3712]{2,1,0:T(8,128)(2,1)S(1)}, u32[]{:S(2)}, u32[]{:S(2)}) collective-permute-start(bf16[2,32,3712]{2,1,0:T(8,128)(2,1)S(1)} %collective-permute-done.refs_1_), channel_id=1, source_target_pairs={{0,224},{32,0},{64,32},{96,64},{128,96},{160,128},{192,160},{224,1... | collective-permute-start | bytes 1425416 | tf_op jit(solution)/shard_map/ppermute | solution.py:17
  39.3 9.9 %collective-permute-done.4.refs_10_ = bf16[512,896]{1,0:T(8,128)(2,1)S(1)} collective-permute-done((bf16[512,896]{1,0:T(8,128)(2,1)S(1)}, bf16[512,896]{1,0:T(8,128)(2,1)S(1)}, u32[]{:S(2)}, u32[]{:S(2)}) %collective-permute-start.4) | collective-permute-done | bytes 917536 | tf_op jit(solution)/shard_map/ppermute | solution.py:17
  49.5 1.1 collective-permute-done.3.refs_7_
  50.6 1.9 collective-permute-start.6
  52.5 4.0 %collective-permute-start.7 = (bf16[512,896]{1,0:T(8,128)(2,1)S(1)}, bf16[512,896]{1,0:T(8,128)(2,1)}, u32[]{:S(2)}, u32[]{:S(2)}) collective-permute-start(bf16[512,896]{1,0:T(8,128)(2,1)S(1)} %get-tuple-element.44), channel_id=1, source_target_pairs={{0,2},{1,3},{2,0},{3,1},{4,6},{5,7},{6,4},{7,5},{8,10},{9,11},{10,... | collective-permute-start | bytes 2752520 | tf_op jit(solution)/shard_map/ppermute | solution.py:17
  56.6 4.6 %collective-permute-done.6.refs_3_ = bf16[2,32,3712]{2,1,0:T(8,128)(2,1)S(1)} collective-permute-done((bf16[2,32,3712]{2,1,0:T(8,128)(2,1)S(1)}, bf16[2,32,3712]{2,1,0:T(8,128)(2,1)S(1)}, u32[]{:S(2)}, u32[]{:S(2)}) %collective-permute-start.6) | collective-permute-done | bytes 475168 | tf_op jit(solution)/shard_map/ppermute | solution.py:17
  61.2 2.3 %collective-permute-start.8 = (bf16[32,3712]{1,0:T(8,128)(2,1)S(1)}, bf16[32,3712]{1,0:T(8,128)(2,1)S(1)}, u32[]{:S(2)}, u32[]{:S(2)}) collective-permute-start(bf16[32,3712]{1,0:T(8,128)(2,1)S(1)} %slice_bitcast_fusion.1), channel_id=1, source_target_pairs={{0,224},{32,0},{64,32},{96,64},{128,96},{160,128},{192,160},{224,1... | collective-permute-start | bytes 712712 | tf_op jit(solution)/shard_map/ppermute | solution.py:17
  63.6 3.9 %collective-permute-done.9.refs_6_ = bf16[2,32,3712]{2,1,0:T(8,128)(2,1)S(1)} collective-permute-done((bf16[2,32,3712]{2,1,0:T(8,128)(2,1)S(1)}, bf16[2,32,3712]{2,1,0:T(8,128)(2,1)S(1)}, u32[]{:S(2)}, u32[]{:S(2)}) %collective-permute-start.9) | collective-permute-done | bytes 475168 | tf_op jit(solution)/shard_map/ppermute | solution.py:17
  68.2 6.7 %collective-permute-done.10.refs_5_ = bf16[32,3712]{1,0:T(8,128)(2,1)S(1)} collective-permute-done((bf16[32,3712]{1,0:T(8,128)(2,1)S(1)}, bf16[32,3712]{1,0:T(8,128)(2,1)S(1)}, u32[]{:S(2)}, u32[]{:S(2)}) %collective-permute-start.10) | collective-permute-done | bytes 237600 | tf_op jit(solution)/shard_map/ppermute | solution.py:17
  74.9 0.7 copy-done.28
  75.7 2.7 %collective-permute-done.13.refs_15_ = bf16[512,896]{1,0:T(8,128)(2,1)} collective-permute-done((bf16[512,896]{1,0:T(8,128)(2,1)}, bf16[512,896]{1,0:T(8,128)(2,1)}, u32[]{:S(2)}, u32[]{:S(2)}) %collective-permute-start.13) | collective-permute-done | bytes 917536 | tf_op jit(solution)/shard_map/ppermute | solution.py:21
  78.5 9.6 %shard_map.58 = (f32[1024,512]{1,0:T(8,128)}, f32[8,128]{1,0:T(8,128)S(1)}, s32[1,512]{1,0:T(1,128)S(1)}, bf16[512,896]{1,0:T(8,128)(2,1)S(1)}) custom-call(s32[6]{0:T(128)S(1)} %stack.43.pos, bf16[2,32,3712]{2,1,0:T(8,128)(2,1)} %copy-done.22, bf16[2,32,3712]{2,1,0:T(8,128)(2,1)} %copy-done.23, bf16[2,32,3712]{2,1,0:T(8,128)(2,1)} %copy-done.25, ...), custom_call_target="tpu_custom_call" | custom-call | flops 3758096384 | bytes 13631488 | tf_op jit(solution)/shard_map/pallas_call | solution.py:103
  88.1 10.4 %all_to_all.25 = f32[16,8,128]{2,1,0:T(8,128)S(1)} all-to-all(f32[16,8,128]{2,1,0:T(8,128)S(1)} %broadcast_in_dim.10), channel_id=1, replica_groups=mesh['z'=8,'x'=4,'c'=2,'y'=4] {'x','y'}, dimensions={0} | all-to-all | bytes 131072 | tf_op jit(solution)/shard_map/all_to_all | solution.py:301
  98.6 11.1 %all_to_all.26.got = f32[8,8,128]{2,1,0:T(8,128)S(1)} all-to-all(f32[8,8,128]{2,1,0:T(8,128)S(1)} %broadcast_in_dim.11), channel_id=1, replica_groups=mesh['z'=8,'x'=4,'c'=2,'y'=4] {'z'}, dimensions={0} | all-to-all | bytes 65536 | tf_op jit(solution)/shard_map/all_to_all | solution.py:303
  109.6 2.1 %shard_map.59 = (f32[8,128]{1,0:T(8,128)S(1)}, bf16[1024,256]{1,0:T(8,128)(2,1)S(1)}, bf16[1024,256]{1,0:T(8,128)(2,1)S(1)}) custom-call(s32[6]{0:T(128)S(1)} %stack.43.pos, f32[8,8,128]{2,1,0:T(8,128)S(1)} %all_to_all.26.got, f32[1024,512]{1,0:T(8,128)} %get-tuple-element.52.capped_ref, s32[1,512]{1,0:T(1,128)S(1)} %get-tuple-element.53.wanted_ref), custom_call_target="tpu_custom_call" | custom-call | flops 4194304 | bytes 3145728 | tf_op jit(solution)/shard_map/pallas_call | solution.py:159
  111.7 0.9 collective-permute-start.15
  112.6 2.7 %collective-permute-start.16 = (bf16[1024,256]{1,0:T(8,128)(2,1)S(1)}, bf16[1024,256]{1,0:T(8,128)(2,1)}, u32[]{:S(2)}, u32[]{:S(2)}) collective-permute-start(bf16[1024,256]{1,0:T(8,128)(2,1)S(1)} %get-tuple-element.69.refs_0_), channel_id=1, source_target_pairs={{0,2},{1,3},{2,0},{3,1},{4,6},{5,7},{6,4},{7,5},{8,10},{9,11},{10,... | collective-permute-start | bytes 1572872 | tf_op jit(solution)/shard_map/ppermute | solution.py:17
  116.6 6.2 %dynamic-slice_bitcast_fusion.2 = (bf16[512,896]{1,0:T(8,128)(2,1)}, bf16[512,896]{1,0:T(8,128)(2,1)}, bf16[512,896]{1,0:T(8,128)(2,1)}, bf16[512,896]{1,0:T(8,1...) fusion(bf16[4,512,896]{2,1,0:T(8,128)(2,1)} %bitcast.23.refs_13, ...), kind=kLoop, calls=%fused_computation.23 | loop fusion | bytes 14680080 | tf_op jit(solution)/shard_map/jit(dynamic_index_in_dim)/squeeze | solution.py:278
  124.0 2.7 %collective-permute-done.15.refs_1_ = bf16[1024,256]{1,0:T(8,128)(2,1)S(1)} collective-permute-done((bf16[1024,256]{1,0:T(8,128)(2,1)S(1)}, bf16[1024,256]{1,0:T(8,128)(2,1)S(1)}, u32[]{:S(2)}, u32[]{:S(2)}) %collective-permute-start.15) | collective-permute-done | bytes 524320 | tf_op jit(solution)/shard_map/ppermute | solution.py:17
  126.7 2.4 %collective-permute-done.16.refs_2_ = bf16[1024,256]{1,0:T(8,128)(2,1)} collective-permute-done((bf16[1024,256]{1,0:T(8,128)(2,1)S(1)}, bf16[1024,256]{1,0:T(8,128)(2,1)}, u32[]{:S(2)}, u32[]{:S(2)}) %collective-permute-start.16) | collective-permute-done | bytes 524320 | tf_op jit(solution)/shard_map/ppermute | solution.py:17
  129.1 7.4 %collective-permute-done.17.refs_3_ = bf16[1024,256]{1,0:T(8,128)(2,1)S(1)} collective-permute-done((bf16[1024,256]{1,0:T(8,128)(2,1)S(1)}, bf16[1024,256]{1,0:T(8,128)(2,1)S(1)}, u32[]{:S(2)}, u32[]{:S(2)}) %collective-permute-start.17) | collective-permute-done | bytes 524320 | tf_op jit(solution)/shard_map/ppermute | solution.py:17
  136.4 2.5 %collective-permute-start.18 = (bf16[1024,256]{1,0:T(8,128)(2,1)S(1)}, bf16[1024,256]{1,0:T(8,128)(2,1)}, u32[]{:S(2)}, u32[]{:S(2)}) collective-permute-start(bf16[1024,256]{1,0:T(8,128)(2,1)S(1)} %get-tuple-element.73.refs_0_.refs_4_), channel_id=1, source_target_pairs={{0,2},{1,3},{2,0},{3,1},{4,6},{5,7},{6,4},{7,5},{8,10},{9,11},{10,... | collective-permute-start | bytes 1572872 | tf_op jit(solution)/shard_map/ppermute | solution.py:17
  139.1 1.8 collective-permute-start.20
  140.9 2.3 %fusion.11 = f32[256,896]{1,0:T(8,128)S(1)} fusion(bf16[1024,256]{1,0:T(8,128)(2,1)S(1)} %collective-permute-done.15.refs_1_, bf16[512,896]{1,0:T(8,128)(2,1)} %get-tuple-element.85, bf16[512,896]{1,0:T(8,128)(2,1)} %get-tuple-element.98), kind=kOutput, calls=%fused_computation.18 | convolution fusion | flops 473432064 | bytes 3276800 | tf_op jit(solution)/shard_map/dot_general | solution.py:313
  143.3 0.7 convolution_add_fusion.2
  144.8 1.9 fusion.8
  146.7 1.6 fusion.5
  148.3 4.8 %all-to-all-start.3 = ((bf16[32,8,896]{2,1,0:T(8,128)(2,1)}), bf16[32,8,896]{2,1,0:T(8,128)(2,1)}, u32[]{:S(2)}, u32[]{:S(2)}) async-start(bf16[32,8,896]{2,1,0:T(8,128)(2,1)} %fusion.5), calls=%async_computation.3 | async-start | bytes 917504 | tf_op jit(solution)/shard_map/all_to_all | solution.py:322
  153.1 1.3 shard_map.60
  154.6 1.9 fusion.7
  156.5 6.6 %collective-permute-done.21.refs_3_.refs_7_ = bf16[1024,256]{1,0:T(8,128)(2,1)} collective-permute-done((bf16[1024,256]{1,0:T(8,128)(2,1)S(1)}, bf16[1024,256]{1,0:T(8,128)(2,1)}, u32[]{:S(2)}, u32[]{:S(2)}) %collective-permute-start.21) | collective-permute-done | bytes 524320 | tf_op jit(solution)/shard_map/ppermute | solution.py:17
  163.1 1.8 fusion.9
  165.0 1.9 fusion.10
  166.9 1.5 fusion.6
  168.4 1.2 all-to-all-done.3
  169.6 1.2 shard_map.61
  171.5 4.1 %all-to-all-start.4 = ((bf16[32,8,896]{2,1,0:T(8,128)(2,1)}), bf16[32,8,896]{2,1,0:T(8,128)(2,1)S(1)}, u32[]{:S(2)}, u32[]{:S(2)}) async-start(bf16[32,8,896]{2,1,0:T(8,128)(2,1)} %fusion.6), calls=%async_computation.4 | async-start | bytes 917504 | tf_op jit(solution)/shard_map/all_to_all | solution.py:326
  175.5 1.1 convert_reduce_fusion.1
  176.7 9.4 %shard_map.62 = f32[2048,896]{1,0:T(8,128)} custom-call(s32[6]{0:T(128)S(1)} %stack.43.pos, bf16[512,896]{1,0:T(8,128)(2,1)} %copy-done.2, bf16[512,896]{1,0:T(8,128)(2,1)} %collective-permute-done.22.beside_states, bf16[1024,256]{1,0:T(8,128)(2,1)} %copy-done.1, bf16[1024,256]{1,0:T(8,128)(2,1)} %copy-done.12, ...), custom_call_target="tpu_custom_call" | custom-call | flops 1048576 | bytes 262144 | tf_op jit(solution)/shard_map/pallas_call | solution.py:243
  186.1 6.4 %all-to-all-done.4 = bf16[32,8,896]{2,1,0:T(8,128)(2,1)S(1)} async-done(((bf16[32,8,896]{2,1,0:T(8,128)(2,1)}), bf16[32,8,896]{2,1,0:T(8,128)(2,1)S(1)}, u32[]{:S(2)}, u32[]{:S(2)}) %all-to-all-start.4) | async-done | bytes 458784 | tf_op jit(solution)/shard_map/all_to_all | solution.py:326
  (104 shorter events, 6.3 us)
Async XLA Ops:
  3.0 17.5 %all-to-all-start = ((bf16[16,16,1024]{2,1,0:T(8,128)(2,1)}), bf16[16,16,1024]{2,1,0:T(8,128)(2,1)S(1)}, u32[]{:S(2)}, u32[]{:S(2)}) async-start(bf16[16,16,1024]{2,1,0:T(8,128)(2,1)} %broadcast_in_dim.9), calls=%async_computation | async-start | bytes 1048576 | tf_op jit(solution)/shard_map/all_to_all | solution.py:272
  20.7 7.9 %copy-start.22 = (bf16[2,32,3712]{2,1,0:T(8,128)(2,1)}, bf16[2,32,3712]{2,1,0:T(8,128)(2,1)S(1)}, u32[]{:S(2)}) copy-start(bf16[2,32,3712]{2,1,0:T(8,128)(2,1)S(1)} %bitcast_dynamic-update-slice_fusion.4.refs_0_) | copy-start | bytes 1425412
  20.7 14.8 %collective-permute-start = (bf16[2,32,3712]{2,1,0:T(8,128)(2,1)S(1)}, bf16[2,32,3712]{2,1,0:T(8,128)(2,1)S(1)}, u32[]{:S(2)}, u32[]{:S(2)}) collective-permute-start(bf16[2,32,3712]{2,1,0:T(8,128)(2,1)S(1)} %bitcast_dynamic-update-slice_fusion.4.refs_0_), channel_id=1, source_target_pairs={{0,224},{32,0},{64,32},{96,64},{128,96},{160,128},{192,160},{224,1... | collective-permute-start | bytes 1425416 | tf_op jit(solution)/shard_map/ppermute | solution.py:17
  26.6 12.6 %collective-permute-start.2 = (bf16[2,32,3712]{2,1,0:T(8,128)(2,1)S(1)}, bf16[2,32,3712]{2,1,0:T(8,128)(2,1)S(1)}, u32[]{:S(2)}, u32[]{:S(2)}) collective-permute-start(bf16[2,32,3712]{2,1,0:T(8,128)(2,1)S(1)} %bitcast_dynamic-update-slice_fusion.4.refs_0_), channel_id=1, source_target_pairs={{0,32},{32,64},{64,96},{96,128},{128,160},{160,192},{192,224},{224... | collective-permute-start | bytes 1425416 | tf_op jit(solution)/shard_map/ppermute | solution.py:17
  28.6 20.7 %collective-permute-start.4 = (bf16[512,896]{1,0:T(8,128)(2,1)S(1)}, bf16[512,896]{1,0:T(8,128)(2,1)S(1)}, u32[]{:S(2)}, u32[]{:S(2)}) collective-permute-start(bf16[512,896]{1,0:T(8,128)(2,1)S(1)} %get-tuple-element.89), channel_id=1, source_target_pairs={{0,1},{1,2},{2,3},{3,0},{4,5},{5,6},{6,7},{7,4},{8,9},{9,10},{10,1... | collective-permute-start | bytes 2752520 | tf_op jit(solution)/shard_map/ppermute | solution.py:17
  29.2 20.3 %collective-permute-start.5 = (bf16[512,896]{1,0:T(8,128)(2,1)S(1)}, bf16[512,896]{1,0:T(8,128)(2,1)S(1)}, u32[]{:S(2)}, u32[]{:S(2)}) collective-permute-start(bf16[512,896]{1,0:T(8,128)(2,1)S(1)} %get-tuple-element.88), channel_id=1, source_target_pairs={{0,3},{1,0},{2,1},{3,2},{4,7},{5,4},{6,5},{7,6},{8,11},{9,8},{10,9... | collective-permute-start | bytes 2752520 | tf_op jit(solution)/shard_map/ppermute | solution.py:17
  35.5 13.9 %copy-start.23 = (bf16[2,32,3712]{2,1,0:T(8,128)(2,1)}, bf16[2,32,3712]{2,1,0:T(8,128)(2,1)S(1)}, u32[]{:S(2)}) copy-start(bf16[2,32,3712]{2,1,0:T(8,128)(2,1)S(1)} %collective-permute-done.refs_1_) | copy-start | bytes 1425412
  35.5 13.9 %collective-permute-start.1 = (bf16[2,32,3712]{2,1,0:T(8,128)(2,1)S(1)}, bf16[2,32,3712]{2,1,0:T(8,128)(2,1)S(1)}, u32[]{:S(2)}, u32[]{:S(2)}) collective-permute-start(bf16[2,32,3712]{2,1,0:T(8,128)(2,1)S(1)} %collective-permute-done.refs_1_), channel_id=1, source_target_pairs={{0,224},{32,0},{64,32},{96,64},{128,96},{160,128},{192,160},{224,1... | collective-permute-start | bytes 1425416 | tf_op jit(solution)/shard_map/ppermute | solution.py:17
  39.2 13.3 %copy-start.24 = (bf16[2,32,3712]{2,1,0:T(8,128)(2,1)}, bf16[2,32,3712]{2,1,0:T(8,128)(2,1)S(1)}, u32[]{:S(2)}) copy-start(bf16[2,32,3712]{2,1,0:T(8,128)(2,1)S(1)} %collective-permute-done.2.refs_8_) | copy-start | bytes 1425412
  39.2 11.4 %collective-permute-start.3 = (bf16[2,32,3712]{2,1,0:T(8,128)(2,1)S(1)}, bf16[2,32,3712]{2,1,0:T(8,128)(2,1)S(1)}, u32[]{:S(2)}, u32[]{:S(2)}) collective-permute-start(bf16[2,32,3712]{2,1,0:T(8,128)(2,1)S(1)} %collective-permute-done.2.refs_8_), channel_id=1, source_target_pairs={{0,32},{32,64},{64,96},{96,128},{128,160},{160,192},{192,224},{224... | collective-permute-start | bytes 1425416 | tf_op jit(solution)/shard_map/ppermute | solution.py:17
  39.2 39.2 %collective-permute-start.11 = (bf16[2048,896]{1,0:T(8,128)(2,1)}, bf16[2048,896]{1,0:T(8,128)(2,1)}, u32[]{:S(2)}, u32[]{:S(2)}) collective-permute-start(bf16[2048,896]{1,0:T(8,128)(2,1)} %param.4), channel_id=1, source_target_pairs={{0,4},{4,0},{1,5},{5,1},{2,6},{6,2},{3,7},{7,3},{8,12},{12,8},{9,1... | collective-permute-start | bytes 11010056 | tf_op jit(solution)/shard_map/ppermute | solution.py:21
  49.2 29.2 %copy-start.15 = (bf16[512,896]{1,0:T(8,128)(2,1)}, bf16[512,896]{1,0:T(8,128)(2,1)S(1)}, u32[]{:S(2)}) copy-start(bf16[512,896]{1,0:T(8,128)(2,1)S(1)} %collective-permute-done.4.refs_10_) | copy-start | bytes 2752516
  49.5 29.0 %copy-start.16 = (bf16[512,896]{1,0:T(8,128)(2,1)}, bf16[512,896]{1,0:T(8,128)(2,1)S(1)}, u32[]{:S(2)}) copy-start(bf16[512,896]{1,0:T(8,128)(2,1)S(1)} %collective-permute-done.5.refs_12_) | copy-start | bytes 2752516
  49.5 7.1 %copy-start.25 = (bf16[2,32,3712]{2,1,0:T(8,128)(2,1)}, bf16[2,32,3712]{2,1,0:T(8,128)(2,1)S(1)}, u32[]{:S(2)}) copy-start(bf16[2,32,3712]{2,1,0:T(8,128)(2,1)S(1)} %collective-permute-done.1.refs_2_) | copy-start | bytes 1425412
  50.6 27.8 %copy-start.26 = (bf16[2,32,3712]{2,1,0:T(8,128)(2,1)}, bf16[2,32,3712]{2,1,0:T(8,128)(2,1)S(1)}, u32[]{:S(2)}) copy-start(bf16[2,32,3712]{2,1,0:T(8,128)(2,1)S(1)} %collective-permute-done.3.refs_7_) | copy-start | bytes 1425412
  50.6 10.6 %collective-permute-start.6 = (bf16[2,32,3712]{2,1,0:T(8,128)(2,1)S(1)}, bf16[2,32,3712]{2,1,0:T(8,128)(2,1)S(1)}, u32[]{:S(2)}, u32[]{:S(2)}) collective-permute-start(bf16[2,32,3712]{2,1,0:T(8,128)(2,1)S(1)} %collective-permute-done.1.refs_2_), channel_id=1, source_target_pairs={{0,224},{32,0},{64,32},{96,64},{128,96},{160,128},{192,160},{224,1... | collective-permute-start | bytes 1425416 | tf_op jit(solution)/shard_map/ppermute | solution.py:17
  52.5 22.4 %collective-permute-start.7 = (bf16[512,896]{1,0:T(8,128)(2,1)S(1)}, bf16[512,896]{1,0:T(8,128)(2,1)}, u32[]{:S(2)}, u32[]{:S(2)}) collective-permute-start(bf16[512,896]{1,0:T(8,128)(2,1)S(1)} %get-tuple-element.44), channel_id=1, source_target_pairs={{0,2},{1,3},{2,0},{3,1},{4,6},{5,7},{6,4},{7,5},{8,10},{9,11},{10,... | collective-permute-start | bytes 2752520 | tf_op jit(solution)/shard_map/ppermute | solution.py:17
  56.6 10.9 %collective-permute-start.9 = (bf16[2,32,3712]{2,1,0:T(8,128)(2,1)S(1)}, bf16[2,32,3712]{2,1,0:T(8,128)(2,1)S(1)}, u32[]{:S(2)}, u32[]{:S(2)}) collective-permute-start(bf16[2,32,3712]{2,1,0:T(8,128)(2,1)S(1)} %collective-permute-done.3.refs_7_), channel_id=1, source_target_pairs={{0,32},{32,64},{64,96},{96,128},{128,160},{160,192},{192,224},{224... | collective-permute-start | bytes 1425416 | tf_op jit(solution)/shard_map/ppermute | solution.py:17
  61.2 17.2 %copy-start.13 = (bf16[2,32,3712]{2,1,0:T(8,128)(2,1)}, bf16[2,32,3712]{2,1,0:T(8,128)(2,1)S(1)}, u32[]{:S(2)}) copy-start(bf16[2,32,3712]{2,1,0:T(8,128)(2,1)S(1)} %collective-permute-done.6.refs_3_) | copy-start | bytes 1425412
  61.2 6.5 %collective-permute-start.8 = (bf16[32,3712]{1,0:T(8,128)(2,1)S(1)}, bf16[32,3712]{1,0:T(8,128)(2,1)S(1)}, u32[]{:S(2)}, u32[]{:S(2)}) collective-permute-start(bf16[32,3712]{1,0:T(8,128)(2,1)S(1)} %slice_bitcast_fusion.1), channel_id=1, source_target_pairs={{0,224},{32,0},{64,32},{96,64},{128,96},{160,128},{192,160},{224,1... | collective-permute-start | bytes 712712 | tf_op jit(solution)/shard_map/ppermute | solution.py:17
  67.5 11.0 %copy-start.14 = (bf16[2,32,3712]{2,1,0:T(8,128)(2,1)}, bf16[2,32,3712]{2,1,0:T(8,128)(2,1)S(1)}, u32[]{:S(2)}) copy-start(bf16[2,32,3712]{2,1,0:T(8,128)(2,1)S(1)} %collective-permute-done.9.refs_6_) | copy-start | bytes 1425412
  67.5 7.4 %collective-permute-start.10 = (bf16[32,3712]{1,0:T(8,128)(2,1)S(1)}, bf16[32,3712]{1,0:T(8,128)(2,1)S(1)}, u32[]{:S(2)}, u32[]{:S(2)}) collective-permute-start(bf16[32,3712]{1,0:T(8,128)(2,1)S(1)} %slice_bitcast_fusion), channel_id=1, source_target_pairs={{0,32},{32,64},{64,96},{96,128},{128,160},{160,192},{192,224},{224... | collective-permute-start | bytes 712712 | tf_op jit(solution)/shard_map/ppermute | solution.py:17
  67.6 8.1 %collective-permute-start.12 = (bf16[512,896]{1,0:T(8,128)(2,1)S(1)}, bf16[512,896]{1,0:T(8,128)(2,1)}, u32[]{:S(2)}, u32[]{:S(2)}) collective-permute-start(bf16[512,896]{1,0:T(8,128)(2,1)S(1)} %collective-permute-done.4.refs_10_), channel_id=1, source_target_pairs={{0,4},{4,0},{1,5},{5,1},{2,6},{6,2},{3,7},{7,3},{8,12},{12,8},{9,1... | collective-permute-start | bytes 2752520 | tf_op jit(solution)/shard_map/ppermute | solution.py:21
  67.7 10.7 %copy-start.27 = (bf16[32,3712]{1,0:T(8,128)(2,1)}, bf16[32,3712]{1,0:T(8,128)(2,1)S(1)}, u32[]{:S(2)}) copy-start(bf16[32,3712]{1,0:T(8,128)(2,1)S(1)} %collective-permute-done.8.refs_4_) | copy-start | bytes 712708
  67.7 8.0 %collective-permute-start.14 = (bf16[512,896]{1,0:T(8,128)(2,1)S(1)}, bf16[512,896]{1,0:T(8,128)(2,1)}, u32[]{:S(2)}, u32[]{:S(2)}) collective-permute-start(bf16[512,896]{1,0:T(8,128)(2,1)S(1)} %collective-permute-done.5.refs_12_), channel_id=1, source_target_pairs={{0,4},{4,0},{1,5},{5,1},{2,6},{6,2},{3,7},{7,3},{8,12},{12,8},{9,1... | collective-permute-start | bytes 2752520 | tf_op jit(solution)/shard_map/ppermute | solution.py:21
  75.6 2.8 %collective-permute-start.13 = (bf16[512,896]{1,0:T(8,128)(2,1)}, bf16[512,896]{1,0:T(8,128)(2,1)}, u32[]{:S(2)}, u32[]{:S(2)}) collective-permute-start(bf16[512,896]{1,0:T(8,128)(2,1)} %collective-permute-done.7.refs_11_), channel_id=1, source_target_pairs={{0,4},{4,0},{1,5},{5,1},{2,6},{6,2},{3,7},{7,3},{8,12},{12,8},{9,1... | collective-permute-start | bytes 2752520 | tf_op jit(solution)/shard_map/ppermute | solution.py:21
  88.1 82.8 %copy-start.2 = (bf16[512,896]{1,0:T(8,128)(2,1)}, bf16[512,896]{1,0:T(8,128)(2,1)S(1)}, u32[]{:S(2)}) copy-start(bf16[512,896]{1,0:T(8,128)(2,1)S(1)} %get-tuple-element.68.own_states) | copy-start | bytes 2752516
  111.7 31.6 %copy-start.1 = (bf16[1024,256]{1,0:T(8,128)(2,1)}, bf16[1024,256]{1,0:T(8,128)(2,1)S(1)}, u32[]{:S(2)}) copy-start(bf16[1024,256]{1,0:T(8,128)(2,1)S(1)} %get-tuple-element.69.refs_0_) | copy-start | bytes 1572868
  111.7 55.2 %copy-start = (bf16[1024,256]{1,0:T(8,128)(2,1)}, bf16[1024,256]{1,0:T(8,128)(2,1)S(1)}, u32[]{:S(2)}) copy-start(bf16[1024,256]{1,0:T(8,128)(2,1)S(1)} %get-tuple-element.73.refs_0_.refs_4_) | copy-start | bytes 1572868
  111.7 14.9 %collective-permute-start.15 = (bf16[1024,256]{1,0:T(8,128)(2,1)S(1)}, bf16[1024,256]{1,0:T(8,128)(2,1)S(1)}, u32[]{:S(2)}, u32[]{:S(2)}) collective-permute-start(bf16[1024,256]{1,0:T(8,128)(2,1)S(1)} %get-tuple-element.69.refs_0_), channel_id=1, source_target_pairs={{0,1},{1,2},{2,3},{3,0},{4,5},{5,6},{6,7},{7,4},{8,9},{9,10},{10,1... | collective-permute-start | bytes 1572872 | tf_op jit(solution)/shard_map/ppermute | solution.py:17
  112.6 16.5 %collective-permute-start.16 = (bf16[1024,256]{1,0:T(8,128)(2,1)S(1)}, bf16[1024,256]{1,0:T(8,128)(2,1)}, u32[]{:S(2)}, u32[]{:S(2)}) collective-permute-start(bf16[1024,256]{1,0:T(8,128)(2,1)S(1)} %get-tuple-element.69.refs_0_), channel_id=1, source_target_pairs={{0,2},{1,3},{2,0},{3,1},{4,6},{5,7},{6,4},{7,5},{8,10},{9,11},{10,... | collective-permute-start | bytes 1572872 | tf_op jit(solution)/shard_map/ppermute | solution.py:17
  115.3 21.1 %collective-permute-start.17 = (bf16[1024,256]{1,0:T(8,128)(2,1)S(1)}, bf16[1024,256]{1,0:T(8,128)(2,1)S(1)}, u32[]{:S(2)}, u32[]{:S(2)}) collective-permute-start(bf16[1024,256]{1,0:T(8,128)(2,1)S(1)} %get-tuple-element.69.refs_0_), channel_id=1, source_target_pairs={{0,3},{1,0},{2,1},{3,2},{4,7},{5,4},{6,5},{7,6},{8,11},{9,8},{10,9... | collective-permute-start | bytes 1572872 | tf_op jit(solution)/shard_map/ppermute | solution.py:17
  116.6 6.2 %collective-permute-start.19 = (f32[]{:T(128)}, f32[]{:T(128)}, u32[]{:S(2)}, u32[]{:S(2)}) collective-permute-start(f32[]{:T(128)} %subtract_reduce_fusion), channel_id=1, source_target_pairs={{0,4},{4,0},{1,5},{5,1},{2,6},{6,2},{3,7},{7,3},{8,12},{12,8},{9,1... | collective-permute-start | bytes 20 | tf_op jit(solution)/shard_map/ppermute | solution.py:21
  126.7 16.6 %copy-start.12 = (bf16[1024,256]{1,0:T(8,128)(2,1)}, bf16[1024,256]{1,0:T(8,128)(2,1)S(1)}, u32[]{:S(2)}) copy-start(bf16[1024,256]{1,0:T(8,128)(2,1)S(1)} %collective-permute-done.15.refs_1_) | copy-start | bytes 1572868
  136.4 10.2 %copy-start.3 = (bf16[1024,256]{1,0:T(8,128)(2,1)}, bf16[1024,256]{1,0:T(8,128)(2,1)S(1)}, u32[]{:S(2)}) copy-start(bf16[1024,256]{1,0:T(8,128)(2,1)S(1)} %collective-permute-done.17.refs_3_) | copy-start | bytes 1572868
  136.4 18.1 %collective-permute-start.18 = (bf16[1024,256]{1,0:T(8,128)(2,1)S(1)}, bf16[1024,256]{1,0:T(8,128)(2,1)}, u32[]{:S(2)}, u32[]{:S(2)}) collective-permute-start(bf16[1024,256]{1,0:T(8,128)(2,1)S(1)} %get-tuple-element.73.refs_0_.refs_4_), channel_id=1, source_target_pairs={{0,2},{1,3},{2,0},{3,1},{4,6},{5,7},{6,4},{7,5},{8,10},{9,11},{10,... | collective-permute-start | bytes 1572872 | tf_op jit(solution)/shard_map/ppermute | solution.py:17
  138.9 24.2 %collective-permute-start.21 = (bf16[1024,256]{1,0:T(8,128)(2,1)S(1)}, bf16[1024,256]{1,0:T(8,128)(2,1)}, u32[]{:S(2)}, u32[]{:S(2)}) collective-permute-start(bf16[1024,256]{1,0:T(8,128)(2,1)S(1)} %get-tuple-element.73.refs_0_.refs_4_), channel_id=1, source_target_pairs={{0,3},{1,0},{2,1},{3,2},{4,7},{5,4},{6,5},{7,6},{8,11},{9,8},{10,9... | collective-permute-start | bytes 1572872 | tf_op jit(solution)/shard_map/ppermute | solution.py:17
  139.1 25.8 %collective-permute-start.20 = (bf16[1024,256]{1,0:T(8,128)(2,1)S(1)}, bf16[1024,256]{1,0:T(8,128)(2,1)}, u32[]{:S(2)}, u32[]{:S(2)}) collective-permute-start(bf16[1024,256]{1,0:T(8,128)(2,1)S(1)} %get-tuple-element.73.refs_0_.refs_4_), channel_id=1, source_target_pairs={{0,1},{1,2},{2,3},{3,0},{4,5},{5,6},{6,7},{7,4},{8,9},{9,10},{10,1... | collective-permute-start | bytes 1572872 | tf_op jit(solution)/shard_map/ppermute | solution.py:17
  140.9 2.4 %copy-start.6 = (bf16[512,896]{1,0:T(8,128)(2,1)S(1)}, bf16[512,896]{1,0:T(8,128)(2,1)}, u32[]{:S(2)}) copy-start(bf16[512,896]{1,0:T(8,128)(2,1)} %get-tuple-element.97) | copy-start | bytes 2752516
  148.3 21.3 %all-to-all-start.3 = ((bf16[32,8,896]{2,1,0:T(8,128)(2,1)}), bf16[32,8,896]{2,1,0:T(8,128)(2,1)}, u32[]{:S(2)}, u32[]{:S(2)}) async-start(bf16[32,8,896]{2,1,0:T(8,128)(2,1)} %fusion.5), calls=%async_computation.3 | async-start | bytes 917504 | tf_op jit(solution)/shard_map/all_to_all | solution.py:322
  154.4 8.7 %copy-start.9 = (bf16[512,896]{1,0:T(8,128)(2,1)S(1)}, bf16[512,896]{1,0:T(8,128)(2,1)}, u32[]{:S(2)}) copy-start(bf16[512,896]{1,0:T(8,128)(2,1)} %get-tuple-element.83) | copy-start | bytes 2752516
  154.5 8.7 %copy-start.11 = (bf16[512,896]{1,0:T(8,128)(2,1)S(1)}, bf16[512,896]{1,0:T(8,128)(2,1)}, u32[]{:S(2)}) copy-start(bf16[512,896]{1,0:T(8,128)(2,1)} %get-tuple-element.100) | copy-start | bytes 2752516
  154.5 22.2 %collective-permute-start.23 = (bf16[2048,256]{1,0:T(8,128)(2,1)S(1)}, bf16[2048,256]{1,0:T(8,128)(2,1)}, u32[]{:S(2)}, u32[]{:S(2)}) collective-permute-start(bf16[2048,256]{1,0:T(8,128)(2,1)S(1)} %shard_map.60), channel_id=1, source_target_pairs={{0,4},{4,0},{1,5},{5,1},{2,6},{6,2},{3,7},{7,3},{8,12},{12,8},{9,1... | collective-permute-start | bytes 3145736 | tf_op jit(solution)/shard_map/ppermute | solution.py:21
  156.5 8.5 %copy-start.17 = (bf16[512,896]{1,0:T(8,128)(2,1)S(1)}, bf16[512,896]{1,0:T(8,128)(2,1)}, u32[]{:S(2)}) copy-start(bf16[512,896]{1,0:T(8,128)(2,1)} %get-tuple-element.85) | copy-start | bytes 2752516
  156.5 8.5 %copy-start.18 = (bf16[512,896]{1,0:T(8,128)(2,1)S(1)}, bf16[512,896]{1,0:T(8,128)(2,1)}, u32[]{:S(2)}) copy-start(bf16[512,896]{1,0:T(8,128)(2,1)} %get-tuple-element.98) | copy-start | bytes 2752516
  170.9 5.8 %collective-permute-start.24 = (bf16[2048,256]{1,0:T(8,128)(2,1)S(1)}, bf16[2048,256]{1,0:T(8,128)(2,1)}, u32[]{:S(2)}, u32[]{:S(2)}) collective-permute-start(bf16[2048,256]{1,0:T(8,128)(2,1)S(1)} %shard_map.61), channel_id=1, source_target_pairs={{0,4},{4,0},{1,5},{5,1},{2,6},{6,2},{3,7},{7,3},{8,12},{12,8},{9,1... | collective-permute-start | bytes 3145736 | tf_op jit(solution)/shard_map/ppermute | solution.py:21
  171.0 5.7 %collective-permute-start.22 = (bf16[512,896]{1,0:T(8,128)(2,1)S(1)}, bf16[512,896]{1,0:T(8,128)(2,1)}, u32[]{:S(2)}, u32[]{:S(2)}) collective-permute-start(bf16[512,896]{1,0:T(8,128)(2,1)S(1)} %get-tuple-element.68.own_states), channel_id=1, source_target_pairs={{0,4},{4,0},{1,5},{5,1},{2,6},{6,2},{3,7},{7,3},{8,12},{12,8},{9,1... | collective-permute-start | bytes 2752520 | tf_op jit(solution)/shard_map/ppermute | solution.py:21
  171.5 21.0 %all-to-all-start.4 = ((bf16[32,8,896]{2,1,0:T(8,128)(2,1)}), bf16[32,8,896]{2,1,0:T(8,128)(2,1)S(1)}, u32[]{:S(2)}, u32[]{:S(2)}) async-start(bf16[32,8,896]{2,1,0:T(8,128)(2,1)} %fusion.6), calls=%async_computation.4 | async-start | bytes 917504 | tf_op jit(solution)/shard_map/all_to_all | solution.py:326
  (9 other events, 15.0 us)
